TPU v7x, 512 devices: a whole 4x4x16 slice. The times are simulated.
512 devices in a mesh: expert: 8 (over x, core), shard: 64 (over y, z).
Axes of the slice: x: 4, y: 4, z: 16, core: 2. Of those that a mesh axis runs over, the one named last changes fastest.
Arguments:
- grad: bfloat16 [32, 2048, 1408], P('expert', 'shard'), may hold values from -6 to 6
- momentum: float32 [32, 2048, 1408], P('expert', 'shard'), may hold values from -6 to 6
- owner: int32 [8, 4], P('expert'), may hold values from 0 to 3, each once within a row
Outputs:
- new_momentum: float32 [32, 2048, 1408], P('expert', 'shard')
- update: bfloat16 [32, 2048, 1408], P('expert', 'shard')
- column_residual_norms: float32 [8, 5632], P('expert', 'shard')
Inputs may be any that keep to these rules, and one draw needn't show every extreme that they name: Each row of owner is a permutation of the teams 0 to 3.
All inputs are finite; a program needn't handle non-finite values.
Results may differ from a plain program's by a relative error of at most 0.017.
Values may be sent and summed in bfloat16 or wider, within the bound.
No kernel may reach another device: no remote copies, remote signals or barrier semaphores. Data moves between devices by JAX's collectives and lax.ppermute only.
A program may use at most 64 MiB of HBM per device.

v0:
```python
import math

import jax
import jax.numpy as jnp
from jax import lax
from jax.sharding import PartitionSpec as P

DECAY = 0.95
COEF_A = 3.4445
COEF_B = -4.775
COEF_C = 2.0315
EPSILON = 1e-07


def left_product(first_operand, second_operand):
    return lax.dot_general(
        first_operand, second_operand, (((0,), (0,)), ((), ())), preferred_element_type=jnp.float32
    )


def rows_times(block_rows, matrix):
    return jnp.dot(block_rows, matrix, preferred_element_type=jnp.float32)


def columns_times(block_rows, matrix):
    return lax.dot_general(
        block_rows, matrix, (((1,), (1,)), ((), ())), preferred_element_type=jnp.float32
    )


def on_device(grad, momentum, owner):
    matrices, count_of_rows, columns = grad.shape
    count_of_parts = lax.axis_size("shard")
    team_size = count_of_parts // matrices
    block_width = columns // team_size
    total_rows = count_of_rows * count_of_parts
    position = lax.axis_index("shard")
    member = position % team_size
    new_momentum = DECAY * momentum + grad.astype(jnp.float32)
    rounded = new_momentum.astype(jnp.bfloat16)
    selector_mask = (owner[0][None, :] == jnp.arange(matrices, dtype=jnp.int32)[:, None]).astype(
        jnp.bfloat16
    )
    widened = rounded.astype(jnp.float32)
    squares = lax.psum(jnp.sum(widened * widened, axis=(1, 2)), "shard")
    factor = 0.5 * math.sqrt(columns) / (jnp.sqrt(squares) + EPSILON)
    moving_average = (widened * factor[:, None, None]).astype(jnp.bfloat16)
    matrices_each_team = jnp.einsum(
        "zd,dbe->zbe", selector_mask, moving_average, preferred_element_type=jnp.float32
    ).astype(jnp.bfloat16)
    payload = jnp.broadcast_to(
        matrices_each_team[:, None], (matrices, team_size, count_of_rows, columns)
    ).reshape(count_of_parts, count_of_rows, columns)
    whole = lax.all_to_all(payload, "shard", split_axis=0, concat_axis=0, tiled=True).reshape(
        total_rows, columns
    )
    start = member * block_width
    own_columns = lax.dynamic_slice_in_dim(whole, start, block_width, 1)
    gram_rows = left_product(own_columns, whole).astype(jnp.bfloat16)
    lifted_rows = columns_times(gram_rows, whole).astype(jnp.bfloat16)
    square_rows = rows_times(lifted_rows, whole)
    polynomial_row_block = (COEF_B * gram_rows.astype(jnp.float32) + COEF_C * square_rows).astype(
        jnp.bfloat16
    )
    ortho_rows = COEF_A * own_columns.T.astype(jnp.float32) + columns_times(
        polynomial_row_block, whole
    )
    ortho_b = ortho_rows.astype(jnp.bfloat16)
    update_rows = (math.sqrt(total_rows) * ortho_rows).astype(jnp.bfloat16)
    cross_rows = rows_times(ortho_b, whole).astype(jnp.bfloat16)
    first_rows = columns_times(cross_rows, whole).astype(jnp.bfloat16)
    second_rows = rows_times(first_rows, whole).astype(jnp.bfloat16)
    third_power_rows = columns_times(second_rows, whole).astype(jnp.bfloat16)
    fourth_rows = rows_times(third_power_rows, whole)
    identity_rows = (
        (start + jnp.arange(block_width, dtype=jnp.int32))[:, None]
        == jnp.arange(columns, dtype=jnp.int32)[None, :]
    ).astype(jnp.float32)
    resid_rows = (
        COEF_A * cross_rows.astype(jnp.float32)
        + COEF_B * second_rows.astype(jnp.float32)
        + COEF_C * fourth_rows
        - identity_rows
    )
    column_residual_norms = jnp.sqrt(jnp.sum(resid_rows * resid_rows, axis=1))[None, :]
    returned = lax.all_to_all(update_rows, "shard", split_axis=1, concat_axis=1, tiled=True)
    returned = returned.reshape(block_width, matrices, team_size, count_of_rows)
    regrouped = jnp.einsum(
        "tm,wtjr->mrjw", selector_mask, returned, preferred_element_type=jnp.float32
    ).astype(jnp.bfloat16)
    out_update = regrouped.reshape(matrices, count_of_rows, columns)
    return (new_momentum, out_update, column_residual_norms)


def solution(mesh):
    in_specs = (P("expert", "shard", None), P("expert", "shard", None), P("expert", None))
    out_specs = (P("expert", "shard", None), P("expert", "shard", None), P("expert", "shard"))
    return jax.shard_map(
        on_device, mesh=mesh, in_specs=in_specs, out_specs=out_specs, check_vma=False
    )
```

profile of v0, /device:TPU:6, one launch (start us, length us, event | category | flops | bytes accessed | tf_op | source)
XLA Modules:
  0.0 439.6 jit_solution(6337219587815028677)
XLA Ops:
  0.6 1.4 fusion.7
  2.1 0.0 copy-start
  2.1 158.6 %psum.7 = f32[4]{0:T(128)S(1)} all-reduce(f32[4]{0:T(128)S(1)} %get-tuple-element.3), channel_id=1, replica_groups=mesh['expert'=8,'shard'=64] {'shard'}, use_global_device_ids=true, to_apply=%region_1.2 | all-reduce | flops 4 | bytes 32 | tf_op jit(solution)/shard_map/psum | solution.py:45
  160.7 0.1 fusion.8
  160.8 1.1 convolution_convert_fusion
  162.0 3.0 broadcast_in_dim.2
  165.0 0.0 copy-done
  165.0 6.2 %all-to-all-start = ((bf16[64,32,1408]{2,1,0:T(8,128)(2,1)}), bf16[64,32,1408]{2,1,0:T(8,128)(2,1)}, u32[]{:S(2)}, u32[]{:S(2)}) async-start(bf16[64,32,1408]{2,1,0:T(8,128)(2,1)} %bitcast.36), calls=%async_computation | async-start | bytes 11534336 | tf_op jit(solution)/shard_map/all_to_all | solution.py:54
  171.2 217.1 %all-to-all-done = bf16[64,32,1408]{2,1,0:T(8,128)(2,1)} async-done(((bf16[64,32,1408]{2,1,0:T(8,128)(2,1)}), bf16[64,32,1408]{2,1,0:T(8,128)(2,1)}, u32[]{:S(2)}, u32[]{:S(2)}) %all-to-all-start) | async-done | bytes 5767200 | tf_op jit(solution)/shard_map/all_to_all | solution.py:54
  388.3 1.4 constant_dynamic-slice_fusion
  389.8 3.7 convolution_convert_fusion.6
  393.4 0.2 copy.19
  393.7 7.3 %fusion.4 = bf16[88,1408]{1,0:T(8,128)(2,1)S(1)} fusion(bf16[2048,1408]{1,0:T(8,128)(2,1)} %bitcast.3, bf16[88,1408]{1,0:T(8,128)(2,1)S(1)} %convolution_convert_fusion.6), kind=kOutput, calls=%fused_computation.8 | convolution fusion | flops 1015821312 | bytes 6262784 | tf_op jit(solution)/shard_map/dot_general | solution.py:22
  400.9 4.6 %multiply_convert_fusion = (bf16[88,2048]{1,0:T(8,128)(2,1)S(1)}, bf16[88,2048]{1,0:T(8,128)(2,1)S(1)}) fusion(bf16[88,1408]{1,0:T(8,128)(2,1)S(1)} %fusion.4, bf16[2048,1408]{1,0:T(8,128)(2,1)} %bitcast.3, bf16[2048,88]{0,1:T(8,128)(2,1)S(1)} %copy.19), kind=kOutput, calls=%fused_computation.22 | convolution fusion | flops 508592128 | bytes 7096320 | tf_op jit(solution)/shard_map/dot_general | solution.py:26
  405.6 1.0 copy.13
  406.6 9.2 %all-to-all-start.1 = ((bf16[88,64,32]{0,2,1:T(8,128)(2,1)}), bf16[88,64,32]{0,2,1:T(8,128)(2,1)S(1)}, u32[]{:S(2)}, u32[]{:S(2)}) async-start(bf16[88,64,32]{0,2,1:T(8,128)(2,1)} %bitcast.5), calls=%async_computation.1 | async-start | bytes 1048576 | tf_op jit(solution)/shard_map/all_to_all | solution.py:86
  415.8 3.7 convolution_convert_fusion.4
  419.5 7.3 %convolution_convert_fusion.2 = bf16[88,1408]{1,0:T(8,128)(2,1)S(1)} fusion(bf16[2048,1408]{1,0:T(8,128)(2,1)} %bitcast.3, bf16[88,1408]{1,0:T(8,128)(2,1)S(1)} %convolution_convert_fusion.4), kind=kOutput, calls=%fused_computation.10 | convolution fusion | flops 1015325696 | bytes 6262784 | tf_op jit(solution)/shard_map/dot_general | solution.py:22
  426.8 0.0 copy-start.1
  426.8 7.4 %fusion.6 = f32[88]{0:T(128)S(1)} fusion(bf16[2048,1408]{1,0:T(8,128)(2,1)} %bitcast.3, bf16[88,1408]{1,0:T(8,128)(2,1)S(1)} %convolution_convert_fusion.2, bf16[88,1408]{1,0:T(8,128)(2,1)S(1)} %convolution_convert_fusion.4, s32[88]{0:T(128)S(1)} %iota_add_fusion), kind=kOutput, calls=%fused_computation.17 | convolution fusion | flops 1016688576 | bytes 6263488 | tf_op jit(solution)/shard_map/dot_general | solution.py:22
  434.2 0.5 sqrt_bitcast_fusion
  434.8 2.6 all-to-all-done.1
  437.4 0.0 copy-done.1
  437.4 0.6 fusion.5
  437.9 0.3 copy.15
  438.3 1.3 reshape.38
  (3 shorter events, 0.1 us)
Async XLA Ops:
  2.1 162.9 %copy-start = (f32[4,32,1408]{2,1,0:T(8,128)}, f32[4,32,1408]{2,1,0:T(8,128)S(1)}, u32[]{:S(2)}) copy-start(f32[4,32,1408]{2,1,0:T(8,128)S(1)} %get-tuple-element.4) | copy-start | bytes 2162692
  165.0 223.3 %all-to-all-start = ((bf16[64,32,1408]{2,1,0:T(8,128)(2,1)}), bf16[64,32,1408]{2,1,0:T(8,128)(2,1)}, u32[]{:S(2)}, u32[]{:S(2)}) async-start(bf16[64,32,1408]{2,1,0:T(8,128)(2,1)} %bitcast.36), calls=%async_computation | async-start | bytes 11534336 | tf_op jit(solution)/shard_map/all_to_all | solution.py:54
  406.6 30.7 %all-to-all-start.1 = ((bf16[88,64,32]{0,2,1:T(8,128)(2,1)}), bf16[88,64,32]{0,2,1:T(8,128)(2,1)S(1)}, u32[]{:S(2)}, u32[]{:S(2)}) async-start(bf16[88,64,32]{0,2,1:T(8,128)(2,1)} %bitcast.5), calls=%async_computation.1 | async-start | bytes 1048576 | tf_op jit(solution)/shard_map/all_to_all | solution.py:86
  426.8 10.6 %copy-start.1 = (s32[1,4]{1,0:T(1,128)S(1)}, s32[1,4]{1,0:T(1,128)}, u32[]{:S(2)}) copy-start(s32[1,4]{1,0:T(1,128)} %param.5) | copy-start | bytes 52
where the time goes:
time: 440 us
  waiting for transfers between devices  220 us (50%)
  blocking collectives  159 us (36%)
  matrix products  35.6 us (8%)
  starting transfers between devices  15.4 us (4%)
  local copies, waits for them, and re-layouts  7.87 us (2%)
    all_to_all x1, waiting for transfers between devices, on_device(): lax.all_to_all(payload, 'shard', split_axis=0, concat_axis=0, tiled=True)  217 us
    psum x1, blocking collectives, on_device(): squares = lax.psum(jnp.sum(widened * widened, axis=(1, 2)), 'shard')  159 us
    dot_general x4, matrix products, rows_times(): return jnp.dot(block_rows, matrix, preferred_element_type=jnp.float32)  25.6 us
    all_to_all x1, starting transfers between devices, on_device(): lax.all_to_all(update_rows, 'shard', split_axis=1, concat_axis=1, tiled=T...  9.22 us
  transfers between devices with their start and end apart: 2, of which 2 were waited for; matrix products, arithmetic and copies ran while one was open for 4% of the time, Pallas kernels for 0%

commit v1 on v0

v1 whole, which is shorter than its diff:
```python
import math

import jax
import jax.numpy as jnp
from jax import lax
from jax.experimental import pallas as pl
from jax.experimental.pallas import tpu as pltpu
from jax.sharding import Mesh, PartitionSpec as P

DECAY = 0.95
COEF_A = 3.4445
COEF_B = -4.775
COEF_C = 2.0315
EPSILON = 1e-07

F32 = jnp.float32
BF16 = jnp.bfloat16
VMEM_LIMIT = 56 * 1024 * 1024


def momentum_kernel(owner_ref, grad_ref, momentum_ref, new_ref, payload_ref):
    new = DECAY * momentum_ref[...] + grad_ref[...].astype(F32)
    new_ref[...] = new
    payload_ref[...] = new.astype(BF16)


def momentum_step(grad, momentum, owner):
    matrices, rows, columns = grad.shape
    block = (1, rows, columns)
    return pl.pallas_call(
        momentum_kernel,
        grid_spec=pltpu.PrefetchScalarGridSpec(
            num_scalar_prefetch=1,
            grid=(matrices,),
            in_specs=[pl.BlockSpec(block, lambda m, own: (m, 0, 0))] * 2,
            out_specs=[
                pl.BlockSpec(block, lambda m, own: (m, 0, 0)),
                pl.BlockSpec(block, lambda m, own: (own[m], 0, 0)),
            ],
        ),
        out_shape=[
            jax.ShapeDtypeStruct(grad.shape, F32),
            jax.ShapeDtypeStruct(grad.shape, BF16),
        ],
        name="momentum_step",
    )(owner, grad, momentum)


def times(block, x_ref):
    return jnp.dot(block, x_ref[...], preferred_element_type=F32)


def times_transposed(block, x_ref):
    return lax.dot_general(
        block, x_ref[...], (((1,), (1,)), ((), ())), preferred_element_type=F32
    )


def ortho_kernel(width, start_ref, x_ref, update_ref, ortho_ref, scale_ref):
    total_rows, columns = x_ref.shape
    padded = ortho_ref.shape[0]
    total = jnp.zeros((16, columns), F32)
    for at in range(0, total_rows, 16):
        piece = x_ref[at : at + 16, :].astype(F32)
        total = total + piece * piece
    scale = 0.5 * math.sqrt(columns) / (jnp.sqrt(jnp.sum(total, keepdims=True)) + EPSILON)
    scale_ref[...] = jnp.broadcast_to(scale, scale_ref.shape)
    row = lax.broadcasted_iota(jnp.int32, (padded, columns), 0)
    column = lax.broadcasted_iota(jnp.int32, (padded, columns), 1)
    chosen = ((column == row + start_ref[0]) & (row < width)).astype(F32).astype(BF16)
    own = times_transposed(chosen, x_ref).astype(BF16)
    gram = ((scale * scale) * times(own, x_ref)).astype(BF16)
    lifted = (scale * times_transposed(gram, x_ref)).astype(BF16)
    square = scale * times(lifted, x_ref)
    poly = (COEF_B * gram.astype(F32) + COEF_C * square).astype(BF16)
    ortho = scale * (COEF_A * own.astype(F32) + times_transposed(poly, x_ref))
    ortho_ref[...] = ortho.astype(BF16)
    update_ref[...] = (math.sqrt(total_rows) * ortho).T[:, :width].astype(BF16)


def residual_kernel(width, start_ref, scale_ref, x_ref, ortho_ref, norms_ref):
    columns = x_ref.shape[1]
    padded = ortho_ref.shape[0]
    scale = scale_ref[0:1, 0:1]
    cross = (scale * times(ortho_ref[...], x_ref)).astype(BF16)
    first = (scale * times_transposed(cross, x_ref)).astype(BF16)
    second = (scale * times(first, x_ref)).astype(BF16)
    third = (scale * times_transposed(second, x_ref)).astype(BF16)
    fourth = scale * times(third, x_ref)
    row = lax.broadcasted_iota(jnp.int32, (padded, columns), 0)
    column = lax.broadcasted_iota(jnp.int32, (padded, columns), 1)
    identity = (column == row + start_ref[0]).astype(F32)
    resid = (
        COEF_A * cross.astype(F32) + COEF_B * second.astype(F32) + COEF_C * fourth - identity
    )
    norms_ref[...] = jnp.sqrt(jnp.sum(resid * resid, axis=1, keepdims=True))


def regroup_kernel(width, owner_ref, returned_ref, update_ref):
    for at in range(returned_ref.shape[1]):
        update_ref[0, :, at * width : (at + 1) * width] = returned_ref[0, at]


def regroup(returned, owner):
    matrices, members, rows, width = returned.shape
    return pl.pallas_call(
        lambda *refs: regroup_kernel(width, *refs),
        grid_spec=pltpu.PrefetchScalarGridSpec(
            num_scalar_prefetch=1,
            grid=(matrices,),
            in_specs=[
                pl.BlockSpec((1, members, rows, width), lambda m, own: (own[m], 0, 0, 0))
            ],
            out_specs=pl.BlockSpec((1, rows, members * width), lambda m, own: (m, 0, 0)),
        ),
        out_shape=jax.ShapeDtypeStruct((matrices, rows, members * width), BF16),
        name="regroup",
    )(owner, returned)


def on_device(grad, momentum, owner):
    matrices, rows, columns = grad.shape
    members = lax.axis_size("z")
    width = columns // members
    total_rows = rows * matrices * members
    padded = -(-width // 16) * 16
    owner = owner.reshape(matrices)
    new_momentum, payload = momentum_step(grad, momentum, owner)
    mine = lax.all_to_all(payload, "y", split_axis=0, concat_axis=0, tiled=True)
    whole = lax.all_gather(mine.reshape(matrices * rows, columns), "z", axis=0, tiled=True)
    start = (lax.axis_index("z") * width).astype(jnp.int32).reshape(1)
    smem = pl.BlockSpec(memory_space=pltpu.SMEM)
    vmem = pl.BlockSpec(memory_space=pltpu.VMEM)
    flops = 2 * padded * total_rows * columns
    update, ortho, scale = pl.pallas_call(
        lambda *refs: ortho_kernel(width, *refs),
        in_specs=[smem, vmem],
        out_specs=[vmem, vmem, vmem],
        out_shape=[
            jax.ShapeDtypeStruct((total_rows, width), BF16),
            jax.ShapeDtypeStruct((padded, total_rows), BF16),
            jax.ShapeDtypeStruct((8, 128), F32),
        ],
        compiler_params=pltpu.CompilerParams(vmem_limit_bytes=VMEM_LIMIT),
        cost_estimate=pl.CostEstimate(
            flops=5 * flops, bytes_accessed=2 * total_rows * columns, transcendentals=0
        ),
        name="ortho",
    )(start, whole)
    returned = lax.all_to_all(
        update.reshape(members, matrices, rows, width).swapaxes(0, 1).reshape(-1, rows, width),
        ("y", "z"),
        split_axis=0,
        concat_axis=0,
        tiled=True,
    )
    norms = pl.pallas_call(
        lambda *refs: residual_kernel(width, *refs),
        in_specs=[smem, vmem, vmem, vmem],
        out_specs=vmem,
        out_shape=jax.ShapeDtypeStruct((padded, 1), F32),
        compiler_params=pltpu.CompilerParams(vmem_limit_bytes=VMEM_LIMIT),
        cost_estimate=pl.CostEstimate(
            flops=5 * flops, bytes_accessed=2 * total_rows * columns, transcendentals=0
        ),
        name="residual",
    )(start, scale, whole, ortho)
    out_update = regroup(returned.reshape(matrices, members, rows, width), owner)
    return new_momentum, out_update, norms[:width, 0][None, :]


def solution(mesh):
    experts, shards = mesh.devices.shape
    split = Mesh(mesh.devices.reshape(experts // 2, 2, 4, shards // 4), ("x", "core", "y", "z"))
    groups, rows = ("x", "core"), ("y", "z")
    return jax.shard_map(
        on_device,
        mesh=split,
        in_specs=(P(groups, rows, None), P(groups, rows, None), P(groups, None)),
        out_specs=(P(groups, rows, None), P(groups, rows, None), P(groups, rows)),
        check_vma=False,
    )
```

time: 440 us -> 172 us (0.39)
  blocking collectives: 159 us -> 12.3 us
  waiting for transfers between devices: 220 us -> 102 us
  matrix products: 35.6 us -> 0 us
  Pallas kernels: 0 us -> 28.8 us
  between operations: 0.77 us -> 14 us
  starting transfers between devices: 15.4 us -> 10.6 us
    all_to_all x2 -> x1, waiting for transfers between devices: 220 us -> 15.6 us  [on_device(): lax.all_to_all(update.reshape(members, matrices, rows, width).swapaxes(0,...]
    psum x1 -> x0, blocking collectives: 159 us -> none  [on_device(): squares = lax.psum(jnp.sum(widened * widened, axis=(1, 2)), 'shard')]
    all_gather x0 -> x1, waiting for transfers between devices: none -> 86.5 us  [on_device(): lax.all_gather(mine.reshape(matrices * rows, columns), 'z', axis=0, tiled...]
    dot_general x8 -> x0, matrix products: 35.6 us -> none  [the longest x4 25.6 us: rows_times(): return jnp.dot(block_rows, matrix, preferred_element_type=jnp.float32)]
    pallas_call x0 -> x4, Pallas kernels: none -> 28.8 us  [the longest x1 11 us: on_device(): pl.pallas_call(lambda *refs: ortho_kernel(width, *refs), in_specs=[smem,...]
    all_to_all x0 -> x1, blocking collectives: none -> 12.3 us  [on_device(): mine = lax.all_to_all(payload, 'y', split_axis=0, concat_axis=0, tiled=True)]
    all_to_all x2 -> x1, starting transfers between devices: 15.4 us -> 10.5 us  [on_device(): lax.all_to_all(update.reshape(members, matrices, rows, width).swapaxes(0,...]
  transfers between devices with their start and end apart: 2 -> 2, of which waited for: 2 -> 2; matrix products, arithmetic and copies ran while one was open for 4% -> 1% of each run, Pallas kernels for 0% -> 6%
where the time goes in v1:
time: 172 us
  waiting for transfers between devices  102 us (59%)
  Pallas kernels  28.8 us (17%)
  between operations  14 us (8%)
  blocking collectives  12.3 us (7%)
  starting transfers between devices  10.6 us (6%)
  local copies, waits for them, and re-layouts  4.07 us (2%)
    all_gather x1, waiting for transfers between devices, on_device(): lax.all_gather(mine.reshape(matrices * rows, columns), 'z', axis=0, tiled...  86.5 us
    all_to_all x1, waiting for transfers between devices, on_device(): lax.all_to_all(update.reshape(members, matrices, rows, width).swapaxes(0,...  15.6 us
    all_to_all x1, blocking collectives, on_device(): mine = lax.all_to_all(payload, 'y', split_axis=0, concat_axis=0, tiled=True)  12.3 us
    pallas_call x1, Pallas kernels, on_device(): pl.pallas_call(lambda *refs: ortho_kernel(width, *refs), in_specs=[smem,...  11 us
    all_to_all x1, starting transfers between devices, on_device(): lax.all_to_all(update.reshape(members, matrices, rows, width).swapaxes(0,...  10.5 us
    pallas_call x1, Pallas kernels, on_device(): pl.pallas_call(lambda *refs: residual_kernel(width, *refs), in_specs=[sme...  9.71 us
    pallas_call x1, Pallas kernels, momentum_step(): pl.pallas_call(momentum_kernel, grid_spec=pltpu.PrefetchScalarGridSpec(nu...  4.08 us
    pallas_call x1, Pallas kernels, regroup(): pl.pallas_call(lambda *refs: regroup_kernel(width, *refs), grid_spec=pltp...  4.03 us
  transfers between devices with their start and end apart: 2, of which 2 were waited for; matrix products, arithmetic and copies ran while one was open for 1% of the time, Pallas kernels for 6%

profile of v1, /device:TPU:6, one launch (start us, length us, event | category | flops | bytes accessed | tf_op | source)
XLA Modules:
  0.0 171.8 jit_solution(263847843036997151)
XLA Ops:
  7.2 0.0 all-gather.2.cloned.1.call-start
  7.2 4.1 %momentum_step.1 = (f32[4,32,1408]{2,1,0:T(8,128)}, bf16[4,32,1408]{2,1,0:T(8,128)(2,1)}) custom-call(s32[4]{0:T(128)} %bitcast.12, bf16[4,32,1408]{2,1,0:T(8,128)(2,1)} %grad_ref.1, f32[4,32,1408]{2,1,0:T(8,128)} %momentum_ref.1), custom_call_target="tpu_custom_call" | custom-call | tf_op jit(solution)/shard_map/momentum_step/pallas_call | solution.py:30
  11.3 12.3 %all_to_all.10 = bf16[4,32,1408]{2,1,0:T(8,128)(2,1)} all-to-all(bf16[4,32,1408]{2,1,0:T(8,128)(2,1)} %get-tuple-element.9), channel_id=1, replica_groups=mesh['x'=4,'core'=2,'y'=4,'z'=16] {'y'}, dimensions={0} | all-to-all | bytes 720896 | tf_op jit(solution)/shard_map/all_to_all | solution.py:129
  23.6 0.0 all-gather.2.cloned.1.call-update
  23.6 86.5 %all-gather.2.cloned.1.call-done.refs_1_.refs_2_ = bf16[2048,1408]{1,0:T(8,128)(2,1)} async-done(((bf16[128,1408]{1,0:T(8,128)(2,1)}), bf16[2048,1408]{1,0:T(8,128)(2,1)}) %all-gather.2.cloned.1.call-update) | async-done | bytes 5767184 | tf_op jit(solution)/shard_map/all_gather | solution.py:130
  110.1 11.0 %ortho.1 = (bf16[2048,88]{1,0:T(8,128)(2,1)}, bf16[96,2048]{1,0:T(8,128)(2,1)}, f32[8,128]{1,0:T(8,128)}) custom-call(s32[1]{0:T(128)} %bitcast.1.refs_0_, bf16[2048,1408]{1,0:T(8,128)(2,1)} %all-gather.2.cloned.1.call-done.refs_1_.refs_2_), custom_call_target="tpu_custom_call" | custom-call | flops 2768240640 | bytes 5767168 | tf_op jit(solution)/shard_map/ortho/pallas_call | solution.py:135
  121.0 1.9 %copy.7 = bf16[4,16,32,88]{3,2,1,0:T(8,128)(2,1)} copy(bf16[4,16,32,88]{3,2,0,1:T(8,128)(2,1)} %bitcast.11) | data formatting | bytes 720896 | tf_op jit(solution)/shard_map/transpose | solution.py:151
  122.9 10.5 %all-to-all-start.1 = ((bf16[64,32,88]{2,1,0:T(8,128)(2,1)}), bf16[64,32,88]{2,1,0:T(8,128)(2,1)S(1)}, u32[]{:S(2)}, u32[]{:S(2)}) async-start(bf16[64,32,88]{2,1,0:T(8,128)(2,1)} %bitcast.5), calls=%async_computation.1 | async-start | bytes 1048576 | tf_op jit(solution)/shard_map/all_to_all | solution.py:150
  133.4 9.7 %residual.1 = f32[96,1]{1,0:T(8,128)} custom-call(s32[1]{0:T(128)} %bitcast.1.refs_0_, f32[8,128]{1,0:T(8,128)} %get-tuple-element.11.refs_1_, bf16[2048,1408]{1,0:T(8,128)(2,1)} %all-gather.2.cloned.1.call-done.refs_1_.refs_2_, bf16[96,2048]{1,0:T(8,128)(2,1)} %get-tuple-element.12.refs_3_), custom_call_target="tpu_custom_call" | custom-call | flops 2768240640 | bytes 5767168 | tf_op jit(solution)/shard_map/residual/pallas_call | solution.py:157
  143.1 1.4 slice_reduce_fusion
  144.6 15.6 %all-to-all-done.1 = bf16[64,32,88]{2,1,0:T(8,128)(2,1)S(1)} async-done(((bf16[64,32,88]{2,1,0:T(8,128)(2,1)}), bf16[64,32,88]{2,1,0:T(8,128)(2,1)S(1)}, u32[]{:S(2)}, u32[]{:S(2)}) %all-to-all-start.1) | async-done | bytes 360480 | tf_op jit(solution)/shard_map/all_to_all | solution.py:150
  160.1 0.0 copy-start
  160.2 0.8 copy-done
  160.9 4.0 %regroup.1 = bf16[4,32,1408]{2,1,0:T(8,128)(2,1)} custom-call(s32[4]{0:T(128)} %bitcast.13, bf16[4,16,32,88]{3,2,1,0:T(8,128)(2,1)} %bitcast.9), custom_call_target="tpu_custom_call" | custom-call | tf_op jit(solution)/shard_map/regroup/pallas_call | solution.py:106
Async XLA Ops:
  7.2 102.9 %all-gather.2.cloned.1.call-start = ((), (), s32[]{:S(2)}) async-start(), calls=%async_computation.2 | async-start | bytes 6127616 | tf_op jit(solution)/shard_map/all_gather | solution.py:130
  122.9 37.2 %all-to-all-start.1 = ((bf16[64,32,88]{2,1,0:T(8,128)(2,1)}), bf16[64,32,88]{2,1,0:T(8,128)(2,1)S(1)}, u32[]{:S(2)}, u32[]{:S(2)}) async-start(bf16[64,32,88]{2,1,0:T(8,128)(2,1)} %bitcast.5), calls=%async_computation.1 | async-start | bytes 1048576 | tf_op jit(solution)/shard_map/all_to_all | solution.py:150
  160.1 0.8 copy-start
Sparse Core Ops, SparseCore 0:
  23.7 86.2 all-gather.1

commit v2 on v1

v2 whole, which is shorter than its diff:
```python
import math

import jax
import jax.numpy as jnp
from jax import lax
from jax.experimental import pallas as pl
from jax.experimental.pallas import tpu as pltpu
from jax.sharding import Mesh, PartitionSpec as P

DECAY = 0.95
COEF_A = 3.4445
COEF_B = -4.775
COEF_C = 2.0315
EPSILON = 1e-07

F32 = jnp.float32
BF16 = jnp.bfloat16
VMEM_LIMIT = 56 * 1024 * 1024
LANES = 128
Y_OFFSETS = (0, 3, 1, 2)


def momentum_kernel(grad_ref, momentum_ref, new_ref, payload_ref):
    new = DECAY * momentum_ref[...] + grad_ref[...].astype(F32)
    new_ref[...] = new
    rounded = new.astype(BF16)
    half = payload_ref.shape[2]
    payload_ref[0] = rounded[:, :half]
    payload_ref[1] = rounded[:, half:]


def momentum_step(grad, momentum):
    matrices, rows, columns = grad.shape
    vmem = pl.BlockSpec(memory_space=pltpu.VMEM)
    return pl.pallas_call(
        momentum_kernel,
        in_specs=[vmem, vmem],
        out_specs=[vmem, vmem],
        out_shape=[
            jax.ShapeDtypeStruct(grad.shape, F32),
            jax.ShapeDtypeStruct((2, matrices, rows // 2, columns), BF16),
        ],
        compiler_params=pltpu.CompilerParams(vmem_limit_bytes=VMEM_LIMIT),
        name="momentum_step",
    )(grad, momentum)


def times(block, x_ref):
    return jnp.dot(block, x_ref[...], preferred_element_type=F32)


def times_transposed(block, x_ref):
    return lax.dot_general(
        block, x_ref[...], (((1,), (1,)), ((), ())), preferred_element_type=F32
    )


def products_kernel(width, padded, place_ref, *refs):
    sections = refs[:16]
    slots_ref, x_ref, sems = refs[16:]
    core, y, b = place_ref[0], place_ref[1], place_ref[2]
    total_rows, columns = x_ref.shape
    section_rows = total_rows // 16
    copies = [
        pltpu.make_async_copy(
            ref, x_ref.at[pl.ds(at * section_rows, section_rows)], sems.at[at]
        )
        for at, ref in enumerate(sections)
    ]
    for copy in copies:
        copy.start()
    total = jnp.zeros((16, columns), F32)
    for at, copy in enumerate(copies):
        copy.wait()
        for low in range(at * section_rows, (at + 1) * section_rows, 16):
            piece = x_ref[low : low + 16, :].astype(F32)
            total = total + piece * piece
    scale = 0.5 * math.sqrt(columns) / (jnp.sqrt(jnp.sum(total, keepdims=True)) + EPSILON)
    start = width * (core * 8 + y * 2 + b)
    row = lax.broadcasted_iota(jnp.int32, (padded, columns), 0)
    column = lax.broadcasted_iota(jnp.int32, (padded, columns), 1)
    identity = ((column == row + start) & (row < width)).astype(F32)
    own = times_transposed(identity.astype(BF16), x_ref).astype(BF16)
    gram = ((scale * scale) * times(own, x_ref)).astype(BF16)
    lifted = (scale * times_transposed(gram, x_ref)).astype(BF16)
    square = scale * times(lifted, x_ref)
    poly = (COEF_B * gram.astype(F32) + COEF_C * square).astype(BF16)
    ortho = scale * (COEF_A * own.astype(F32) + times_transposed(poly, x_ref))
    cross = (scale * times(ortho.astype(BF16), x_ref)).astype(BF16)
    first = (scale * times_transposed(cross, x_ref)).astype(BF16)
    second = (scale * times(first, x_ref)).astype(BF16)
    third = (scale * times_transposed(second, x_ref)).astype(BF16)
    fourth = scale * times(third, x_ref)
    resid = (
        COEF_A * cross.astype(F32) + COEF_B * second.astype(F32) + COEF_C * fourth - identity
    )
    norms = jnp.sqrt(jnp.sum(resid * resid, axis=1, keepdims=True))
    high = norms.astype(BF16).astype(F32)
    low = norms - high
    lane = lax.broadcasted_iota(jnp.int32, (32, LANES), 1)
    extra = jnp.zeros((32, LANES), F32)
    for part in range(3):
        cut = slice(32 * part, 32 * part + 32)
        extra = jnp.where(lane == width + part, high[cut], extra)
        extra = jnp.where(lane == width + 3 + part, low[cut], extra)
    update = math.sqrt(total_rows) * ortho
    below = jnp.zeros((LANES - padded, section_rows), F32)

    def turned(at):
        piece = update[:, at * section_rows : (at + 1) * section_rows]
        return jnp.concatenate([piece, below], axis=0).T.reshape(16, 8, LANES)

    for core_step in range(2):
        half = core ^ core_step
        place = pl.ds(pl.multiple_of(half * 16, 16), 16)
        tail = jnp.where(half == 0, extra[:16], extra[16:])
        for step, offset in enumerate(Y_OFFSETS):
            mine = turned((core_step * 4 + step) * 2)
            other = turned((core_step * 4 + step) * 2 + 1)
            ordered = jnp.concatenate(
                [jnp.where(b == 0, mine, other), jnp.where(b == 0, other, mine)], axis=1
            )
            slots_ref[:, (y + offset) % 4, place, :] = (ordered + tail[None]).astype(BF16)


def products(sections, place, width, padded):
    section_rows, columns = sections[0].shape
    total_rows = 16 * section_rows
    return pl.pallas_call(
        lambda *refs: products_kernel(width, padded, *refs),
        in_specs=[pl.BlockSpec(memory_space=pltpu.SMEM)]
        + [pl.BlockSpec(memory_space=pl.ANY)] * 16,
        out_specs=pl.BlockSpec(memory_space=pltpu.VMEM),
        out_shape=jax.ShapeDtypeStruct((16, 4, 32, LANES), BF16),
        scratch_shapes=[
            pltpu.VMEM((total_rows, columns), BF16),
            pltpu.SemaphoreType.DMA((16,)),
        ],
        compiler_params=pltpu.CompilerParams(vmem_limit_bytes=VMEM_LIMIT),
        cost_estimate=pl.CostEstimate(
            flops=20 * padded * total_rows * columns,
            bytes_accessed=2 * total_rows * columns,
            transcendentals=0,
        ),
        name="products",
    )(place, *sections)


def regroup_kernel(width, place_ref, owner_ref, returned_ref, update_ref, norms_ref):
    y, z = place_ref[1], place_ref[3]
    matrices = update_ref.shape[0]
    for m in range(matrices):
        for at in range(16):
            core, source_y, b = at // 8, (at // 2) % 4, at % 2
            update_ref[m, :, at * width : (at + 1) * width] = returned_ref[
                core, m, b, source_y, :, :width
            ]

        @pl.when(owner_ref[m] == y)
        def _():
            slot = returned_ref[z // 8, m, z % 2, (z // 2) % 4].astype(F32).T
            for part in range(3):
                value = slot[width + part : width + part + 1]
                value = value + slot[width + 3 + part : width + 4 + part]
                size = min(32, width - 32 * part)
                norms_ref[:, 32 * part : 32 * part + size] = value[:, :size]


def regroup(returned, place, owner, width):
    matrices, rows = returned.shape[1], returned.shape[4]
    smem = pl.BlockSpec(memory_space=pltpu.SMEM)
    vmem = pl.BlockSpec(memory_space=pltpu.VMEM)
    return pl.pallas_call(
        lambda *refs: regroup_kernel(width, *refs),
        in_specs=[smem, smem, vmem],
        out_specs=[vmem, vmem],
        out_shape=[
            jax.ShapeDtypeStruct((matrices, rows, 16 * width), BF16),
            jax.ShapeDtypeStruct((1, width), F32),
        ],
        compiler_params=pltpu.CompilerParams(vmem_limit_bytes=VMEM_LIMIT),
        name="regroup",
    )(place, owner, returned)


def on_device(grad, momentum, owner):
    matrices, rows, columns = grad.shape
    width = columns // 16
    padded = -(-width // 16) * 16
    core, y, z = lax.axis_index("core"), lax.axis_index("y"), lax.axis_index("z")
    place = jnp.stack([core, y, z % 2, z]).astype(jnp.int32)
    up = [(i, (i + 1) % 4) for i in range(4)]
    down = [((i + 1) % 4, i) for i in range(4)]

    new_momentum, payload = momentum_step(grad, momentum)
    halves = lax.all_to_all(payload, "core", split_axis=0, concat_axis=0, tiled=True)
    mine = lax.all_to_all(
        halves.reshape(16, rows // 4, columns), "z", split_axis=0, concat_axis=0, tiled=True
    ).reshape(-1, columns)
    other = lax.ppermute(mine, "z", [(i, i ^ 1) for i in range(16)])
    mine_left = lax.ppermute(mine, "y", up)
    mine_right = lax.ppermute(mine, "y", down)
    other_left = lax.ppermute(other, "y", up)
    other_right = lax.ppermute(other, "y", down)
    mine_far = lax.ppermute(mine_left, "y", up)
    other_far = lax.ppermute(other_right, "y", down)
    near = [mine, other, mine_left, other_left, mine_right, other_right, mine_far, other_far]
    swapped = [lax.ppermute(part, "core", [(0, 1), (1, 0)]) for part in near]

    slots = products(near + swapped, place, width, padded)
    returned = lax.all_to_all(
        slots.reshape(64, rows, LANES), ("z", "y"), split_axis=0, concat_axis=0, tiled=True
    )
    returned = lax.all_to_all(
        returned.reshape(2, -1, rows, LANES), "core", split_axis=0, concat_axis=0, tiled=True
    )
    returned = returned.reshape(2, matrices, 2, 4, rows, LANES)
    out_update, norms = regroup(returned, place, owner.reshape(matrices), width)
    return new_momentum, out_update, norms


def solution(mesh):
    experts, shards = mesh.devices.shape
    split = Mesh(mesh.devices.reshape(experts // 2, 2, 4, shards // 4), ("x", "core", "y", "z"))
    groups, rows = ("x", "core"), ("y", "z")
    return jax.shard_map(
        on_device,
        mesh=split,
        in_specs=(P(groups, rows, None), P(groups, rows, None), P(groups, None)),
        out_specs=(P(groups, rows, None), P(groups, rows, None), P(groups, rows)),
        check_vma=False,
    )
```

time: 172 us -> 164 us (0.953); the launches traced: 172 us -> 162 us
  waiting for transfers between devices: 102 us -> 7.03 us
  blocking collectives: 12.3 us -> 90.4 us
  starting transfers between devices: 10.6 us -> 40.4 us
  between operations: 14 us -> 0.92 us
  Pallas kernels: 28.8 us -> 22.5 us
  local copies, waits for them, and re-layouts: 4.07 us -> 0.04 us
    all_gather x1 -> x0, waiting for transfers between devices: 86.5 us -> none  [on_device(): lax.all_gather(mine.reshape(matrices * rows, columns), 'z', axis=0, tiled...]
    all_to_all x1 -> x4, blocking collectives: 12.3 us -> 90.4 us  [the longest x1 42.4 us: on_device(): lax.all_to_all(slots.reshape(64, rows, LANES), ('z', 'y'), split_axis=0,...]
    ppermute x0 -> x15, starting transfers between devices: none -> 40.4 us  [the longest x8 16.7 us: on_device(): swapped = [lax.ppermute(part, 'core', [(0, 1), (1, 0)]) for part in near]]
    all_to_all x1 -> x0, waiting for transfers between devices: 15.6 us -> none  [on_device(): lax.all_to_all(update.reshape(members, matrices, rows, width).swapaxes(0,...]
    all_to_all x1 -> x0, starting transfers between devices: 10.5 us -> none  [on_device(): lax.all_to_all(update.reshape(members, matrices, rows, width).swapaxes(0,...]
    ppermute x0 -> x15, waiting for transfers between devices: none -> 7.03 us  [the longest x1 5.34 us: on_device(): other_left = lax.ppermute(other, 'y', up)]
    pallas_call x4 -> x3, Pallas kernels: 28.8 us -> 22.5 us  [the longest x1 17.8 us: products(): pl.pallas_call(lambda *refs: products_kernel(width, padded, *refs), in_sp...]
    transpose x1 -> x0, local copies, waits for them, and re-layouts: 1.87 us -> none  [on_device(): update.reshape(members, matrices, rows, width).swapaxes(0, 1)]
  transfers between devices with their start and end apart: 2 -> 15, of which waited for: 2 -> 4; matrix products, arithmetic and copies ran while one was open for 1% -> 0% of each run, Pallas kernels for 6% -> 0%
where the time goes in v2:
time: 164 us; the launch traced here: 162 us
  blocking collectives  90.4 us (55%)
  starting transfers between devices  40.4 us (25%)
  Pallas kernels  22.5 us (14%)
  waiting for transfers between devices  7.03 us (4%)
    all_to_all x1, blocking collectives, on_device(): lax.all_to_all(slots.reshape(64, rows, LANES), ('z', 'y'), split_axis=0,...  42.4 us
    all_to_all x1, blocking collectives, on_device(): lax.all_to_all(halves.reshape(16, rows // 4, columns), 'z', split_axis=0,...  38 us
    pallas_call x1, Pallas kernels, products(): pl.pallas_call(lambda *refs: products_kernel(width, padded, *refs), in_sp...  17.8 us
    ppermute x8, starting transfers between devices, on_device(): swapped = [lax.ppermute(part, 'core', [(0, 1), (1, 0)]) for part in near]  16.7 us
    ppermute x1, starting transfers between devices, on_device(): other_far = lax.ppermute(other_right, 'y', down)  5.59 us
    ppermute x1, waiting for transfers between devices, on_device(): other_left = lax.ppermute(other, 'y', up)  5.34 us
    ppermute x1, starting transfers between devices, on_device(): other_right = lax.ppermute(other, 'y', down)  5.13 us
    all_to_all x1, blocking collectives, on_device(): lax.all_to_all(payload, 'core', split_axis=0, concat_axis=0, tiled=True)  5.07 us
  transfers between devices with their start and end apart: 15, of which 4 were waited for; matrix products, arithmetic and copies ran while one was open for 0% of the time, Pallas kernels for 0%

profile of v2, /device:TPU:6, one launch (start us, length us, event | category | flops | bytes accessed | tf_op | source)
XLA Modules:
  0.0 161.9 jit_solution(11420410581731006071)
XLA Ops:
  0.6 2.3 %momentum_step.1 = (f32[4,32,1408]{2,1,0:T(8,128)}, bf16[2,4,16,1408]{3,2,1,0:T(8,128)(2,1)}) custom-call(bf16[4,32,1408]{2,1,0:T(8,128)(2,1)} %grad_ref.1, f32[4,32,1408]{2,1,0:T(8,128)} %momentum_ref.1), custom_call_target="tpu_custom_call" | custom-call | tf_op jit(solution)/shard_map/momentum_step/pallas_call | solution.py:35
  2.9 5.1 %all_to_all.20 = bf16[2,4,16,1408]{3,2,1,0:T(8,128)(2,1)S(1)} all-to-all(bf16[2,4,16,1408]{3,2,1,0:T(8,128)(2,1)} %get-tuple-element.8), channel_id=1, replica_groups=mesh['x'=4,'core'=2,'y'=4,'z'=16] {'core'}, dimensions={0} | all-to-all | bytes 720896 | tf_op jit(solution)/shard_map/all_to_all | solution.py:196
  8.0 38.0 %all_to_all.21 = bf16[16,8,1408]{2,1,0:T(8,128)(2,1)S(1)} all-to-all(bf16[16,8,1408]{2,1,0:T(8,128)(2,1)S(1)} %bitcast.12), channel_id=1, replica_groups=mesh['x'=4,'core'=2,'y'=4,'z'=16] {'z'}, dimensions={0} | all-to-all | bytes 720896 | tf_op jit(solution)/shard_map/all_to_all | solution.py:197
  46.0 2.4 %collective-permute-start = (bf16[128,1408]{1,0:T(8,128)(2,1)S(1)}, bf16[128,1408]{1,0:T(8,128)(2,1)S(1)}, u32[]{:S(2)}, u32[]{:S(2)}) collective-permute-start(bf16[128,1408]{1,0:T(8,128)(2,1)S(1)} %bitcast.14), channel_id=1, source_target_pairs={{0,1},{1,0},{2,3},{3,2},{4,5},{5,4},{6,7},{7,6},{8,9},{9,8},{10,11... | collective-permute-start | bytes 1081352 | tf_op jit(solution)/shard_map/ppermute | solution.py:200
  48.4 4.9 %collective-permute-start.3 = (bf16[128,1408]{1,0:T(8,128)(2,1)S(1)}, bf16[128,1408]{1,0:T(8,128)(2,1)S(1)}, u32[]{:S(2)}, u32[]{:S(2)}) collective-permute-start(bf16[128,1408]{1,0:T(8,128)(2,1)S(1)} %bitcast.15), channel_id=1, source_target_pairs={{16,0},{32,16},{48,32},{0,48},{17,1},{33,17},{49,33},{1,49},{18,2}... | collective-permute-start | bytes 1081352 | tf_op jit(solution)/shard_map/ppermute | solution.py:202
  53.3 1.9 %collective-permute-start.1 = (bf16[128,1408]{1,0:T(8,128)(2,1)S(1)}, bf16[128,1408]{1,0:T(8,128)(2,1)S(1)}, u32[]{:S(2)}, u32[]{:S(2)}) collective-permute-start(bf16[128,1408]{1,0:T(8,128)(2,1)S(1)} %bitcast.16), channel_id=1, source_target_pairs={{0,16},{16,32},{32,48},{48,0},{1,17},{17,33},{33,49},{49,1},{2,18}... | collective-permute-start | bytes 1081352 | tf_op jit(solution)/shard_map/ppermute | solution.py:201
  55.2 1.9 %collective-permute-start.7 = (bf16[128,1408]{1,0:T(8,128)(2,1)S(1)}, bf16[128,1408]{1,0:T(8,128)(2,1)S(1)}, u32[]{:S(2)}, u32[]{:S(2)}) collective-permute-start(bf16[128,1408]{1,0:T(8,128)(2,1)S(1)} %bitcast.17), channel_id=1, source_target_pairs={{0,64},{64,0},{1,65},{65,1},{2,66},{66,2},{3,67},{67,3},{4,68},{68... | collective-permute-start | bytes 1081352 | tf_op jit(solution)/shard_map/ppermute | solution.py:208
  57.2 0.0 collective-permute-done.refs_2_
  57.2 5.1 %collective-permute-start.4 = (bf16[128,1408]{1,0:T(8,128)(2,1)S(1)}, bf16[128,1408]{1,0:T(8,128)(2,1)S(1)}, u32[]{:S(2)}, u32[]{:S(2)}) collective-permute-start(bf16[128,1408]{1,0:T(8,128)(2,1)S(1)} %collective-permute-done.refs_2_), channel_id=1, source_target_pairs={{16,0},{32,16},{48,32},{0,48},{17,1},{33,17},{49,33},{1,49},{18,2}... | collective-permute-start | bytes 1081352 | tf_op jit(solution)/shard_map/ppermute | solution.py:204
  62.3 0.0 collective-permute-done.3.refs_5_
  62.3 2.1 %collective-permute-start.11 = (bf16[128,1408]{1,0:T(8,128)(2,1)S(1)}, bf16[128,1408]{1,0:T(8,128)(2,1)S(1)}, u32[]{:S(2)}, u32[]{:S(2)}) collective-permute-start(bf16[128,1408]{1,0:T(8,128)(2,1)S(1)} %collective-permute-done.3.refs_5_), channel_id=1, source_target_pairs={{0,64},{64,0},{1,65},{65,1},{2,66},{66,2},{3,67},{67,3},{4,68},{68... | collective-permute-start | bytes 1081352 | tf_op jit(solution)/shard_map/ppermute | solution.py:208
  64.5 0.2 collective-permute-done.1.refs_3_
  64.7 2.0 %collective-permute-start.9 = (bf16[128,1408]{1,0:T(8,128)(2,1)S(1)}, bf16[128,1408]{1,0:T(8,128)(2,1)S(1)}, u32[]{:S(2)}, u32[]{:S(2)}) collective-permute-start(bf16[128,1408]{1,0:T(8,128)(2,1)S(1)} %collective-permute-done.1.refs_3_), channel_id=1, source_target_pairs={{0,64},{64,0},{1,65},{65,1},{2,66},{66,2},{3,67},{67,3},{4,68},{68... | collective-permute-start | bytes 1081352 | tf_op jit(solution)/shard_map/ppermute | solution.py:208
  66.7 1.9 %collective-permute-start.5 = (bf16[128,1408]{1,0:T(8,128)(2,1)S(1)}, bf16[128,1408]{1,0:T(8,128)(2,1)S(1)}, u32[]{:S(2)}, u32[]{:S(2)}) collective-permute-start(bf16[128,1408]{1,0:T(8,128)(2,1)S(1)} %collective-permute-done.1.refs_3_), channel_id=1, source_target_pairs={{0,16},{16,32},{32,48},{48,0},{1,17},{17,33},{33,49},{49,1},{2,18}... | collective-permute-start | bytes 1081352 | tf_op jit(solution)/shard_map/ppermute | solution.py:205
  68.7 1.9 %collective-permute-start.2 = (bf16[128,1408]{1,0:T(8,128)(2,1)S(1)}, bf16[128,1408]{1,0:T(8,128)(2,1)}, u32[]{:S(2)}, u32[]{:S(2)}) collective-permute-start(bf16[128,1408]{1,0:T(8,128)(2,1)S(1)} %collective-permute-done.refs_2_), channel_id=1, source_target_pairs={{0,16},{16,32},{32,48},{48,0},{1,17},{17,33},{33,49},{49,1},{2,18}... | collective-permute-start | bytes 1081352 | tf_op jit(solution)/shard_map/ppermute | solution.py:203
  70.6 0.1 collective-permute-done.4.refs_6_
  70.6 5.6 %collective-permute-start.6 = (bf16[128,1408]{1,0:T(8,128)(2,1)S(1)}, bf16[128,1408]{1,0:T(8,128)(2,1)}, u32[]{:S(2)}, u32[]{:S(2)}) collective-permute-start(bf16[128,1408]{1,0:T(8,128)(2,1)S(1)} %collective-permute-done.4.refs_6_), channel_id=1, source_target_pairs={{16,0},{32,16},{48,32},{0,48},{17,1},{33,17},{49,33},{1,49},{18,2}... | collective-permute-start | bytes 1081352 | tf_op jit(solution)/shard_map/ppermute | solution.py:206
  76.3 1.9 %collective-permute-start.8 = (bf16[128,1408]{1,0:T(8,128)(2,1)S(1)}, bf16[128,1408]{1,0:T(8,128)(2,1)}, u32[]{:S(2)}, u32[]{:S(2)}) collective-permute-start(bf16[128,1408]{1,0:T(8,128)(2,1)S(1)} %collective-permute-done.refs_2_), channel_id=1, source_target_pairs={{0,64},{64,0},{1,65},{65,1},{2,66},{66,2},{3,67},{67,3},{4,68},{68... | collective-permute-start | bytes 1081352 | tf_op jit(solution)/shard_map/ppermute | solution.py:208
  78.2 2.4 %collective-permute-start.12 = (bf16[128,1408]{1,0:T(8,128)(2,1)S(1)}, bf16[128,1408]{1,0:T(8,128)(2,1)}, u32[]{:S(2)}, u32[]{:S(2)}) collective-permute-start(bf16[128,1408]{1,0:T(8,128)(2,1)S(1)} %collective-permute-done.4.refs_6_), channel_id=1, source_target_pairs={{0,64},{64,0},{1,65},{65,1},{2,66},{66,2},{3,67},{67,3},{4,68},{68... | collective-permute-start | bytes 1081352 | tf_op jit(solution)/shard_map/ppermute | solution.py:208
  80.6 0.4 collective-permute-done.5.refs_7_
  81.1 1.9 %collective-permute-start.13 = (bf16[128,1408]{1,0:T(8,128)(2,1)S(1)}, bf16[128,1408]{1,0:T(8,128)(2,1)}, u32[]{:S(2)}, u32[]{:S(2)}) collective-permute-start(bf16[128,1408]{1,0:T(8,128)(2,1)S(1)} %collective-permute-done.5.refs_7_), channel_id=1, source_target_pairs={{0,64},{64,0},{1,65},{65,1},{2,66},{66,2},{3,67},{67,3},{4,68},{68... | collective-permute-start | bytes 1081352 | tf_op jit(solution)/shard_map/ppermute | solution.py:208
  83.0 5.3 %collective-permute-done.2.refs_4_ = bf16[128,1408]{1,0:T(8,128)(2,1)} collective-permute-done((bf16[128,1408]{1,0:T(8,128)(2,1)S(1)}, bf16[128,1408]{1,0:T(8,128)(2,1)}, u32[]{:S(2)}, u32[]{:S(2)}) %collective-permute-start.2) | collective-permute-done | bytes 360480 | tf_op jit(solution)/shard_map/ppermute | solution.py:203
  88.3 1.9 %collective-permute-start.10 = (bf16[128,1408]{1,0:T(8,128)(2,1)}, bf16[128,1408]{1,0:T(8,128)(2,1)}, u32[]{:S(2)}, u32[]{:S(2)}) collective-permute-start(bf16[128,1408]{1,0:T(8,128)(2,1)} %collective-permute-done.2.refs_4_), channel_id=1, source_target_pairs={{0,64},{64,0},{1,65},{65,1},{2,66},{66,2},{3,67},{67,3},{4,68},{68... | collective-permute-start | bytes 1081352 | tf_op jit(solution)/shard_map/ppermute | solution.py:208
  90.2 2.4 %collective-permute-start.14 = (bf16[128,1408]{1,0:T(8,128)(2,1)}, bf16[128,1408]{1,0:T(8,128)(2,1)}, u32[]{:S(2)}, u32[]{:S(2)}) collective-permute-start(bf16[128,1408]{1,0:T(8,128)(2,1)} %collective-permute-done.6.refs_8_), channel_id=1, source_target_pairs={{0,64},{64,0},{1,65},{65,1},{2,66},{66,2},{3,67},{67,3},{4,68},{68... | collective-permute-start | bytes 1081352 | tf_op jit(solution)/shard_map/ppermute | solution.py:208
  92.7 0.6 pad_add_fusion.refs_0_
  93.3 0.0 collective-permute-done.13.refs_15_
  93.3 0.0 collective-permute-done.12.refs_14_
  93.3 1.0 collective-permute-done.14.refs_16_
  94.3 17.8 %products.1 = bf16[16,4,32,128]{3,2,1,0:T(8,128)(2,1)} custom-call(s32[4]{0:T(128)} %pad_add_fusion.refs_0_, bf16[128,1408]{1,0:T(8,128)(2,1)} %bitcast.18, bf16[128,1408]{1,0:T(8,128)(2,1)} %copy-done.1, bf16[128,1408]{1,0:T(8,128)(2,1)} %copy-done.3, bf16[128,1408]{1,0:T(8,128)(2,1)} %collective-permute-done.2.refs_4_, bf16[128,1408]{1,0:T(8,128)(2,1)} %copy-done.2, ...), custom_call_target="tpu_custom_call" | custom-call | flops 5536481280 | bytes 5767168 | tf_op jit(solution)/shard_map/products/pallas_call | solution.py:129
  112.1 42.4 %all_to_all.22 = bf16[64,32,128]{2,1,0:T(8,128)(2,1)S(1)} all-to-all(bf16[64,32,128]{2,1,0:T(8,128)(2,1)} %bitcast.13), channel_id=1, replica_groups=mesh['x'=4,'core'=2,'y'=4,'z'=16] {'z','y'}, dimensions={0} | all-to-all | bytes 1048576 | tf_op jit(solution)/shard_map/all_to_all | solution.py:211
  154.5 4.9 %all_to_all.23 = bf16[2,32,32,128]{3,2,1,0:T(8,128)(2,1)} all-to-all(bf16[2,32,32,128]{3,2,1,0:T(8,128)(2,1)S(1)} %bitcast.11), channel_id=1, replica_groups=mesh['x'=4,'core'=2,'y'=4,'z'=16] {'core'}, dimensions={0} | all-to-all | bytes 1048576 | tf_op jit(solution)/shard_map/all_to_all | solution.py:214
  159.4 2.5 %regroup.1 = (bf16[4,32,1408]{2,1,0:T(8,128)(2,1)}, f32[1,88]{1,0:T(1,128)}) custom-call(s32[4]{0:T(128)} %pad_add_fusion.refs_0_, s32[4]{0:T(128)} %bitcast.19, bf16[2,4,2,4,32,128]{5,4,3,2,1,0:T(8,128)(2,1)} %bitcast.10), custom_call_target="tpu_custom_call" | custom-call | tf_op jit(solution)/shard_map/regroup/pallas_call | solution.py:173
  (24 shorter events, 0.1 us)
Async XLA Ops:
  46.0 48.3 %copy-start = (bf16[16,8,1408]{2,1,0:T(8,128)(2,1)}, bf16[16,8,1408]{2,1,0:T(8,128)(2,1)S(1)}, u32[]{:S(2)}) copy-start(bf16[16,8,1408]{2,1,0:T(8,128)(2,1)S(1)} %all_to_all.21) | copy-start | bytes 1081348
  46.0 11.2 %collective-permute-start = (bf16[128,1408]{1,0:T(8,128)(2,1)S(1)}, bf16[128,1408]{1,0:T(8,128)(2,1)S(1)}, u32[]{:S(2)}, u32[]{:S(2)}) collective-permute-start(bf16[128,1408]{1,0:T(8,128)(2,1)S(1)} %bitcast.14), channel_id=1, source_target_pairs={{0,1},{1,0},{2,3},{3,2},{4,5},{5,4},{6,7},{7,6},{8,9},{9,8},{10,11... | collective-permute-start | bytes 1081352 | tf_op jit(solution)/shard_map/ppermute | solution.py:200
  48.4 14.0 %collective-permute-start.3 = (bf16[128,1408]{1,0:T(8,128)(2,1)S(1)}, bf16[128,1408]{1,0:T(8,128)(2,1)S(1)}, u32[]{:S(2)}, u32[]{:S(2)}) collective-permute-start(bf16[128,1408]{1,0:T(8,128)(2,1)S(1)} %bitcast.15), channel_id=1, source_target_pairs={{16,0},{32,16},{48,32},{0,48},{17,1},{33,17},{49,33},{1,49},{18,2}... | collective-permute-start | bytes 1081352 | tf_op jit(solution)/shard_map/ppermute | solution.py:202
  53.3 11.3 %collective-permute-start.1 = (bf16[128,1408]{1,0:T(8,128)(2,1)S(1)}, bf16[128,1408]{1,0:T(8,128)(2,1)S(1)}, u32[]{:S(2)}, u32[]{:S(2)}) collective-permute-start(bf16[128,1408]{1,0:T(8,128)(2,1)S(1)} %bitcast.16), channel_id=1, source_target_pairs={{0,16},{16,32},{32,48},{48,0},{1,17},{17,33},{33,49},{49,1},{2,18}... | collective-permute-start | bytes 1081352 | tf_op jit(solution)/shard_map/ppermute | solution.py:201
  55.2 13.4 %collective-permute-start.7 = (bf16[128,1408]{1,0:T(8,128)(2,1)S(1)}, bf16[128,1408]{1,0:T(8,128)(2,1)S(1)}, u32[]{:S(2)}, u32[]{:S(2)}) collective-permute-start(bf16[128,1408]{1,0:T(8,128)(2,1)S(1)} %bitcast.17), channel_id=1, source_target_pairs={{0,64},{64,0},{1,65},{65,1},{2,66},{66,2},{3,67},{67,3},{4,68},{68... | collective-permute-start | bytes 1081352 | tf_op jit(solution)/shard_map/ppermute | solution.py:208
  57.2 37.1 %copy-start.1 = (bf16[128,1408]{1,0:T(8,128)(2,1)}, bf16[128,1408]{1,0:T(8,128)(2,1)S(1)}, u32[]{:S(2)}) copy-start(bf16[128,1408]{1,0:T(8,128)(2,1)S(1)} %collective-permute-done.refs_2_) | copy-start | bytes 1081348
  57.2 13.5 %collective-permute-start.4 = (bf16[128,1408]{1,0:T(8,128)(2,1)S(1)}, bf16[128,1408]{1,0:T(8,128)(2,1)S(1)}, u32[]{:S(2)}, u32[]{:S(2)}) collective-permute-start(bf16[128,1408]{1,0:T(8,128)(2,1)S(1)} %collective-permute-done.refs_2_), channel_id=1, source_target_pairs={{16,0},{32,16},{48,32},{0,48},{17,1},{33,17},{49,33},{1,49},{18,2}... | collective-permute-start | bytes 1081352 | tf_op jit(solution)/shard_map/ppermute | solution.py:204
  62.3 32.0 %copy-start.2 = (bf16[128,1408]{1,0:T(8,128)(2,1)}, bf16[128,1408]{1,0:T(8,128)(2,1)S(1)}, u32[]{:S(2)}) copy-start(bf16[128,1408]{1,0:T(8,128)(2,1)S(1)} %collective-permute-done.3.refs_5_) | copy-start | bytes 1081348
  62.3 13.9 %collective-permute-start.11 = (bf16[128,1408]{1,0:T(8,128)(2,1)S(1)}, bf16[128,1408]{1,0:T(8,128)(2,1)S(1)}, u32[]{:S(2)}, u32[]{:S(2)}) collective-permute-start(bf16[128,1408]{1,0:T(8,128)(2,1)S(1)} %collective-permute-done.3.refs_5_), channel_id=1, source_target_pairs={{0,64},{64,0},{1,65},{65,1},{2,66},{66,2},{3,67},{67,3},{4,68},{68... | collective-permute-start | bytes 1081352 | tf_op jit(solution)/shard_map/ppermute | solution.py:208
  64.6 29.6 %copy-start.3 = (bf16[128,1408]{1,0:T(8,128)(2,1)}, bf16[128,1408]{1,0:T(8,128)(2,1)S(1)}, u32[]{:S(2)}) copy-start(bf16[128,1408]{1,0:T(8,128)(2,1)S(1)} %collective-permute-done.1.refs_3_) | copy-start | bytes 1081348
  64.7 13.5 %collective-permute-start.9 = (bf16[128,1408]{1,0:T(8,128)(2,1)S(1)}, bf16[128,1408]{1,0:T(8,128)(2,1)S(1)}, u32[]{:S(2)}, u32[]{:S(2)}) collective-permute-start(bf16[128,1408]{1,0:T(8,128)(2,1)S(1)} %collective-permute-done.1.refs_3_), channel_id=1, source_target_pairs={{0,64},{64,0},{1,65},{65,1},{2,66},{66,2},{3,67},{67,3},{4,68},{68... | collective-permute-start | bytes 1081352 | tf_op jit(solution)/shard_map/ppermute | solution.py:208
  66.7 14.4 %collective-permute-start.5 = (bf16[128,1408]{1,0:T(8,128)(2,1)S(1)}, bf16[128,1408]{1,0:T(8,128)(2,1)S(1)}, u32[]{:S(2)}, u32[]{:S(2)}) collective-permute-start(bf16[128,1408]{1,0:T(8,128)(2,1)S(1)} %collective-permute-done.1.refs_3_), channel_id=1, source_target_pairs={{0,16},{16,32},{32,48},{48,0},{1,17},{17,33},{33,49},{49,1},{2,18}... | collective-permute-start | bytes 1081352 | tf_op jit(solution)/shard_map/ppermute | solution.py:205
  68.6 25.7 %copy-start.4 = (bf16[128,1408]{1,0:T(8,128)(2,1)}, bf16[128,1408]{1,0:T(8,128)(2,1)S(1)}, u32[]{:S(2)}) copy-start(bf16[128,1408]{1,0:T(8,128)(2,1)S(1)} %collective-permute-done.7.refs_9_) | copy-start | bytes 1081348
  68.7 19.7 %collective-permute-start.2 = (bf16[128,1408]{1,0:T(8,128)(2,1)S(1)}, bf16[128,1408]{1,0:T(8,128)(2,1)}, u32[]{:S(2)}, u32[]{:S(2)}) collective-permute-start(bf16[128,1408]{1,0:T(8,128)(2,1)S(1)} %collective-permute-done.refs_2_), channel_id=1, source_target_pairs={{0,16},{16,32},{32,48},{48,0},{1,17},{17,33},{33,49},{49,1},{2,18}... | collective-permute-start | bytes 1081352 | tf_op jit(solution)/shard_map/ppermute | solution.py:203
  70.6 23.7 %copy-start.5 = (bf16[128,1408]{1,0:T(8,128)(2,1)}, bf16[128,1408]{1,0:T(8,128)(2,1)S(1)}, u32[]{:S(2)}) copy-start(bf16[128,1408]{1,0:T(8,128)(2,1)S(1)} %collective-permute-done.4.refs_6_) | copy-start | bytes 1081348
  70.6 19.6 %collective-permute-start.6 = (bf16[128,1408]{1,0:T(8,128)(2,1)S(1)}, bf16[128,1408]{1,0:T(8,128)(2,1)}, u32[]{:S(2)}, u32[]{:S(2)}) collective-permute-start(bf16[128,1408]{1,0:T(8,128)(2,1)S(1)} %collective-permute-done.4.refs_6_), channel_id=1, source_target_pairs={{16,0},{32,16},{48,32},{0,48},{17,1},{33,17},{49,33},{1,49},{18,2}... | collective-permute-start | bytes 1081352 | tf_op jit(solution)/shard_map/ppermute | solution.py:206
  76.2 18.1 %copy-start.6 = (bf16[128,1408]{1,0:T(8,128)(2,1)}, bf16[128,1408]{1,0:T(8,128)(2,1)S(1)}, u32[]{:S(2)}) copy-start(bf16[128,1408]{1,0:T(8,128)(2,1)S(1)} %collective-permute-done.11.refs_13_) | copy-start | bytes 1081348
  76.3 17.0 %collective-permute-start.8 = (bf16[128,1408]{1,0:T(8,128)(2,1)S(1)}, bf16[128,1408]{1,0:T(8,128)(2,1)}, u32[]{:S(2)}, u32[]{:S(2)}) collective-permute-start(bf16[128,1408]{1,0:T(8,128)(2,1)S(1)} %collective-permute-done.refs_2_), channel_id=1, source_target_pairs={{0,64},{64,0},{1,65},{65,1},{2,66},{66,2},{3,67},{67,3},{4,68},{68... | collective-permute-start | bytes 1081352 | tf_op jit(solution)/shard_map/ppermute | solution.py:208
  78.2 16.1 %copy-start.7 = (bf16[128,1408]{1,0:T(8,128)(2,1)}, bf16[128,1408]{1,0:T(8,128)(2,1)S(1)}, u32[]{:S(2)}) copy-start(bf16[128,1408]{1,0:T(8,128)(2,1)S(1)} %collective-permute-done.9.refs_11_) | copy-start | bytes 1081348
  78.2 15.1 %collective-permute-start.12 = (bf16[128,1408]{1,0:T(8,128)(2,1)S(1)}, bf16[128,1408]{1,0:T(8,128)(2,1)}, u32[]{:S(2)}, u32[]{:S(2)}) collective-permute-start(bf16[128,1408]{1,0:T(8,128)(2,1)S(1)} %collective-permute-done.4.refs_6_), channel_id=1, source_target_pairs={{0,64},{64,0},{1,65},{65,1},{2,66},{66,2},{3,67},{67,3},{4,68},{68... | collective-permute-start | bytes 1081352 | tf_op jit(solution)/shard_map/ppermute | solution.py:208
  81.1 13.3 %copy-start.8 = (bf16[128,1408]{1,0:T(8,128)(2,1)}, bf16[128,1408]{1,0:T(8,128)(2,1)S(1)}, u32[]{:S(2)}) copy-start(bf16[128,1408]{1,0:T(8,128)(2,1)S(1)} %collective-permute-done.5.refs_7_) | copy-start | bytes 1081348
  81.1 12.2 %collective-permute-start.13 = (bf16[128,1408]{1,0:T(8,128)(2,1)S(1)}, bf16[128,1408]{1,0:T(8,128)(2,1)}, u32[]{:S(2)}, u32[]{:S(2)}) collective-permute-start(bf16[128,1408]{1,0:T(8,128)(2,1)S(1)} %collective-permute-done.5.refs_7_), channel_id=1, source_target_pairs={{0,64},{64,0},{1,65},{65,1},{2,66},{66,2},{3,67},{67,3},{4,68},{68... | collective-permute-start | bytes 1081352 | tf_op jit(solution)/shard_map/ppermute | solution.py:208
  88.3 5.0 %collective-permute-start.10 = (bf16[128,1408]{1,0:T(8,128)(2,1)}, bf16[128,1408]{1,0:T(8,128)(2,1)}, u32[]{:S(2)}, u32[]{:S(2)}) collective-permute-start(bf16[128,1408]{1,0:T(8,128)(2,1)} %collective-permute-done.2.refs_4_), channel_id=1, source_target_pairs={{0,64},{64,0},{1,65},{65,1},{2,66},{66,2},{3,67},{67,3},{4,68},{68... | collective-permute-start | bytes 1081352 | tf_op jit(solution)/shard_map/ppermute | solution.py:208
  90.2 4.0 %collective-permute-start.14 = (bf16[128,1408]{1,0:T(8,128)(2,1)}, bf16[128,1408]{1,0:T(8,128)(2,1)}, u32[]{:S(2)}, u32[]{:S(2)}) collective-permute-start(bf16[128,1408]{1,0:T(8,128)(2,1)} %collective-permute-done.6.refs_8_), channel_id=1, source_target_pairs={{0,64},{64,0},{1,65},{65,1},{2,66},{66,2},{3,67},{67,3},{4,68},{68... | collective-permute-start | bytes 1081352 | tf_op jit(solution)/shard_map/ppermute | solution.py:208

commit v3 on v2

v3 whole, which is shorter than its diff:
```python
import math

import jax
import jax.numpy as jnp
from jax import lax
from jax.experimental import pallas as pl
from jax.experimental.pallas import tpu as pltpu
from jax.sharding import Mesh, PartitionSpec as P

DECAY = 0.95
COEF_A = 3.4445
COEF_B = -4.775
COEF_C = 2.0315
EPSILON = 1e-07

F32 = jnp.float32
BF16 = jnp.bfloat16
VMEM_LIMIT = 56 * 1024 * 1024
LANES = 128
SECTION_SIZES = (1, 1, 1, 1, 2, 2, 2, 2, 2, 2)
SLOT_ROWS = 24
HIGH_LANE = 96
LOW_LANE = 112


def momentum_kernel(grad_ref, momentum_ref, new_ref, payload_ref):
    new = DECAY * momentum_ref[...] + grad_ref[...].astype(F32)
    new_ref[...] = new
    rounded = new.astype(BF16)
    half = payload_ref.shape[2]
    payload_ref[0] = rounded[:, :half]
    payload_ref[1] = rounded[:, half:]


def momentum_step(grad, momentum):
    matrices, rows, columns = grad.shape
    vmem = pl.BlockSpec(memory_space=pltpu.VMEM)
    return pl.pallas_call(
        momentum_kernel,
        in_specs=[vmem, vmem],
        out_specs=[vmem, vmem],
        out_shape=[
            jax.ShapeDtypeStruct(grad.shape, F32),
            jax.ShapeDtypeStruct((2, matrices, rows // 2, columns), BF16),
        ],
        compiler_params=pltpu.CompilerParams(vmem_limit_bytes=VMEM_LIMIT),
        name="momentum_step",
    )(grad, momentum)


def times(block, x_ref):
    return jnp.dot(block, x_ref[...], preferred_element_type=F32)


def times_transposed(block, x_ref):
    return lax.dot_general(
        block, x_ref[...], (((1,), (1,)), ((), ())), preferred_element_type=F32
    )


def products_kernel(width, padded, place_ref, *refs):
    count = len(SECTION_SIZES)
    sections = refs[:count]
    slots_ref, x_ref, sems = refs[count:]
    core, y, b = place_ref[0], place_ref[1], place_ref[2]
    total_rows, columns = x_ref.shape
    section_rows = total_rows // 16
    copies = []
    at = 0
    for ref, size in zip(sections, SECTION_SIZES):
        rows = pl.ds(at * section_rows, size * section_rows)
        copies.append(pltpu.make_async_copy(ref, x_ref.at[rows], sems.at[len(copies)]))
        at += size
    for copy in copies:
        copy.start()
    total = jnp.zeros((16, columns), F32)
    at = 0
    for copy, size in zip(copies, SECTION_SIZES):
        copy.wait()
        for low in range(at * section_rows, (at + size) * section_rows, 16):
            piece = x_ref[low : low + 16, :].astype(F32)
            total = total + piece * piece
        at += size
    scale = 0.5 * math.sqrt(columns) / (jnp.sqrt(jnp.sum(total, keepdims=True)) + EPSILON)
    start = width * (core * 8 + y * 2 + b)
    row = lax.broadcasted_iota(jnp.int32, (padded, columns), 0)
    column = lax.broadcasted_iota(jnp.int32, (padded, columns), 1)
    identity = ((column == row + start) & (row < width)).astype(F32)
    own = times_transposed(identity.astype(BF16), x_ref).astype(BF16)
    gram = ((scale * scale) * times(own, x_ref)).astype(BF16)
    lifted = (scale * times_transposed(gram, x_ref)).astype(BF16)
    square = scale * times(lifted, x_ref)
    poly = (COEF_B * gram.astype(F32) + COEF_C * square).astype(BF16)
    ortho = scale * (COEF_A * own.astype(F32) + times_transposed(poly, x_ref))
    cross = (scale * times(ortho.astype(BF16), x_ref)).astype(BF16)
    first = (scale * times_transposed(cross, x_ref)).astype(BF16)
    second = (scale * times(first, x_ref)).astype(BF16)
    third = (scale * times_transposed(second, x_ref)).astype(BF16)
    fourth = scale * times(third, x_ref)
    resid = (
        COEF_A * cross.astype(F32) + COEF_B * second.astype(F32) + COEF_C * fourth - identity
    )
    norms = jnp.sqrt(jnp.sum(resid * resid, axis=1, keepdims=True))
    high = norms.astype(BF16).astype(F32)
    low = norms - high
    lane = lax.broadcasted_iota(jnp.int32, (8, LANES), 1)
    extra = jnp.zeros((8, LANES), F32)
    for part in range(width // 8):
        cut = slice(8 * part, 8 * part + 8)
        extra = jnp.where(lane == HIGH_LANE + part, high[cut], extra)
        extra = jnp.where(lane == LOW_LANE + part, low[cut], extra)
    update = math.sqrt(total_rows) * ortho
    below = jnp.zeros((LANES - padded, section_rows), F32)
    spare = lax.broadcasted_iota(jnp.int32, (16, 8, LANES), 2) >= width

    def turned(at):
        piece = update[:, at * section_rows : (at + 1) * section_rows]
        return jnp.concatenate([piece, below], axis=0).T.reshape(16, 8, LANES)

    def spill(rows, by):
        return jnp.where(spare, pltpu.roll(rows, by, 2), 0.0)

    for offset, flip, mine, other in (
        (0, 0, (0, 2), (1, 3)),
        (3 - 2 * core, 0, (4, 6), (5, 7)),
        (1 + 2 * core, 0, (9, 11), (8, 10)),
        (2, core, (12, 15), (13, 14)),
    ):
        swap = (flip ^ b) == 1
        parts = []
        for pair in (mine, other):
            one, two = turned(pair[0]), turned(pair[1])
            parts.append((jnp.where(swap, two, one), jnp.where(swap, one, two)))
        tiles = [jnp.where(core == 0, parts[0][i], parts[1][i]) for i in range(2)]
        tiles += [jnp.where(core == 0, parts[1][i], parts[0][i]) for i in range(2)]
        last = tiles[3]
        packed = jnp.concatenate(
            [
                tiles[0] + spill(last, 88),
                tiles[1] + spill(last, 48),
                tiles[2] + spill(last, 8) + extra,
            ],
            axis=1,
        )
        slots_ref[:, (y + offset) % 4] = packed.astype(BF16)


def products(sections, place, width, padded):
    columns = sections[0].shape[1]
    total_rows = sum(part.shape[0] for part in sections)
    return pl.pallas_call(
        lambda *refs: products_kernel(width, padded, *refs),
        in_specs=[pl.BlockSpec(memory_space=pltpu.SMEM)]
        + [pl.BlockSpec(memory_space=pl.ANY)] * len(sections),
        out_specs=pl.BlockSpec(memory_space=pltpu.VMEM),
        out_shape=jax.ShapeDtypeStruct((16, 4, SLOT_ROWS, LANES), BF16),
        scratch_shapes=[
            pltpu.VMEM((total_rows, columns), BF16),
            pltpu.SemaphoreType.DMA((len(sections),)),
        ],
        compiler_params=pltpu.CompilerParams(vmem_limit_bytes=VMEM_LIMIT),
        cost_estimate=pl.CostEstimate(
            flops=20 * padded * total_rows * columns,
            bytes_accessed=2 * total_rows * columns,
            transcendentals=0,
        ),
        name="products",
    )(place, *sections)


def regroup_kernel(width, place_ref, owner_ref, returned_ref, update_ref, norms_ref):
    y, z = place_ref[1], place_ref[3]
    matrices = update_ref.shape[0]
    lane = lax.broadcasted_iota(jnp.int32, (8, LANES), 1)
    for m in range(matrices):
        for at in range(16):
            core, source_y, b = at // 8, (at // 2) % 4, at % 2
            slot = returned_ref[core, m, b, source_y].astype(F32)
            last = jnp.where(
                lane < 40,
                pltpu.roll(slot[:8], 40, 1),
                jnp.where(lane < 80, pltpu.roll(slot[8:16], 80, 1), pltpu.roll(slot[16:], 120, 1)),
            )
            rows = jnp.concatenate([slot, last], axis=0).astype(BF16)
            update_ref[m, :, at * width : (at + 1) * width] = rows[:, :width]

        @pl.when(owner_ref[m] == y)
        def _():
            slot = returned_ref[z // 8, m, z % 2, (z // 2) % 4].astype(F32)
            turned = jnp.concatenate([slot[16:], slot], axis=0).T
            for part in range(width // 8):
                value = turned[HIGH_LANE + part : HIGH_LANE + part + 1, :8]
                value = value + turned[LOW_LANE + part : LOW_LANE + part + 1, :8]
                norms_ref[:, 8 * part : 8 * part + 8] = value


def regroup(returned, place, owner, width):
    matrices = returned.shape[1]
    smem = pl.BlockSpec(memory_space=pltpu.SMEM)
    vmem = pl.BlockSpec(memory_space=pltpu.VMEM)
    return pl.pallas_call(
        lambda *refs: regroup_kernel(width, *refs),
        in_specs=[smem, smem, vmem],
        out_specs=[vmem, vmem],
        out_shape=[
            jax.ShapeDtypeStruct((matrices, SLOT_ROWS + 8, 16 * width), BF16),
            jax.ShapeDtypeStruct((1, width), F32),
        ],
        compiler_params=pltpu.CompilerParams(vmem_limit_bytes=VMEM_LIMIT),
        name="regroup",
    )(place, owner, returned)


def on_device(grad, momentum, owner):
    matrices, rows, columns = grad.shape
    width = columns // 16
    padded = -(-width // 16) * 16
    core, y, z = lax.axis_index("core"), lax.axis_index("y"), lax.axis_index("z")
    place = jnp.stack([core, y, z % 2, z]).astype(jnp.int32)
    ring = [(i, (i + 1) % 4) for i in range(4)] + [(4 + i, 4 + (i + 3) % 4) for i in range(4)]
    swap = [(0, 1), (1, 0)]

    new_momentum, payload = momentum_step(grad, momentum)
    halves = lax.all_to_all(payload, "core", split_axis=0, concat_axis=0, tiled=True)
    mine = lax.all_to_all(
        halves.reshape(16, rows // 4, columns), "z", split_axis=0, concat_axis=0, tiled=True
    ).reshape(-1, columns)
    other = lax.ppermute(mine, "z", [(i, i ^ 1) for i in range(16)])
    mine_swapped = lax.ppermute(mine, "core", swap)
    both_mine = jnp.concatenate([mine, mine_swapped], axis=0)
    near_mine = lax.ppermute(both_mine, ("core", "y"), ring)
    other_swapped = lax.ppermute(other, "core", swap)
    both_other = jnp.concatenate([other, other_swapped], axis=0)
    near_other = lax.ppermute(both_other, ("core", "y"), ring)
    far = lax.ppermute(jnp.where(core == 0, near_mine, near_other), ("core", "y"), ring)
    near_mine_swapped = lax.ppermute(near_mine, "core", swap)
    near_other_swapped = lax.ppermute(near_other, "core", swap)
    far_swapped = lax.ppermute(far, "core", swap)
    sections = [mine, mine_swapped, other, other_swapped, near_mine, near_other]
    sections += [near_mine_swapped, near_other_swapped, far, far_swapped]

    slots = products(sections, place, width, padded)
    returned = lax.all_to_all(
        slots.reshape(64, SLOT_ROWS, LANES), ("z", "y"), split_axis=0, concat_axis=0, tiled=True
    )
    returned = lax.all_to_all(
        returned.reshape(2, -1, SLOT_ROWS, LANES), "core", split_axis=0, concat_axis=0, tiled=True
    )
    returned = returned.reshape(2, matrices, 2, 4, SLOT_ROWS, LANES)
    out_update, norms = regroup(returned, place, owner.reshape(matrices), width)
    return new_momentum, out_update, norms


def solution(mesh):
    experts, shards = mesh.devices.shape
    split = Mesh(mesh.devices.reshape(experts // 2, 2, 4, shards // 4), ("x", "core", "y", "z"))
    groups, rows = ("x", "core"), ("y", "z")
    return jax.shard_map(
        on_device,
        mesh=split,
        in_specs=(P(groups, rows, None), P(groups, rows, None), P(groups, None)),
        out_specs=(P(groups, rows, None), P(groups, rows, None), P(groups, rows)),
        check_vma=False,
    )
```

time: 164 us -> 163 us (level)
  waiting for transfers between devices: 7.03 us -> 27.7 us
  starting transfers between devices: 40.4 us -> 22.9 us
  blocking collectives: 90.4 us -> 85.2 us
    ppermute x14 -> x8, starting transfers between devices: 38.1 us -> 20.5 us  [the longest x1 3.63 us: on_device(): near_mine_swapped = lax.ppermute(near_mine, 'core', swap)]
    ppermute x14 -> x8, waiting for transfers between devices: 7.03 us -> 22.5 us  [the longest x1 7.72 us: on_device(): near_other = lax.ppermute(both_other, ('core', 'y'), ring)]
    all_to_all x2, blocking collectives: 47.3 us -> 42.1 us  [the longest x1 37.3 us: on_device(): lax.all_to_all(slots.reshape(64, SLOT_ROWS, LANES), ('z', 'y'), split_axi...]
    ppermute x1, waiting for transfers between devices: 0.01 us -> 5.11 us  [on_device(): other = lax.ppermute(mine, 'z', [(i, i ^ 1) for i in range(16)])]
  transfers between devices with their start and end apart: 15 -> 9, of which waited for: 4 -> 5; matrix products, arithmetic and copies ran while one was open for 0% -> 0% of each run, Pallas kernels for 0% -> 0%
where the time goes in v3:
time: 163 us; the launch traced here: 161 us
  blocking collectives  85.2 us (52%)
  waiting for transfers between devices  27.7 us (17%)
  starting transfers between devices  22.9 us (14%)
  Pallas kernels  22.6 us (14%)
    all_to_all x1, blocking collectives, on_device(): lax.all_to_all(halves.reshape(16, rows // 4, columns), 'z', split_axis=0,...  38 us
    all_to_all x1, blocking collectives, on_device(): lax.all_to_all(slots.reshape(64, SLOT_ROWS, LANES), ('z', 'y'), split_axi...  37.3 us
    pallas_call x1, Pallas kernels, products(): pl.pallas_call(lambda *refs: products_kernel(width, padded, *refs), in_sp...  17.6 us
    ppermute x1, waiting for transfers between devices, on_device(): near_other = lax.ppermute(both_other, ('core', 'y'), ring)  7.72 us
    ppermute x1, waiting for transfers between devices, on_device(): near_mine = lax.ppermute(both_mine, ('core', 'y'), ring)  6.64 us
    ppermute x1, waiting for transfers between devices, on_device(): lax.ppermute(jnp.where(core == 0, near_mine, near_other), ('core', 'y'),...  6.53 us
    ppermute x1, waiting for transfers between devices, on_device(): other = lax.ppermute(mine, 'z', [(i, i ^ 1) for i in range(16)])  5.11 us
    all_to_all x1, blocking collectives, on_device(): lax.all_to_all(payload, 'core', split_axis=0, concat_axis=0, tiled=True)  5.07 us
  transfers between devices with their start and end apart: 9, of which 5 were waited for; matrix products, arithmetic and copies ran while one was open for 0% of the time, Pallas kernels for 0%

profile of v3, /device:TPU:6, one launch (start us, length us, event | category | flops | bytes accessed | tf_op | source)
XLA Modules:
  0.0 161.3 jit_solution(10657574959797515433)
XLA Ops:
  0.6 2.3 %momentum_step.1 = (f32[4,32,1408]{2,1,0:T(8,128)}, bf16[2,4,16,1408]{3,2,1,0:T(8,128)(2,1)}) custom-call(bf16[4,32,1408]{2,1,0:T(8,128)(2,1)} %grad_ref.1, f32[4,32,1408]{2,1,0:T(8,128)} %momentum_ref.1), custom_call_target="tpu_custom_call" | custom-call | tf_op jit(solution)/shard_map/momentum_step/pallas_call | solution.py:38
  2.9 5.1 %all_to_all.20 = bf16[2,4,16,1408]{3,2,1,0:T(8,128)(2,1)S(1)} all-to-all(bf16[2,4,16,1408]{3,2,1,0:T(8,128)(2,1)} %get-tuple-element.8), channel_id=1, replica_groups=mesh['x'=4,'core'=2,'y'=4,'z'=16] {'core'}, dimensions={0} | all-to-all | bytes 720896 | tf_op jit(solution)/shard_map/all_to_all | solution.py:224
  8.0 38.0 %all_to_all.21 = bf16[16,8,1408]{2,1,0:T(8,128)(2,1)S(1)} all-to-all(bf16[16,8,1408]{2,1,0:T(8,128)(2,1)S(1)} %bitcast.12), channel_id=1, replica_groups=mesh['x'=4,'core'=2,'y'=4,'z'=16] {'z'}, dimensions={0} | all-to-all | bytes 720896 | tf_op jit(solution)/shard_map/all_to_all | solution.py:225
  46.0 2.4 %collective-permute-start.1 = (bf16[128,1408]{1,0:T(8,128)(2,1)S(1)}, bf16[128,1408]{1,0:T(8,128)(2,1)S(1)}, u32[]{:S(2)}, u32[]{:S(2)}) collective-permute-start(bf16[128,1408]{1,0:T(8,128)(2,1)S(1)} %bitcast.13), channel_id=1, source_target_pairs={{0,1},{1,0},{2,3},{3,2},{4,5},{5,4},{6,7},{7,6},{8,9},{9,8},{10,11... | collective-permute-start | bytes 1081352 | tf_op jit(solution)/shard_map/ppermute | solution.py:228
  48.4 1.9 %collective-permute-start = (bf16[128,1408]{1,0:T(8,128)(2,1)S(1)}, bf16[128,1408]{1,0:T(8,128)(2,1)S(1)}, u32[]{:S(2)}, u32[]{:S(2)}) collective-permute-start(bf16[128,1408]{1,0:T(8,128)(2,1)S(1)} %bitcast.14), channel_id=1, source_target_pairs={{0,64},{64,0},{1,65},{65,1},{2,66},{66,2},{3,67},{67,3},{4,68},{68... | collective-permute-start | bytes 1081352 | tf_op jit(solution)/shard_map/ppermute | solution.py:229
  50.3 5.1 %collective-permute-done.1.refs_3_ = bf16[128,1408]{1,0:T(8,128)(2,1)S(1)} collective-permute-done((bf16[128,1408]{1,0:T(8,128)(2,1)S(1)}, bf16[128,1408]{1,0:T(8,128)(2,1)S(1)}, u32[]{:S(2)}, u32[]{:S(2)}) %collective-permute-start.1) | collective-permute-done | bytes 360480 | tf_op jit(solution)/shard_map/ppermute | solution.py:228
  55.4 1.9 %collective-permute-start.2 = (bf16[128,1408]{1,0:T(8,128)(2,1)S(1)}, bf16[128,1408]{1,0:T(8,128)(2,1)S(1)}, u32[]{:S(2)}, u32[]{:S(2)}) collective-permute-start(bf16[128,1408]{1,0:T(8,128)(2,1)S(1)} %collective-permute-done.1.refs_3_), channel_id=1, source_target_pairs={{0,64},{64,0},{1,65},{65,1},{2,66},{66,2},{3,67},{67,3},{4,68},{68... | collective-permute-start | bytes 1081352 | tf_op jit(solution)/shard_map/ppermute | solution.py:232
  57.3 0.0 collective-permute-done.refs_2_
  57.4 0.1 pad_maximum_fusion
  57.4 0.7 copy-done.4
  58.1 3.5 %collective-permute-start.3 = (bf16[256,1408]{1,0:T(8,128)(2,1)S(1)}, bf16[256,1408]{1,0:T(8,128)(2,1)S(1)}, u32[]{:S(2)}, u32[]{:S(2)}) collective-permute-start(bf16[256,1408]{1,0:T(8,128)(2,1)S(1)} %pad_maximum_fusion), channel_id=1, source_target_pairs={{0,16},{16,32},{32,48},{48,0},{64,112},{80,64},{96,80},{112,96},{1... | collective-permute-start | bytes 2162696 | tf_op jit(solution)/shard_map/ppermute | solution.py:231
  61.6 0.0 collective-permute-done.2.refs_4_
  61.6 0.1 pad_maximum_fusion.1
  61.7 0.7 copy-done.5
  62.3 3.5 %collective-permute-start.4 = (bf16[256,1408]{1,0:T(8,128)(2,1)S(1)}, bf16[256,1408]{1,0:T(8,128)(2,1)S(1)}, u32[]{:S(2)}, u32[]{:S(2)}) collective-permute-start(bf16[256,1408]{1,0:T(8,128)(2,1)S(1)} %pad_maximum_fusion.1), channel_id=1, source_target_pairs={{0,16},{16,32},{32,48},{48,0},{64,112},{80,64},{96,80},{112,96},{1... | collective-permute-start | bytes 2162696 | tf_op jit(solution)/shard_map/ppermute | solution.py:234
  65.8 6.6 %collective-permute-done.3.refs_5_ = bf16[256,1408]{1,0:T(8,128)(2,1)S(1)} collective-permute-done((bf16[256,1408]{1,0:T(8,128)(2,1)S(1)}, bf16[256,1408]{1,0:T(8,128)(2,1)S(1)}, u32[]{:S(2)}, u32[]{:S(2)}) %collective-permute-start.3) | collective-permute-done | bytes 720928 | tf_op jit(solution)/shard_map/ppermute | solution.py:231
  72.5 7.7 %collective-permute-done.4.refs_6_ = bf16[256,1408]{1,0:T(8,128)(2,1)S(1)} collective-permute-done((bf16[256,1408]{1,0:T(8,128)(2,1)S(1)}, bf16[256,1408]{1,0:T(8,128)(2,1)S(1)}, u32[]{:S(2)}, u32[]{:S(2)}) %collective-permute-start.4) | collective-permute-done | bytes 720928 | tf_op jit(solution)/shard_map/ppermute | solution.py:234
  80.2 0.1 broadcast_select_fusion
  80.3 2.3 %collective-permute-start.7 = (bf16[256,1408]{1,0:T(8,128)(2,1)S(1)}, bf16[256,1408]{1,0:T(8,128)(2,1)S(1)}, u32[]{:S(2)}, u32[]{:S(2)}) collective-permute-start(bf16[256,1408]{1,0:T(8,128)(2,1)S(1)} %broadcast_select_fusion), channel_id=1, source_target_pairs={{0,16},{16,32},{32,48},{48,0},{64,112},{80,64},{96,80},{112,96},{1... | collective-permute-start | bytes 2162696 | tf_op jit(solution)/shard_map/ppermute | solution.py:235
  82.6 3.6 %collective-permute-start.5 = (bf16[256,1408]{1,0:T(8,128)(2,1)S(1)}, bf16[256,1408]{1,0:T(8,128)(2,1)S(1)}, u32[]{:S(2)}, u32[]{:S(2)}) collective-permute-start(bf16[256,1408]{1,0:T(8,128)(2,1)S(1)} %collective-permute-done.3.refs_5_), channel_id=1, source_target_pairs={{0,64},{64,0},{1,65},{65,1},{2,66},{66,2},{3,67},{67,3},{4,68},{68... | collective-permute-start | bytes 2162696 | tf_op jit(solution)/shard_map/ppermute | solution.py:236
  86.2 1.9 %collective-permute-start.6 = (bf16[256,1408]{1,0:T(8,128)(2,1)S(1)}, bf16[256,1408]{1,0:T(8,128)(2,1)}, u32[]{:S(2)}, u32[]{:S(2)}) collective-permute-start(bf16[256,1408]{1,0:T(8,128)(2,1)S(1)} %collective-permute-done.4.refs_6_), channel_id=1, source_target_pairs={{0,64},{64,0},{1,65},{65,1},{2,66},{66,2},{3,67},{67,3},{4,68},{68... | collective-permute-start | bytes 2162696 | tf_op jit(solution)/shard_map/ppermute | solution.py:237
  88.1 6.5 %collective-permute-done.7.refs_9_ = bf16[256,1408]{1,0:T(8,128)(2,1)S(1)} collective-permute-done((bf16[256,1408]{1,0:T(8,128)(2,1)S(1)}, bf16[256,1408]{1,0:T(8,128)(2,1)S(1)}, u32[]{:S(2)}, u32[]{:S(2)}) %collective-permute-start.7) | collective-permute-done | bytes 720928 | tf_op jit(solution)/shard_map/ppermute | solution.py:235
  94.7 1.9 %collective-permute-start.8 = (bf16[256,1408]{1,0:T(8,128)(2,1)S(1)}, bf16[256,1408]{1,0:T(8,128)(2,1)}, u32[]{:S(2)}, u32[]{:S(2)}) collective-permute-start(bf16[256,1408]{1,0:T(8,128)(2,1)S(1)} %collective-permute-done.7.refs_9_), channel_id=1, source_target_pairs={{0,64},{64,0},{1,65},{65,1},{2,66},{66,2},{3,67},{67,3},{4,68},{68... | collective-permute-start | bytes 2162696 | tf_op jit(solution)/shard_map/ppermute | solution.py:238
  96.6 0.6 pad_add_fusion.refs_0_
  97.2 0.0 collective-permute-done.5.refs_7_
  97.2 0.0 collective-permute-done.6.refs_8_
  97.2 1.6 %collective-permute-done.8.refs_10_ = bf16[256,1408]{1,0:T(8,128)(2,1)} collective-permute-done((bf16[256,1408]{1,0:T(8,128)(2,1)S(1)}, bf16[256,1408]{1,0:T(8,128)(2,1)}, u32[]{:S(2)}, u32[]{:S(2)}) %collective-permute-start.8) | collective-permute-done | bytes 720928 | tf_op jit(solution)/shard_map/ppermute | solution.py:238
  98.9 0.0 copy-done.7
  98.9 17.6 %products.1 = bf16[16,4,24,128]{3,2,1,0:T(8,128)(2,1)} custom-call(s32[4]{0:T(128)} %pad_add_fusion.refs_0_, bf16[128,1408]{1,0:T(8,128)(2,1)} %bitcast.16, bf16[128,1408]{1,0:T(8,128)(2,1)} %copy-done.4, bf16[128,1408]{1,0:T(8,128)(2,1)} %copy-done.3, bf16[128,1408]{1,0:T(8,128)(2,1)} %copy-done.5, bf16[256,1408]{1,0:T(8,128)(2,1)} %copy-done.1, ...), custom_call_target="tpu_custom_call" | custom-call | flops 5536481280 | bytes 5767168 | tf_op jit(solution)/shard_map/products/pallas_call | solution.py:151
  116.5 37.3 %all_to_all.22 = bf16[64,24,128]{2,1,0:T(8,128)(2,1)S(1)} all-to-all(bf16[64,24,128]{2,1,0:T(8,128)(2,1)} %bitcast.17), channel_id=1, replica_groups=mesh['x'=4,'core'=2,'y'=4,'z'=16] {'z','y'}, dimensions={0} | all-to-all | bytes 786432 | tf_op jit(solution)/shard_map/all_to_all | solution.py:243
  153.8 4.8 %all_to_all.23 = bf16[2,32,24,128]{3,2,1,0:T(8,128)(2,1)} all-to-all(bf16[2,32,24,128]{3,2,1,0:T(8,128)(2,1)S(1)} %bitcast.11), channel_id=1, replica_groups=mesh['x'=4,'core'=2,'y'=4,'z'=16] {'core'}, dimensions={0} | all-to-all | bytes 786432 | tf_op jit(solution)/shard_map/all_to_all | solution.py:246
  158.6 2.7 %regroup.1 = (bf16[4,32,1408]{2,1,0:T(8,128)(2,1)}, f32[1,88]{1,0:T(1,128)}) custom-call(s32[4]{0:T(128)} %pad_add_fusion.refs_0_, s32[4]{0:T(128)} %bitcast.18, bf16[2,4,2,4,24,128]{5,4,3,2,1,0:T(8,128)(2,1)} %bitcast.10), custom_call_target="tpu_custom_call" | custom-call | tf_op jit(solution)/shard_map/regroup/pallas_call | solution.py:201
  (13 shorter events, 0.0 us)
Async XLA Ops:
  46.0 11.4 %copy-start = (bf16[16,8,1408]{2,1,0:T(8,128)(2,1)}, bf16[16,8,1408]{2,1,0:T(8,128)(2,1)S(1)}, u32[]{:S(2)}) copy-start(bf16[16,8,1408]{2,1,0:T(8,128)(2,1)S(1)} %all_to_all.21) | copy-start | bytes 1081348
  46.0 9.4 %collective-permute-start.1 = (bf16[128,1408]{1,0:T(8,128)(2,1)S(1)}, bf16[128,1408]{1,0:T(8,128)(2,1)S(1)}, u32[]{:S(2)}, u32[]{:S(2)}) collective-permute-start(bf16[128,1408]{1,0:T(8,128)(2,1)S(1)} %bitcast.13), channel_id=1, source_target_pairs={{0,1},{1,0},{2,3},{3,2},{4,5},{5,4},{6,7},{7,6},{8,9},{9,8},{10,11... | collective-permute-start | bytes 1081352 | tf_op jit(solution)/shard_map/ppermute | solution.py:228
  48.4 9.0 %collective-permute-start = (bf16[128,1408]{1,0:T(8,128)(2,1)S(1)}, bf16[128,1408]{1,0:T(8,128)(2,1)S(1)}, u32[]{:S(2)}, u32[]{:S(2)}) collective-permute-start(bf16[128,1408]{1,0:T(8,128)(2,1)S(1)} %bitcast.14), channel_id=1, source_target_pairs={{0,64},{64,0},{1,65},{65,1},{2,66},{66,2},{3,67},{67,3},{4,68},{68... | collective-permute-start | bytes 1081352 | tf_op jit(solution)/shard_map/ppermute | solution.py:229
  55.4 6.2 %copy-start.3 = (bf16[128,1408]{1,0:T(8,128)(2,1)}, bf16[128,1408]{1,0:T(8,128)(2,1)S(1)}, u32[]{:S(2)}) copy-start(bf16[128,1408]{1,0:T(8,128)(2,1)S(1)} %collective-permute-done.1.refs_3_) | copy-start | bytes 1081348
  55.4 6.1 %collective-permute-start.2 = (bf16[128,1408]{1,0:T(8,128)(2,1)S(1)}, bf16[128,1408]{1,0:T(8,128)(2,1)S(1)}, u32[]{:S(2)}, u32[]{:S(2)}) collective-permute-start(bf16[128,1408]{1,0:T(8,128)(2,1)S(1)} %collective-permute-done.1.refs_3_), channel_id=1, source_target_pairs={{0,64},{64,0},{1,65},{65,1},{2,66},{66,2},{3,67},{67,3},{4,68},{68... | collective-permute-start | bytes 1081352 | tf_op jit(solution)/shard_map/ppermute | solution.py:232
  57.3 0.7 copy-start.4
  58.1 14.4 %collective-permute-start.3 = (bf16[256,1408]{1,0:T(8,128)(2,1)S(1)}, bf16[256,1408]{1,0:T(8,128)(2,1)S(1)}, u32[]{:S(2)}, u32[]{:S(2)}) collective-permute-start(bf16[256,1408]{1,0:T(8,128)(2,1)S(1)} %pad_maximum_fusion), channel_id=1, source_target_pairs={{0,16},{16,32},{32,48},{48,0},{64,112},{80,64},{96,80},{112,96},{1... | collective-permute-start | bytes 2162696 | tf_op jit(solution)/shard_map/ppermute | solution.py:231
  61.6 0.8 copy-start.5
  62.3 17.9 %collective-permute-start.4 = (bf16[256,1408]{1,0:T(8,128)(2,1)S(1)}, bf16[256,1408]{1,0:T(8,128)(2,1)S(1)}, u32[]{:S(2)}, u32[]{:S(2)}) collective-permute-start(bf16[256,1408]{1,0:T(8,128)(2,1)S(1)} %pad_maximum_fusion.1), channel_id=1, source_target_pairs={{0,16},{16,32},{32,48},{48,0},{64,112},{80,64},{96,80},{112,96},{1... | collective-permute-start | bytes 2162696 | tf_op jit(solution)/shard_map/ppermute | solution.py:234
  72.5 10.1 %copy-start.1 = (bf16[256,1408]{1,0:T(8,128)(2,1)}, bf16[256,1408]{1,0:T(8,128)(2,1)S(1)}, u32[]{:S(2)}) copy-start(bf16[256,1408]{1,0:T(8,128)(2,1)S(1)} %collective-permute-done.3.refs_5_) | copy-start | bytes 2162692
  80.2 6.0 %copy-start.2 = (bf16[256,1408]{1,0:T(8,128)(2,1)}, bf16[256,1408]{1,0:T(8,128)(2,1)S(1)}, u32[]{:S(2)}) copy-start(bf16[256,1408]{1,0:T(8,128)(2,1)S(1)} %collective-permute-done.4.refs_6_) | copy-start | bytes 2162692
  80.3 14.4 %collective-permute-start.7 = (bf16[256,1408]{1,0:T(8,128)(2,1)S(1)}, bf16[256,1408]{1,0:T(8,128)(2,1)S(1)}, u32[]{:S(2)}, u32[]{:S(2)}) collective-permute-start(bf16[256,1408]{1,0:T(8,128)(2,1)S(1)} %broadcast_select_fusion), channel_id=1, source_target_pairs={{0,16},{16,32},{32,48},{48,0},{64,112},{80,64},{96,80},{112,96},{1... | collective-permute-start | bytes 2162696 | tf_op jit(solution)/shard_map/ppermute | solution.py:235
  82.6 14.7 %collective-permute-start.5 = (bf16[256,1408]{1,0:T(8,128)(2,1)S(1)}, bf16[256,1408]{1,0:T(8,128)(2,1)S(1)}, u32[]{:S(2)}, u32[]{:S(2)}) collective-permute-start(bf16[256,1408]{1,0:T(8,128)(2,1)S(1)} %collective-permute-done.3.refs_5_), channel_id=1, source_target_pairs={{0,64},{64,0},{1,65},{65,1},{2,66},{66,2},{3,67},{67,3},{4,68},{68... | collective-permute-start | bytes 2162696 | tf_op jit(solution)/shard_map/ppermute | solution.py:236
  86.2 11.0 %collective-permute-start.6 = (bf16[256,1408]{1,0:T(8,128)(2,1)S(1)}, bf16[256,1408]{1,0:T(8,128)(2,1)}, u32[]{:S(2)}, u32[]{:S(2)}) collective-permute-start(bf16[256,1408]{1,0:T(8,128)(2,1)S(1)} %collective-permute-done.4.refs_6_), channel_id=1, source_target_pairs={{0,64},{64,0},{1,65},{65,1},{2,66},{66,2},{3,67},{67,3},{4,68},{68... | collective-permute-start | bytes 2162696 | tf_op jit(solution)/shard_map/ppermute | solution.py:237
  94.7 4.2 %copy-start.6 = (bf16[256,1408]{1,0:T(8,128)(2,1)}, bf16[256,1408]{1,0:T(8,128)(2,1)S(1)}, u32[]{:S(2)}) copy-start(bf16[256,1408]{1,0:T(8,128)(2,1)S(1)} %collective-permute-done.7.refs_9_) | copy-start | bytes 2162692
  94.7 4.2 %collective-permute-start.8 = (bf16[256,1408]{1,0:T(8,128)(2,1)S(1)}, bf16[256,1408]{1,0:T(8,128)(2,1)}, u32[]{:S(2)}, u32[]{:S(2)}) collective-permute-start(bf16[256,1408]{1,0:T(8,128)(2,1)S(1)} %collective-permute-done.7.refs_9_), channel_id=1, source_target_pairs={{0,64},{64,0},{1,65},{65,1},{2,66},{66,2},{3,67},{67,3},{4,68},{68... | collective-permute-start | bytes 2162696 | tf_op jit(solution)/shard_map/ppermute | solution.py:238
  97.2 1.7 %copy-start.7 = (bf16[256,1408]{1,0:T(8,128)(2,1)}, bf16[256,1408]{1,0:T(8,128)(2,1)S(1)}, u32[]{:S(2)}) copy-start(bf16[256,1408]{1,0:T(8,128)(2,1)S(1)} %collective-permute-done.5.refs_7_) | copy-start | bytes 2162692

commit v4 on v3

--- a/solution.py
+++ b/solution.py
@@ -15,9 +15,10 @@
 
 F32 = jnp.float32
 BF16 = jnp.bfloat16
-VMEM_LIMIT = 56 * 1024 * 1024
+VMEM_LIMIT = 40 * 1024 * 1024
 LANES = 128
-SECTION_SIZES = (1, 1, 1, 1, 2, 2, 2, 2, 2, 2)
+Y_OFFSETS = (0, 3, 1, 2)
+SECTION_SIZES = (2, 4, 2, 2, 4, 2)
 SLOT_ROWS = 24
 HIGH_LANE = 96
 LOW_LANE = 112
@@ -120,17 +121,11 @@
     def spill(rows, by):
         return jnp.where(spare, pltpu.roll(rows, by, 2), 0.0)
 
-    for offset, flip, mine, other in (
-        (0, 0, (0, 2), (1, 3)),
-        (3 - 2 * core, 0, (4, 6), (5, 7)),
-        (1 + 2 * core, 0, (9, 11), (8, 10)),
-        (2, core, (12, 15), (13, 14)),
-    ):
-        swap = (flip ^ b) == 1
+    for step, offset in enumerate(Y_OFFSETS):
         parts = []
-        for pair in (mine, other):
-            one, two = turned(pair[0]), turned(pair[1])
-            parts.append((jnp.where(swap, two, one), jnp.where(swap, one, two)))
+        for first in (2 * step, 8 + 2 * step):
+            one, two = turned(first), turned(first + 1)
+            parts.append((jnp.where(b == 0, one, two), jnp.where(b == 0, two, one)))
         tiles = [jnp.where(core == 0, parts[0][i], parts[1][i]) for i in range(2)]
         tiles += [jnp.where(core == 0, parts[1][i], parts[0][i]) for i in range(2)]
         last = tiles[3]
@@ -217,7 +212,8 @@
     padded = -(-width // 16) * 16
     core, y, z = lax.axis_index("core"), lax.axis_index("y"), lax.axis_index("z")
     place = jnp.stack([core, y, z % 2, z]).astype(jnp.int32)
-    ring = [(i, (i + 1) % 4) for i in range(4)] + [(4 + i, 4 + (i + 3) % 4) for i in range(4)]
+    up = [(i, (i + 1) % 4) for i in range(4)]
+    down = [((i + 1) % 4, i) for i in range(4)]
     swap = [(0, 1), (1, 0)]
 
     new_momentum, payload = momentum_step(grad, momentum)
@@ -226,18 +222,20 @@
         halves.reshape(16, rows // 4, columns), "z", split_axis=0, concat_axis=0, tiled=True
     ).reshape(-1, columns)
     other = lax.ppermute(mine, "z", [(i, i ^ 1) for i in range(16)])
-    mine_swapped = lax.ppermute(mine, "core", swap)
-    both_mine = jnp.concatenate([mine, mine_swapped], axis=0)
-    near_mine = lax.ppermute(both_mine, ("core", "y"), ring)
-    other_swapped = lax.ppermute(other, "core", swap)
-    both_other = jnp.concatenate([other, other_swapped], axis=0)
-    near_other = lax.ppermute(both_other, ("core", "y"), ring)
-    far = lax.ppermute(jnp.where(core == 0, near_mine, near_other), ("core", "y"), ring)
-    near_mine_swapped = lax.ppermute(near_mine, "core", swap)
-    near_other_swapped = lax.ppermute(near_other, "core", swap)
+    mine_left = lax.ppermute(mine, "y", up)
+    mine_right = lax.ppermute(mine, "y", down)
+    other_left = lax.ppermute(other, "y", up)
+    other_right = lax.ppermute(other, "y", down)
+    mine_far = lax.ppermute(mine_left, "y", up)
+    other_far = lax.ppermute(other_right, "y", down)
+    here = jnp.concatenate([mine, other], axis=0)
+    here, mine_left = lax.optimization_barrier((here, mine_left))
+    here_swapped = lax.ppermute(here, "core", swap)
+    near = jnp.concatenate([mine_left, other_left, mine_right, other_right], axis=0)
+    near_swapped = lax.ppermute(near, "core", swap)
+    far = jnp.concatenate([mine_far, other_far], axis=0)
     far_swapped = lax.ppermute(far, "core", swap)
-    sections = [mine, mine_swapped, other, other_swapped, near_mine, near_other]
-    sections += [near_mine_swapped, near_other_swapped, far, far_swapped]
+    sections = [here, near, far, here_swapped, near_swapped, far_swapped]
 
     slots = products(sections, place, width, padded)
     returned = lax.all_to_all(

time: 163 us -> 154 us (0.945)
  waiting for transfers between devices: 27.7 us -> 13.4 us
  starting transfers between devices: 22.9 us -> 30.9 us
  Pallas kernels: 22.6 us -> 19.8 us
    ppermute x7 -> x8, waiting for transfers between devices: 20.9 us -> 11.2 us  [the longest x1 6.13 us: on_device(): other_far = lax.ppermute(other_right, 'y', down)]
    ppermute x7 -> x8, starting transfers between devices: 18.6 us -> 26.6 us  [the longest x1 5.6 us: on_device(): other_far = lax.ppermute(other_right, 'y', down)]
    ppermute x1, waiting for transfers between devices: 5.11 us -> 0.01 us  [on_device(): other = lax.ppermute(mine, 'z', [(i, i ^ 1) for i in range(16)])]
    all_to_all x1, blocking collectives: 37.3 us -> 39.2 us  [on_device(): lax.all_to_all(slots.reshape(64, SLOT_ROWS, LANES), ('z', 'y'), split_axi...]
  transfers between devices with their start and end apart: 9 -> 10, of which waited for: 5 -> 5; matrix products, arithmetic and copies ran while one was open for 0% -> 0% of each run, Pallas kernels for 0% -> 0%
where the time goes in v4:
time: 154 us; the launch traced here: 153 us
  blocking collectives  85.2 us (55%)
  starting transfers between devices  30.9 us (20%)
  Pallas kernels  19.8 us (13%)
  waiting for transfers between devices  13.4 us (9%)
  local copies, waits for them, and re-layouts  2.29 us (1%)
    all_to_all x1, blocking collectives, on_device(): lax.all_to_all(slots.reshape(64, SLOT_ROWS, LANES), ('z', 'y'), split_axi...  39.2 us
    all_to_all x1, blocking collectives, on_device(): lax.all_to_all(halves.reshape(16, rows // 4, columns), 'z', split_axis=0,...  38 us
    pallas_call x1, Pallas kernels, products(): pl.pallas_call(lambda *refs: products_kernel(width, padded, *refs), in_sp...  16.6 us
    ppermute x1, waiting for transfers between devices, on_device(): other_far = lax.ppermute(other_right, 'y', down)  6.13 us
    ppermute x1, starting transfers between devices, on_device(): other_far = lax.ppermute(other_right, 'y', down)  5.6 us
    ppermute x1, starting transfers between devices, on_device(): other_right = lax.ppermute(other, 'y', down)  4.51 us
    all_to_all x1, blocking collectives, on_device(): lax.all_to_all(returned.reshape(2, -1, SLOT_ROWS, LANES), 'core', split_a...  4.04 us
    all_to_all x1, blocking collectives, on_device(): lax.all_to_all(payload, 'core', split_axis=0, concat_axis=0, tiled=True)  3.99 us
  transfers between devices with their start and end apart: 10, of which 5 were waited for; matrix products, arithmetic and copies ran while one was open for 0% of the time, Pallas kernels for 0%

profile of v4, /device:TPU:6, one launch (start us, length us, event | category | flops | bytes accessed | tf_op | source)
XLA Modules:
  0.0 152.6 jit_solution(3479694639471144894)
XLA Ops:
  0.6 1.1 copy-done
  1.7 1.0 copy-done.1
  2.7 0.9 momentum_step.1
  3.7 4.0 %all_to_all.20 = bf16[2,4,16,1408]{3,2,1,0:T(8,128)(2,1)S(1)} all-to-all(bf16[2,4,16,1408]{3,2,1,0:T(8,128)(2,1)S(1)} %get-tuple-element.10), channel_id=1, replica_groups=mesh['x'=4,'core'=2,'y'=4,'z'=16] {'core'}, dimensions={0} | all-to-all | bytes 720896 | tf_op jit(solution)/shard_map/all_to_all | solution.py:220
  7.7 38.0 %all_to_all.21 = bf16[16,8,1408]{2,1,0:T(8,128)(2,1)S(1)} all-to-all(bf16[16,8,1408]{2,1,0:T(8,128)(2,1)S(1)} %bitcast.14), channel_id=1, replica_groups=mesh['x'=4,'core'=2,'y'=4,'z'=16] {'z'}, dimensions={0} | all-to-all | bytes 720896 | tf_op jit(solution)/shard_map/all_to_all | solution.py:221
  45.7 2.4 %collective-permute-start = (bf16[128,1408]{1,0:T(8,128)(2,1)S(1)}, bf16[128,1408]{1,0:T(8,128)(2,1)S(1)}, u32[]{:S(2)}, u32[]{:S(2)}) collective-permute-start(bf16[128,1408]{1,0:T(8,128)(2,1)S(1)} %bitcast.15), channel_id=1, source_target_pairs={{0,1},{1,0},{2,3},{3,2},{4,5},{5,4},{6,7},{7,6},{8,9},{9,8},{10,11... | collective-permute-start | bytes 1081352 | tf_op jit(solution)/shard_map/ppermute | solution.py:224
  48.1 3.5 %collective-permute-start.1 = (bf16[128,1408]{1,0:T(8,128)(2,1)S(1)}, bf16[128,1408]{1,0:T(8,128)(2,1)S(1)}, u32[]{:S(2)}, u32[]{:S(2)}) collective-permute-start(bf16[128,1408]{1,0:T(8,128)(2,1)S(1)} %bitcast.16), channel_id=1, source_target_pairs={{0,16},{16,32},{32,48},{48,0},{1,17},{17,33},{33,49},{49,1},{2,18}... | collective-permute-start | bytes 1081352 | tf_op jit(solution)/shard_map/ppermute | solution.py:225
  51.5 3.6 %collective-permute-start.3 = (bf16[128,1408]{1,0:T(8,128)(2,1)S(1)}, bf16[128,1408]{1,0:T(8,128)(2,1)S(1)}, u32[]{:S(2)}, u32[]{:S(2)}) collective-permute-start(bf16[128,1408]{1,0:T(8,128)(2,1)S(1)} %bitcast.17), channel_id=1, source_target_pairs={{16,0},{32,16},{48,32},{0,48},{17,1},{33,17},{49,33},{1,49},{18,2}... | collective-permute-start | bytes 1081352 | tf_op jit(solution)/shard_map/ppermute | solution.py:226
  55.1 0.0 collective-permute-done
  55.1 3.4 %collective-permute-start.2 = (bf16[128,1408]{1,0:T(8,128)(2,1)S(1)}, bf16[128,1408]{1,0:T(8,128)(2,1)S(1)}, u32[]{:S(2)}, u32[]{:S(2)}) collective-permute-start(bf16[128,1408]{1,0:T(8,128)(2,1)S(1)} %collective-permute-done), channel_id=1, source_target_pairs={{0,16},{16,32},{32,48},{48,0},{1,17},{17,33},{33,49},{49,1},{2,18}... | collective-permute-start | bytes 1081352 | tf_op jit(solution)/shard_map/ppermute | solution.py:227
  58.6 0.1 pad_maximum_fusion.refs_1_
  58.6 2.2 %collective-permute-done.1 = bf16[128,1408]{1,0:T(8,128)(2,1)S(1)} collective-permute-done((bf16[128,1408]{1,0:T(8,128)(2,1)S(1)}, bf16[128,1408]{1,0:T(8,128)(2,1)S(1)}, u32[]{:S(2)}, u32[]{:S(2)}) %collective-permute-start.1) | collective-permute-done | bytes 360480 | tf_op jit(solution)/shard_map/ppermute | solution.py:225
  60.9 4.5 %collective-permute-start.4 = (bf16[128,1408]{1,0:T(8,128)(2,1)S(1)}, bf16[128,1408]{1,0:T(8,128)(2,1)S(1)}, u32[]{:S(2)}, u32[]{:S(2)}) collective-permute-start(bf16[128,1408]{1,0:T(8,128)(2,1)S(1)} %collective-permute-done), channel_id=1, source_target_pairs={{16,0},{32,16},{48,32},{0,48},{17,1},{33,17},{49,33},{1,49},{18,2}... | collective-permute-start | bytes 1081352 | tf_op jit(solution)/shard_map/ppermute | solution.py:228
  65.4 1.9 %collective-permute-start.5 = (bf16[128,1408]{1,0:T(8,128)(2,1)S(1)}, bf16[128,1408]{1,0:T(8,128)(2,1)S(1)}, u32[]{:S(2)}, u32[]{:S(2)}) collective-permute-start(bf16[128,1408]{1,0:T(8,128)(2,1)S(1)} %collective-permute-done.1), channel_id=1, source_target_pairs={{0,16},{16,32},{32,48},{48,0},{1,17},{17,33},{33,49},{49,1},{2,18}... | collective-permute-start | bytes 1081352 | tf_op jit(solution)/shard_map/ppermute | solution.py:229
  67.4 1.4 collective-permute-done.2
  68.8 0.0 collective-permute-done.3
  68.9 1.4 collective-permute-done.4
  70.4 1.9 %collective-permute-start.8 = (bf16[512,1408]{1,0:T(8,128)(2,1)S(1)}, bf16[512,1408]{1,0:T(8,128)(2,1)}, u32[]{:S(2)}, u32[]{:S(2)}) collective-permute-start(bf16[512,1408]{1,0:T(8,128)(2,1)S(1)} %constant_dynamic-update-slice_fusion.refs_2_), channel_id=1, source_target_pairs={{0,64},{64,0},{1,65},{65,1},{2,66},{66,2},{3,67},{67,3},{4,68},{68... | collective-permute-start | bytes 4325384 | tf_op jit(solution)/shard_map/ppermute | solution.py:235
  72.3 5.6 %collective-permute-start.6 = (bf16[128,1408]{1,0:T(8,128)(2,1)S(1)}, bf16[128,1408]{1,0:T(8,128)(2,1)S(1)}, u32[]{:S(2)}, u32[]{:S(2)}) collective-permute-start(bf16[128,1408]{1,0:T(8,128)(2,1)S(1)} %collective-permute-done.4), channel_id=1, source_target_pairs={{16,0},{32,16},{48,32},{0,48},{17,1},{33,17},{49,33},{1,49},{18,2}... | collective-permute-start | bytes 1081352 | tf_op jit(solution)/shard_map/ppermute | solution.py:230
  77.9 2.1 %collective-permute-start.7 = (bf16[256,1408]{1,0:T(8,128)(2,1)S(1)}, bf16[256,1408]{1,0:T(8,128)(2,1)}, u32[]{:S(2)}, u32[]{:S(2)}) collective-permute-start(bf16[256,1408]{1,0:T(8,128)(2,1)S(1)} %pad_maximum_fusion.refs_1_), channel_id=1, source_target_pairs={{0,64},{64,0},{1,65},{65,1},{2,66},{66,2},{3,67},{67,3},{4,68},{68... | collective-permute-start | bytes 2162696 | tf_op jit(solution)/shard_map/ppermute | solution.py:233
  80.0 0.0 collective-permute-done.5
  80.1 6.1 %collective-permute-done.6 = bf16[128,1408]{1,0:T(8,128)(2,1)S(1)} collective-permute-done((bf16[128,1408]{1,0:T(8,128)(2,1)S(1)}, bf16[128,1408]{1,0:T(8,128)(2,1)S(1)}, u32[]{:S(2)}, u32[]{:S(2)}) %collective-permute-start.6) | collective-permute-done | bytes 360480 | tf_op jit(solution)/shard_map/ppermute | solution.py:230
  86.2 1.9 %collective-permute-start.9 = (bf16[256,1408]{1,0:T(8,128)(2,1)S(1)}, bf16[256,1408]{1,0:T(8,128)(2,1)}, u32[]{:S(2)}, u32[]{:S(2)}) collective-permute-start(bf16[256,1408]{1,0:T(8,128)(2,1)S(1)} %constant_dynamic-update-slice_fusion.4.refs_3_), channel_id=1, source_target_pairs={{0,64},{64,0},{1,65},{65,1},{2,66},{66,2},{3,67},{67,3},{4,68},{68... | collective-permute-start | bytes 2162696 | tf_op jit(solution)/shard_map/ppermute | solution.py:237
  88.2 0.1 pad_add_fusion.refs_0_
  88.3 0.0 collective-permute-done.7.refs_4_
  88.3 2.2 %collective-permute-done.9.refs_6_ = bf16[256,1408]{1,0:T(8,128)(2,1)} collective-permute-done((bf16[256,1408]{1,0:T(8,128)(2,1)S(1)}, bf16[256,1408]{1,0:T(8,128)(2,1)}, u32[]{:S(2)}, u32[]{:S(2)}) %collective-permute-start.9) | collective-permute-done | bytes 720928 | tf_op jit(solution)/shard_map/ppermute | solution.py:237
  90.5 0.0 collective-permute-done.8.refs_5_
  90.5 16.6 %products.1 = bf16[16,4,24,128]{3,2,1,0:T(8,128)(2,1)S(1)} custom-call(s32[4]{0:T(128)S(1)} %pad_add_fusion.refs_0_, bf16[256,1408]{1,0:T(8,128)(2,1)S(1)} %pad_maximum_fusion.refs_1_, bf16[512,1408]{1,0:T(8,128)(2,1)S(1)} %constant_dynamic-update-slice_fusion.refs_2_, bf16[256,1408]{1,0:T(8,128)(2,1)S(1)} %constant_dynamic-update-slice_fusion.4.refs_3_, ...), custom_call_target="tpu_custom_call" | custom-call | flops 5536481280 | bytes 5767168 | tf_op jit(solution)/shard_map/products/pallas_call | solution.py:146
  107.1 0.0 copy-start.2
  107.1 39.2 %all_to_all.22 = bf16[64,24,128]{2,1,0:T(8,128)(2,1)S(1)} all-to-all(bf16[64,24,128]{2,1,0:T(8,128)(2,1)S(1)} %bitcast.11), channel_id=1, replica_groups=mesh['x'=4,'core'=2,'y'=4,'z'=16] {'z','y'}, dimensions={0} | all-to-all | bytes 786432 | tf_op jit(solution)/shard_map/all_to_all | solution.py:241
  146.3 4.0 %all_to_all.23 = bf16[2,32,24,128]{3,2,1,0:T(8,128)(2,1)S(1)} all-to-all(bf16[2,32,24,128]{3,2,1,0:T(8,128)(2,1)S(1)} %bitcast.13), channel_id=1, replica_groups=mesh['x'=4,'core'=2,'y'=4,'z'=16] {'core'}, dimensions={0} | all-to-all | bytes 786432 | tf_op jit(solution)/shard_map/all_to_all | solution.py:244
  150.3 2.2 %regroup.1 = (bf16[4,32,1408]{2,1,0:T(8,128)(2,1)}, f32[1,88]{1,0:T(1,128)}) custom-call(s32[4]{0:T(128)S(1)} %pad_add_fusion.refs_0_, s32[4]{0:T(128)S(1)} %bitcast.12, bf16[2,4,2,4,24,128]{5,4,3,2,1,0:T(8,128)(2,1)S(1)} %bitcast.10), custom_call_target="tpu_custom_call" | custom-call | tf_op jit(solution)/shard_map/regroup/pallas_call | solution.py:196
  (9 shorter events, 0.2 us)
Async XLA Ops:
  0.6 1.1 copy-start
  1.7 1.0 copy-start.1
  45.7 9.5 %collective-permute-start = (bf16[128,1408]{1,0:T(8,128)(2,1)S(1)}, bf16[128,1408]{1,0:T(8,128)(2,1)S(1)}, u32[]{:S(2)}, u32[]{:S(2)}) collective-permute-start(bf16[128,1408]{1,0:T(8,128)(2,1)S(1)} %bitcast.15), channel_id=1, source_target_pairs={{0,1},{1,0},{2,3},{3,2},{4,5},{5,4},{6,7},{7,6},{8,9},{9,8},{10,11... | collective-permute-start | bytes 1081352 | tf_op jit(solution)/shard_map/ppermute | solution.py:224
  48.1 12.8 %collective-permute-start.1 = (bf16[128,1408]{1,0:T(8,128)(2,1)S(1)}, bf16[128,1408]{1,0:T(8,128)(2,1)S(1)}, u32[]{:S(2)}, u32[]{:S(2)}) collective-permute-start(bf16[128,1408]{1,0:T(8,128)(2,1)S(1)} %bitcast.16), channel_id=1, source_target_pairs={{0,16},{16,32},{32,48},{48,0},{1,17},{17,33},{33,49},{49,1},{2,18}... | collective-permute-start | bytes 1081352 | tf_op jit(solution)/shard_map/ppermute | solution.py:225
  51.5 17.3 %collective-permute-start.3 = (bf16[128,1408]{1,0:T(8,128)(2,1)S(1)}, bf16[128,1408]{1,0:T(8,128)(2,1)S(1)}, u32[]{:S(2)}, u32[]{:S(2)}) collective-permute-start(bf16[128,1408]{1,0:T(8,128)(2,1)S(1)} %bitcast.17), channel_id=1, source_target_pairs={{16,0},{32,16},{48,32},{0,48},{17,1},{33,17},{49,33},{1,49},{18,2}... | collective-permute-start | bytes 1081352 | tf_op jit(solution)/shard_map/ppermute | solution.py:226
  55.1 13.7 %collective-permute-start.2 = (bf16[128,1408]{1,0:T(8,128)(2,1)S(1)}, bf16[128,1408]{1,0:T(8,128)(2,1)S(1)}, u32[]{:S(2)}, u32[]{:S(2)}) collective-permute-start(bf16[128,1408]{1,0:T(8,128)(2,1)S(1)} %collective-permute-done), channel_id=1, source_target_pairs={{0,16},{16,32},{32,48},{48,0},{1,17},{17,33},{33,49},{49,1},{2,18}... | collective-permute-start | bytes 1081352 | tf_op jit(solution)/shard_map/ppermute | solution.py:227
  60.9 9.4 %collective-permute-start.4 = (bf16[128,1408]{1,0:T(8,128)(2,1)S(1)}, bf16[128,1408]{1,0:T(8,128)(2,1)S(1)}, u32[]{:S(2)}, u32[]{:S(2)}) collective-permute-start(bf16[128,1408]{1,0:T(8,128)(2,1)S(1)} %collective-permute-done), channel_id=1, source_target_pairs={{16,0},{32,16},{48,32},{0,48},{17,1},{33,17},{49,33},{1,49},{18,2}... | collective-permute-start | bytes 1081352 | tf_op jit(solution)/shard_map/ppermute | solution.py:228
  65.4 14.6 %collective-permute-start.5 = (bf16[128,1408]{1,0:T(8,128)(2,1)S(1)}, bf16[128,1408]{1,0:T(8,128)(2,1)S(1)}, u32[]{:S(2)}, u32[]{:S(2)}) collective-permute-start(bf16[128,1408]{1,0:T(8,128)(2,1)S(1)} %collective-permute-done.1), channel_id=1, source_target_pairs={{0,16},{16,32},{32,48},{48,0},{1,17},{17,33},{33,49},{49,1},{2,18}... | collective-permute-start | bytes 1081352 | tf_op jit(solution)/shard_map/ppermute | solution.py:229
  70.4 20.1 %collective-permute-start.8 = (bf16[512,1408]{1,0:T(8,128)(2,1)S(1)}, bf16[512,1408]{1,0:T(8,128)(2,1)}, u32[]{:S(2)}, u32[]{:S(2)}) collective-permute-start(bf16[512,1408]{1,0:T(8,128)(2,1)S(1)} %constant_dynamic-update-slice_fusion.refs_2_), channel_id=1, source_target_pairs={{0,64},{64,0},{1,65},{65,1},{2,66},{66,2},{3,67},{67,3},{4,68},{68... | collective-permute-start | bytes 4325384 | tf_op jit(solution)/shard_map/ppermute | solution.py:235
  72.3 13.9 %collective-permute-start.6 = (bf16[128,1408]{1,0:T(8,128)(2,1)S(1)}, bf16[128,1408]{1,0:T(8,128)(2,1)S(1)}, u32[]{:S(2)}, u32[]{:S(2)}) collective-permute-start(bf16[128,1408]{1,0:T(8,128)(2,1)S(1)} %collective-permute-done.4), channel_id=1, source_target_pairs={{16,0},{32,16},{48,32},{0,48},{17,1},{33,17},{49,33},{1,49},{18,2}... | collective-permute-start | bytes 1081352 | tf_op jit(solution)/shard_map/ppermute | solution.py:230
  77.9 10.4 %collective-permute-start.7 = (bf16[256,1408]{1,0:T(8,128)(2,1)S(1)}, bf16[256,1408]{1,0:T(8,128)(2,1)}, u32[]{:S(2)}, u32[]{:S(2)}) collective-permute-start(bf16[256,1408]{1,0:T(8,128)(2,1)S(1)} %pad_maximum_fusion.refs_1_), channel_id=1, source_target_pairs={{0,64},{64,0},{1,65},{65,1},{2,66},{66,2},{3,67},{67,3},{4,68},{68... | collective-permute-start | bytes 2162696 | tf_op jit(solution)/shard_map/ppermute | solution.py:233
  86.2 4.2 %collective-permute-start.9 = (bf16[256,1408]{1,0:T(8,128)(2,1)S(1)}, bf16[256,1408]{1,0:T(8,128)(2,1)}, u32[]{:S(2)}, u32[]{:S(2)}) collective-permute-start(bf16[256,1408]{1,0:T(8,128)(2,1)S(1)} %constant_dynamic-update-slice_fusion.4.refs_3_), channel_id=1, source_target_pairs={{0,64},{64,0},{1,65},{65,1},{2,66},{66,2},{3,67},{67,3},{4,68},{68... | collective-permute-start | bytes 2162696 | tf_op jit(solution)/shard_map/ppermute | solution.py:237
  107.1 43.2 %copy-start.2 = (s32[1,4]{1,0:T(1,128)S(1)}, s32[1,4]{1,0:T(1,128)}, u32[]{:S(2)}) copy-start(s32[1,4]{1,0:T(1,128)} %param.5) | copy-start | bytes 52

commit v5 on v4

--- a/solution.py
+++ b/solution.py
@@ -18,7 +18,7 @@
 VMEM_LIMIT = 40 * 1024 * 1024
 LANES = 128
 Y_OFFSETS = (0, 3, 1, 2)
-SECTION_SIZES = (2, 4, 2, 2, 4, 2)
+SECTION_SIZES = (4, 4, 4, 4)
 SLOT_ROWS = 24
 HIGH_LANE = 96
 LOW_LANE = 112
@@ -44,7 +44,7 @@
             jax.ShapeDtypeStruct(grad.shape, F32),
             jax.ShapeDtypeStruct((2, matrices, rows // 2, columns), BF16),
         ],
-        compiler_params=pltpu.CompilerParams(vmem_limit_bytes=VMEM_LIMIT),
+        compiler_params=pltpu.CompilerParams(vmem_limit_bytes=60 * 1024 * 1024),
         name="momentum_step",
     )(grad, momentum)
 
@@ -123,8 +123,8 @@
 
     for step, offset in enumerate(Y_OFFSETS):
         parts = []
-        for first in (2 * step, 8 + 2 * step):
-            one, two = turned(first), turned(first + 1)
+        for first in (step, 8 + step):
+            one, two = turned(first), turned(first + 4)
             parts.append((jnp.where(b == 0, one, two), jnp.where(b == 0, two, one)))
         tiles = [jnp.where(core == 0, parts[0][i], parts[1][i]) for i in range(2)]
         tiles += [jnp.where(core == 0, parts[1][i], parts[0][i]) for i in range(2)]
@@ -228,14 +228,11 @@
     other_right = lax.ppermute(other, "y", down)
     mine_far = lax.ppermute(mine_left, "y", up)
     other_far = lax.ppermute(other_right, "y", down)
-    here = jnp.concatenate([mine, other], axis=0)
-    here, mine_left = lax.optimization_barrier((here, mine_left))
-    here_swapped = lax.ppermute(here, "core", swap)
-    near = jnp.concatenate([mine_left, other_left, mine_right, other_right], axis=0)
-    near_swapped = lax.ppermute(near, "core", swap)
-    far = jnp.concatenate([mine_far, other_far], axis=0)
-    far_swapped = lax.ppermute(far, "core", swap)
-    sections = [here, near, far, here_swapped, near_swapped, far_swapped]
+    mine = jnp.concatenate([mine, mine_left, mine_right, mine_far], axis=0)
+    mine_swapped = lax.ppermute(mine, "core", swap)
+    other = jnp.concatenate([other, other_left, other_right, other_far], axis=0)
+    other_swapped = lax.ppermute(other, "core", swap)
+    sections = [mine, other, mine_swapped, other_swapped]
 
     slots = products(sections, place, width, padded)
     returned = lax.all_to_all(

time: 154 us -> 153 us (level)
  starting transfers between devices: 30.9 us -> 26.1 us
  waiting for transfers between devices: 13.4 us -> 16.1 us
  blocking collectives: 85.2 us -> 87.4 us
  local copies, waits for them, and re-layouts: 2.29 us -> 0.14 us
    ppermute x1, waiting for transfers between devices: 0.01 us -> 3.06 us  [on_device(): mine_far = lax.ppermute(mine_left, 'y', up)]
    ppermute x1, waiting for transfers between devices: 6.13 us -> 8.54 us  [on_device(): other_far = lax.ppermute(other_right, 'y', down)]
    ppermute x3 -> x2, starting transfers between devices: 5.97 us -> 3.84 us  [the longest x1 1.92 us: on_device(): mine_swapped = lax.ppermute(mine, 'core', swap)]
    unnamed x10 -> x5, local copies, waits for them, and re-layouts: 2.22 us -> 0.1 us
    ppermute x1, starting transfers between devices: 5.6 us -> 3.9 us  [on_device(): other_far = lax.ppermute(other_right, 'y', down)]
    ppermute x3 -> x2, waiting for transfers between devices: 2.2 us -> 3.23 us  [the longest x1 3.23 us: on_device(): other_swapped = lax.ppermute(other, 'core', swap)]
  transfers between devices with their start and end apart: 10 -> 9, of which waited for: 5 -> 5; matrix products, arithmetic and copies ran while one was open for 0% -> 0% of each run, Pallas kernels for 0% -> 0%
where the time goes in v5:
time: 153 us; the launch traced here: 152 us
  blocking collectives  87.4 us (57%)
  starting transfers between devices  26.1 us (17%)
  Pallas kernels  20.9 us (14%)
  waiting for transfers between devices  16.1 us (11%)
    all_to_all x1, blocking collectives, on_device(): lax.all_to_all(slots.reshape(64, SLOT_ROWS, LANES), ('z', 'y'), split_axi...  40.3 us
    all_to_all x1, blocking collectives, on_device(): lax.all_to_all(halves.reshape(16, rows // 4, columns), 'z', split_axis=0,...  38 us
    pallas_call x1, Pallas kernels, products(): pl.pallas_call(lambda *refs: products_kernel(width, padded, *refs), in_sp...  16.4 us
    ppermute x1, waiting for transfers between devices, on_device(): other_far = lax.ppermute(other_right, 'y', down)  8.54 us
    all_to_all x1, blocking collectives, on_device(): lax.all_to_all(payload, 'core', split_axis=0, concat_axis=0, tiled=True)  5.07 us
    ppermute x1, starting transfers between devices, on_device(): other_right = lax.ppermute(other, 'y', down)  4.78 us
    all_to_all x1, blocking collectives, on_device(): lax.all_to_all(returned.reshape(2, -1, SLOT_ROWS, LANES), 'core', split_a...  4.04 us
    ppermute x1, starting transfers between devices, on_device(): other_far = lax.ppermute(other_right, 'y', down)  3.9 us
  transfers between devices with their start and end apart: 9, of which 5 were waited for; matrix products, arithmetic and copies ran while one was open for 0% of the time, Pallas kernels for 0%

profile of v5, /device:TPU:6, one launch (start us, length us, event | category | flops | bytes accessed | tf_op | source)
XLA Modules:
  0.0 151.6 jit_solution(832369389695780778)
XLA Ops:
  0.6 2.3 %momentum_step.1 = (f32[4,32,1408]{2,1,0:T(8,128)}, bf16[2,4,16,1408]{3,2,1,0:T(8,128)(2,1)}) custom-call(bf16[4,32,1408]{2,1,0:T(8,128)(2,1)} %grad_ref.1, f32[4,32,1408]{2,1,0:T(8,128)} %momentum_ref.1), custom_call_target="tpu_custom_call" | custom-call | tf_op jit(solution)/shard_map/momentum_step/pallas_call | solution.py:39
  2.9 5.1 %all_to_all.20 = bf16[2,4,16,1408]{3,2,1,0:T(8,128)(2,1)S(1)} all-to-all(bf16[2,4,16,1408]{3,2,1,0:T(8,128)(2,1)} %get-tuple-element.8), channel_id=1, replica_groups=mesh['x'=4,'core'=2,'y'=4,'z'=16] {'core'}, dimensions={0} | all-to-all | bytes 720896 | tf_op jit(solution)/shard_map/all_to_all | solution.py:220
  8.0 38.0 %all_to_all.21 = bf16[16,8,1408]{2,1,0:T(8,128)(2,1)S(1)} all-to-all(bf16[16,8,1408]{2,1,0:T(8,128)(2,1)S(1)} %bitcast.14), channel_id=1, replica_groups=mesh['x'=4,'core'=2,'y'=4,'z'=16] {'z'}, dimensions={0} | all-to-all | bytes 720896 | tf_op jit(solution)/shard_map/all_to_all | solution.py:221
  46.0 3.5 %collective-permute-start = (bf16[128,1408]{1,0:T(8,128)(2,1)S(1)}, bf16[128,1408]{1,0:T(8,128)(2,1)S(1)}, u32[]{:S(2)}, u32[]{:S(2)}) collective-permute-start(bf16[128,1408]{1,0:T(8,128)(2,1)S(1)} %bitcast.15), channel_id=1, source_target_pairs={{0,16},{16,32},{32,48},{48,0},{1,17},{17,33},{33,49},{49,1},{2,18}... | collective-permute-start | bytes 1081352 | tf_op jit(solution)/shard_map/ppermute | solution.py:225
  49.5 2.4 %collective-permute-start.3 = (bf16[128,1408]{1,0:T(8,128)(2,1)S(1)}, bf16[128,1408]{1,0:T(8,128)(2,1)S(1)}, u32[]{:S(2)}, u32[]{:S(2)}) collective-permute-start(bf16[128,1408]{1,0:T(8,128)(2,1)S(1)} %bitcast.16), channel_id=1, source_target_pairs={{0,1},{1,0},{2,3},{3,2},{4,5},{5,4},{6,7},{7,6},{8,9},{9,8},{10,11... | collective-permute-start | bytes 1081352 | tf_op jit(solution)/shard_map/ppermute | solution.py:224
  51.9 3.6 %collective-permute-start.1 = (bf16[128,1408]{1,0:T(8,128)(2,1)S(1)}, bf16[128,1408]{1,0:T(8,128)(2,1)S(1)}, u32[]{:S(2)}, u32[]{:S(2)}) collective-permute-start(bf16[128,1408]{1,0:T(8,128)(2,1)S(1)} %bitcast.17), channel_id=1, source_target_pairs={{16,0},{32,16},{48,32},{0,48},{17,1},{33,17},{49,33},{1,49},{18,2}... | collective-permute-start | bytes 1081352 | tf_op jit(solution)/shard_map/ppermute | solution.py:226
  55.4 1.1 collective-permute-done
  56.5 2.3 %collective-permute-start.2 = (bf16[128,1408]{1,0:T(8,128)(2,1)S(1)}, bf16[128,1408]{1,0:T(8,128)(2,1)S(1)}, u32[]{:S(2)}, u32[]{:S(2)}) collective-permute-start(bf16[128,1408]{1,0:T(8,128)(2,1)S(1)} %collective-permute-done), channel_id=1, source_target_pairs={{0,16},{16,32},{32,48},{48,0},{1,17},{17,33},{33,49},{49,1},{2,18}... | collective-permute-start | bytes 1081352 | tf_op jit(solution)/shard_map/ppermute | solution.py:229
  58.8 0.0 collective-permute-done.3
  58.8 4.8 %collective-permute-start.5 = (bf16[128,1408]{1,0:T(8,128)(2,1)S(1)}, bf16[128,1408]{1,0:T(8,128)(2,1)S(1)}, u32[]{:S(2)}, u32[]{:S(2)}) collective-permute-start(bf16[128,1408]{1,0:T(8,128)(2,1)S(1)} %collective-permute-done.3), channel_id=1, source_target_pairs={{16,0},{32,16},{48,32},{0,48},{17,1},{33,17},{49,33},{1,49},{18,2}... | collective-permute-start | bytes 1081352 | tf_op jit(solution)/shard_map/ppermute | solution.py:228
  63.6 1.9 %collective-permute-start.4 = (bf16[128,1408]{1,0:T(8,128)(2,1)S(1)}, bf16[128,1408]{1,0:T(8,128)(2,1)S(1)}, u32[]{:S(2)}, u32[]{:S(2)}) collective-permute-start(bf16[128,1408]{1,0:T(8,128)(2,1)S(1)} %collective-permute-done.3), channel_id=1, source_target_pairs={{0,16},{16,32},{32,48},{48,0},{1,17},{17,33},{33,49},{49,1},{2,18}... | collective-permute-start | bytes 1081352 | tf_op jit(solution)/shard_map/ppermute | solution.py:227
  65.5 0.0 collective-permute-done.1
  65.6 3.1 %collective-permute-done.2 = bf16[128,1408]{1,0:T(8,128)(2,1)S(1)} collective-permute-done((bf16[128,1408]{1,0:T(8,128)(2,1)S(1)}, bf16[128,1408]{1,0:T(8,128)(2,1)S(1)}, u32[]{:S(2)}, u32[]{:S(2)}) %collective-permute-start.2) | collective-permute-done | bytes 360480 | tf_op jit(solution)/shard_map/ppermute | solution.py:229
  68.6 0.1 pad_maximum_fusion.refs_1_
  68.7 1.9 %collective-permute-start.7 = (bf16[512,1408]{1,0:T(8,128)(2,1)S(1)}, bf16[512,1408]{1,0:T(8,128)(2,1)}, u32[]{:S(2)}, u32[]{:S(2)}) collective-permute-start(bf16[512,1408]{1,0:T(8,128)(2,1)S(1)} %pad_maximum_fusion.refs_1_), channel_id=1, source_target_pairs={{0,64},{64,0},{1,65},{65,1},{2,66},{66,2},{3,67},{67,3},{4,68},{68... | collective-permute-start | bytes 4325384 | tf_op jit(solution)/shard_map/ppermute | solution.py:232
  70.7 0.0 collective-permute-done.5
  70.7 3.9 %collective-permute-start.6 = (bf16[128,1408]{1,0:T(8,128)(2,1)S(1)}, bf16[128,1408]{1,0:T(8,128)(2,1)S(1)}, u32[]{:S(2)}, u32[]{:S(2)}) collective-permute-start(bf16[128,1408]{1,0:T(8,128)(2,1)S(1)} %collective-permute-done.5), channel_id=1, source_target_pairs={{16,0},{32,16},{48,32},{0,48},{17,1},{33,17},{49,33},{1,49},{18,2}... | collective-permute-start | bytes 1081352 | tf_op jit(solution)/shard_map/ppermute | solution.py:230
  74.6 0.2 collective-permute-done.4
  74.8 8.5 %collective-permute-done.6 = bf16[128,1408]{1,0:T(8,128)(2,1)S(1)} collective-permute-done((bf16[128,1408]{1,0:T(8,128)(2,1)S(1)}, bf16[128,1408]{1,0:T(8,128)(2,1)S(1)}, u32[]{:S(2)}, u32[]{:S(2)}) %collective-permute-start.6) | collective-permute-done | bytes 360480 | tf_op jit(solution)/shard_map/ppermute | solution.py:230
  83.4 1.9 %collective-permute-start.8 = (bf16[512,1408]{1,0:T(8,128)(2,1)S(1)}, bf16[512,1408]{1,0:T(8,128)(2,1)}, u32[]{:S(2)}, u32[]{:S(2)}) collective-permute-start(bf16[512,1408]{1,0:T(8,128)(2,1)S(1)} %constant_dynamic-update-slice_fusion.refs_2_), channel_id=1, source_target_pairs={{0,64},{64,0},{1,65},{65,1},{2,66},{66,2},{3,67},{67,3},{4,68},{68... | collective-permute-start | bytes 4325384 | tf_op jit(solution)/shard_map/ppermute | solution.py:234
  85.3 0.1 pad_add_fusion.refs_0_
  85.4 0.0 collective-permute-done.7.refs_3_
  85.4 3.2 %collective-permute-done.8.refs_4_ = bf16[512,1408]{1,0:T(8,128)(2,1)} collective-permute-done((bf16[512,1408]{1,0:T(8,128)(2,1)S(1)}, bf16[512,1408]{1,0:T(8,128)(2,1)}, u32[]{:S(2)}, u32[]{:S(2)}) %collective-permute-start.8) | collective-permute-done | bytes 1441824 | tf_op jit(solution)/shard_map/ppermute | solution.py:234
  88.7 16.4 %products.1 = bf16[16,4,24,128]{3,2,1,0:T(8,128)(2,1)S(1)} custom-call(s32[4]{0:T(128)S(1)} %pad_add_fusion.refs_0_, bf16[512,1408]{1,0:T(8,128)(2,1)S(1)} %pad_maximum_fusion.refs_1_, bf16[512,1408]{1,0:T(8,128)(2,1)S(1)} %constant_dynamic-update-slice_fusion.refs_2_, bf16[512,1408]{1,0:T(8,128)(2,1)} %collective-permute-done.7.refs_3_, ...), custom_call_target="tpu_custom_call" | custom-call | flops 5536481280 | bytes 5767168 | tf_op jit(solution)/shard_map/products/pallas_call | solution.py:146
  105.0 0.0 copy-start
  105.0 40.3 %all_to_all.22 = bf16[64,24,128]{2,1,0:T(8,128)(2,1)S(1)} all-to-all(bf16[64,24,128]{2,1,0:T(8,128)(2,1)S(1)} %bitcast.11), channel_id=1, replica_groups=mesh['x'=4,'core'=2,'y'=4,'z'=16] {'z','y'}, dimensions={0} | all-to-all | bytes 786432 | tf_op jit(solution)/shard_map/all_to_all | solution.py:238
  145.3 4.0 %all_to_all.23 = bf16[2,32,24,128]{3,2,1,0:T(8,128)(2,1)S(1)} all-to-all(bf16[2,32,24,128]{3,2,1,0:T(8,128)(2,1)S(1)} %bitcast.13), channel_id=1, replica_groups=mesh['x'=4,'core'=2,'y'=4,'z'=16] {'core'}, dimensions={0} | all-to-all | bytes 786432 | tf_op jit(solution)/shard_map/all_to_all | solution.py:241
  149.4 0.0 copy-done
  149.4 2.2 %regroup.1 = (bf16[4,32,1408]{2,1,0:T(8,128)(2,1)}, f32[1,88]{1,0:T(1,128)}) custom-call(s32[4]{0:T(128)S(1)} %pad_add_fusion.refs_0_, s32[4]{0:T(128)S(1)} %bitcast.12, bf16[2,4,2,4,24,128]{5,4,3,2,1,0:T(8,128)(2,1)S(1)} %bitcast.10), custom_call_target="tpu_custom_call" | custom-call | tf_op jit(solution)/shard_map/regroup/pallas_call | solution.py:196
  (4 shorter events, 0.1 us)
Async XLA Ops:
  46.0 10.5 %collective-permute-start = (bf16[128,1408]{1,0:T(8,128)(2,1)S(1)}, bf16[128,1408]{1,0:T(8,128)(2,1)S(1)}, u32[]{:S(2)}, u32[]{:S(2)}) collective-permute-start(bf16[128,1408]{1,0:T(8,128)(2,1)S(1)} %bitcast.15), channel_id=1, source_target_pairs={{0,16},{16,32},{32,48},{48,0},{1,17},{17,33},{33,49},{49,1},{2,18}... | collective-permute-start | bytes 1081352 | tf_op jit(solution)/shard_map/ppermute | solution.py:225
  49.5 9.3 %collective-permute-start.3 = (bf16[128,1408]{1,0:T(8,128)(2,1)S(1)}, bf16[128,1408]{1,0:T(8,128)(2,1)S(1)}, u32[]{:S(2)}, u32[]{:S(2)}) collective-permute-start(bf16[128,1408]{1,0:T(8,128)(2,1)S(1)} %bitcast.16), channel_id=1, source_target_pairs={{0,1},{1,0},{2,3},{3,2},{4,5},{5,4},{6,7},{7,6},{8,9},{9,8},{10,11... | collective-permute-start | bytes 1081352 | tf_op jit(solution)/shard_map/ppermute | solution.py:224
  51.9 13.7 %collective-permute-start.1 = (bf16[128,1408]{1,0:T(8,128)(2,1)S(1)}, bf16[128,1408]{1,0:T(8,128)(2,1)S(1)}, u32[]{:S(2)}, u32[]{:S(2)}) collective-permute-start(bf16[128,1408]{1,0:T(8,128)(2,1)S(1)} %bitcast.17), channel_id=1, source_target_pairs={{16,0},{32,16},{48,32},{0,48},{17,1},{33,17},{49,33},{1,49},{18,2}... | collective-permute-start | bytes 1081352 | tf_op jit(solution)/shard_map/ppermute | solution.py:226
  56.5 12.1 %collective-permute-start.2 = (bf16[128,1408]{1,0:T(8,128)(2,1)S(1)}, bf16[128,1408]{1,0:T(8,128)(2,1)S(1)}, u32[]{:S(2)}, u32[]{:S(2)}) collective-permute-start(bf16[128,1408]{1,0:T(8,128)(2,1)S(1)} %collective-permute-done), channel_id=1, source_target_pairs={{0,16},{16,32},{32,48},{48,0},{1,17},{17,33},{33,49},{49,1},{2,18}... | collective-permute-start | bytes 1081352 | tf_op jit(solution)/shard_map/ppermute | solution.py:229
  58.8 11.9 %collective-permute-start.5 = (bf16[128,1408]{1,0:T(8,128)(2,1)S(1)}, bf16[128,1408]{1,0:T(8,128)(2,1)S(1)}, u32[]{:S(2)}, u32[]{:S(2)}) collective-permute-start(bf16[128,1408]{1,0:T(8,128)(2,1)S(1)} %collective-permute-done.3), channel_id=1, source_target_pairs={{16,0},{32,16},{48,32},{0,48},{17,1},{33,17},{49,33},{1,49},{18,2}... | collective-permute-start | bytes 1081352 | tf_op jit(solution)/shard_map/ppermute | solution.py:228
  63.6 11.2 %collective-permute-start.4 = (bf16[128,1408]{1,0:T(8,128)(2,1)S(1)}, bf16[128,1408]{1,0:T(8,128)(2,1)S(1)}, u32[]{:S(2)}, u32[]{:S(2)}) collective-permute-start(bf16[128,1408]{1,0:T(8,128)(2,1)S(1)} %collective-permute-done.3), channel_id=1, source_target_pairs={{0,16},{16,32},{32,48},{48,0},{1,17},{17,33},{33,49},{49,1},{2,18}... | collective-permute-start | bytes 1081352 | tf_op jit(solution)/shard_map/ppermute | solution.py:227
  68.7 16.7 %collective-permute-start.7 = (bf16[512,1408]{1,0:T(8,128)(2,1)S(1)}, bf16[512,1408]{1,0:T(8,128)(2,1)}, u32[]{:S(2)}, u32[]{:S(2)}) collective-permute-start(bf16[512,1408]{1,0:T(8,128)(2,1)S(1)} %pad_maximum_fusion.refs_1_), channel_id=1, source_target_pairs={{0,64},{64,0},{1,65},{65,1},{2,66},{66,2},{3,67},{67,3},{4,68},{68... | collective-permute-start | bytes 4325384 | tf_op jit(solution)/shard_map/ppermute | solution.py:232
  70.7 12.7 %collective-permute-start.6 = (bf16[128,1408]{1,0:T(8,128)(2,1)S(1)}, bf16[128,1408]{1,0:T(8,128)(2,1)S(1)}, u32[]{:S(2)}, u32[]{:S(2)}) collective-permute-start(bf16[128,1408]{1,0:T(8,128)(2,1)S(1)} %collective-permute-done.5), channel_id=1, source_target_pairs={{16,0},{32,16},{48,32},{0,48},{17,1},{33,17},{49,33},{1,49},{18,2}... | collective-permute-start | bytes 1081352 | tf_op jit(solution)/shard_map/ppermute | solution.py:230
  83.4 5.2 %collective-permute-start.8 = (bf16[512,1408]{1,0:T(8,128)(2,1)S(1)}, bf16[512,1408]{1,0:T(8,128)(2,1)}, u32[]{:S(2)}, u32[]{:S(2)}) collective-permute-start(bf16[512,1408]{1,0:T(8,128)(2,1)S(1)} %constant_dynamic-update-slice_fusion.refs_2_), channel_id=1, source_target_pairs={{0,64},{64,0},{1,65},{65,1},{2,66},{66,2},{3,67},{67,3},{4,68},{68... | collective-permute-start | bytes 4325384 | tf_op jit(solution)/shard_map/ppermute | solution.py:234
  105.0 44.4 %copy-start = (s32[1,4]{1,0:T(1,128)S(1)}, s32[1,4]{1,0:T(1,128)}, u32[]{:S(2)}) copy-start(s32[1,4]{1,0:T(1,128)} %param.5) | copy-start | bytes 52

commit v6 on v5

--- a/solution.py
+++ b/solution.py
@@ -15,42 +15,75 @@
 
 F32 = jnp.float32
 BF16 = jnp.bfloat16
-VMEM_LIMIT = 40 * 1024 * 1024
+VMEM_LIMIT = 36 * 1024 * 1024
 LANES = 128
 Y_OFFSETS = (0, 3, 1, 2)
-SECTION_SIZES = (4, 4, 4, 4)
+STRIP = 256
 SLOT_ROWS = 24
 HIGH_LANE = 96
 LOW_LANE = 112
 
 
-def momentum_kernel(grad_ref, momentum_ref, new_ref, payload_ref):
+def momentum_kernel(place_ref, grad_ref, momentum_ref, new_ref, keep_ref, send_ref):
     new = DECAY * momentum_ref[...] + grad_ref[...].astype(F32)
     new_ref[...] = new
-    rounded = new.astype(BF16)
-    half = payload_ref.shape[2]
-    payload_ref[0] = rounded[:, :half]
-    payload_ref[1] = rounded[:, half:]
-
-
-def momentum_step(grad, momentum):
+    half = keep_ref.shape[1]
+    first = place_ref[0] == 0
+    keep_ref[...] = jnp.where(first, new[:, :half], new[:, half:]).astype(BF16)
+    send_ref[...] = jnp.where(first, new[:, half:], new[:, :half]).astype(BF16)
+
+
+def momentum_step(place, grad, momentum):
     matrices, rows, columns = grad.shape
     vmem = pl.BlockSpec(memory_space=pltpu.VMEM)
+    half = jax.ShapeDtypeStruct((matrices, rows // 2, columns), BF16)
     return pl.pallas_call(
         momentum_kernel,
-        in_specs=[vmem, vmem],
-        out_specs=[vmem, vmem],
-        out_shape=[
-            jax.ShapeDtypeStruct(grad.shape, F32),
-            jax.ShapeDtypeStruct((2, matrices, rows // 2, columns), BF16),
-        ],
+        in_specs=[pl.BlockSpec(memory_space=pltpu.SMEM), vmem, vmem],
+        out_specs=[vmem, vmem, vmem],
+        out_shape=[jax.ShapeDtypeStruct(grad.shape, F32), half, half],
         compiler_params=pltpu.CompilerParams(vmem_limit_bytes=60 * 1024 * 1024),
         name="momentum_step",
-    )(grad, momentum)
-
-
-def times(block, x_ref):
-    return jnp.dot(block, x_ref[...], preferred_element_type=F32)
+    )(place, grad, momentum)
+
+
+def strips(columns):
+    return [(at, min(STRIP, columns - at)) for at in range(0, columns, STRIP)]
+
+
+def gram_strip(x_ref, at, size):
+    return lax.dot_general(
+        x_ref[:, at : at + size],
+        x_ref[:, at:],
+        (((0,), (0,)), ((), ())),
+        preferred_element_type=F32,
+    )
+
+
+def gram_part_kernel(one_ref, two_ref, part_ref):
+    for at, size in strips(one_ref.shape[1]):
+        total = gram_strip(one_ref, at, size) + gram_strip(two_ref, at, size)
+        part_ref[at : at + size, at:] = total
+
+
+def gram_part(one, two):
+    rows, columns = one.shape
+    vmem = pl.BlockSpec(memory_space=pltpu.VMEM)
+    return pl.pallas_call(
+        gram_part_kernel,
+        in_specs=[vmem, vmem],
+        out_specs=vmem,
+        out_shape=jax.ShapeDtypeStruct((columns, columns), F32),
+        compiler_params=pltpu.CompilerParams(vmem_limit_bytes=24 * 1024 * 1024),
+        cost_estimate=pl.CostEstimate(
+            flops=2 * rows * columns * columns, bytes_accessed=0, transcendentals=0
+        ),
+        name="gram_part",
+    )(one, two)
+
+
+def times(block, matrix_ref):
+    return jnp.dot(block, matrix_ref[...], preferred_element_type=F32)
 
 
 def times_transposed(block, x_ref):
@@ -59,45 +92,48 @@
     )
 
 
-def products_kernel(width, padded, place_ref, *refs):
-    count = len(SECTION_SIZES)
-    sections = refs[:count]
-    slots_ref, x_ref, sems = refs[count:]
+def products_kernel(
+    width, padded, place_ref, mine_ref, other_ref, mine2_ref, other2_ref, part_ref,
+    slots_ref, gram_ref,
+):
+    sections = (mine_ref, other_ref, mine2_ref, other2_ref)
     core, y, b = place_ref[0], place_ref[1], place_ref[2]
-    total_rows, columns = x_ref.shape
+    columns = mine_ref.shape[1]
+    total_rows = 4 * mine_ref.shape[0]
     section_rows = total_rows // 16
-    copies = []
-    at = 0
-    for ref, size in zip(sections, SECTION_SIZES):
-        rows = pl.ds(at * section_rows, size * section_rows)
-        copies.append(pltpu.make_async_copy(ref, x_ref.at[rows], sems.at[len(copies)]))
-        at += size
-    for copy in copies:
-        copy.start()
-    total = jnp.zeros((16, columns), F32)
-    at = 0
-    for copy, size in zip(copies, SECTION_SIZES):
-        copy.wait()
-        for low in range(at * section_rows, (at + size) * section_rows, 16):
-            piece = x_ref[low : low + 16, :].astype(F32)
-            total = total + piece * piece
-        at += size
-    scale = 0.5 * math.sqrt(columns) / (jnp.sqrt(jnp.sum(total, keepdims=True)) + EPSILON)
+    cuts = strips(columns)
+    squares = jnp.zeros((1, 1), F32)
+    for index, (at, size) in enumerate(cuts):
+        piece = part_ref[at : at + size, at:]
+        piece = piece + gram_strip(other_ref, at, size) + gram_strip(other2_ref, at, size)
+        row = lax.broadcasted_iota(jnp.int32, (size, size), 0)
+        column = lax.broadcasted_iota(jnp.int32, (size, size), 1)
+        diagonal = jnp.where(row == column, piece[:, :size], 0.0)
+        squares = squares + jnp.sum(diagonal, keepdims=True)
+        gram_ref[at : at + size, at:] = piece.astype(BF16)
+        for low, count in cuts[index + 1 :]:
+            gram_ref[low : low + count, at : at + size] = gram_ref[
+                at : at + size, low : low + count
+            ].T
+    scale = 0.5 * math.sqrt(columns) / (jnp.sqrt(squares) + EPSILON)
+    scale_squared = scale * scale
     start = width * (core * 8 + y * 2 + b)
     row = lax.broadcasted_iota(jnp.int32, (padded, columns), 0)
     column = lax.broadcasted_iota(jnp.int32, (padded, columns), 1)
     identity = ((column == row + start) & (row < width)).astype(F32)
-    own = times_transposed(identity.astype(BF16), x_ref).astype(BF16)
-    gram = ((scale * scale) * times(own, x_ref)).astype(BF16)
-    lifted = (scale * times_transposed(gram, x_ref)).astype(BF16)
-    square = scale * times(lifted, x_ref)
-    poly = (COEF_B * gram.astype(F32) + COEF_C * square).astype(BF16)
-    ortho = scale * (COEF_A * own.astype(F32) + times_transposed(poly, x_ref))
-    cross = (scale * times(ortho.astype(BF16), x_ref)).astype(BF16)
-    first = (scale * times_transposed(cross, x_ref)).astype(BF16)
-    second = (scale * times(first, x_ref)).astype(BF16)
-    third = (scale * times_transposed(second, x_ref)).astype(BF16)
-    fourth = scale * times(third, x_ref)
+    aligned = start // 16 * 16
+    found = gram_ref[pl.ds(pl.multiple_of(aligned, 16), padded), :].astype(F32)
+    moved = jnp.concatenate([found[8:], jnp.zeros((8, columns), F32)], axis=0)
+    found = jnp.where(row < width, jnp.where(start == aligned, found, moved), 0.0)
+    gram = (scale_squared * found).astype(BF16)
+    square = scale_squared * times(gram, gram_ref)
+    poly = COEF_B * gram.astype(F32) + COEF_C * square
+    mixed = (COEF_A * identity + poly).astype(BF16)
+    poly = poly.astype(BF16)
+    cross = COEF_A * gram.astype(F32) + scale_squared * times(poly, gram_ref)
+    cross = cross.astype(BF16)
+    second = (scale_squared * times(cross, gram_ref)).astype(BF16)
+    fourth = scale_squared * times(second, gram_ref)
     resid = (
         COEF_A * cross.astype(F32) + COEF_B * second.astype(F32) + COEF_C * fourth - identity
     )
@@ -110,12 +146,14 @@
         cut = slice(8 * part, 8 * part + 8)
         extra = jnp.where(lane == HIGH_LANE + part, high[cut], extra)
         extra = jnp.where(lane == LOW_LANE + part, low[cut], extra)
-    update = math.sqrt(total_rows) * ortho
+    factor = math.sqrt(total_rows) * scale
+    updates = [factor * times_transposed(mixed, ref) for ref in sections]
     below = jnp.zeros((LANES - padded, section_rows), F32)
     spare = lax.broadcasted_iota(jnp.int32, (16, 8, LANES), 2) >= width
 
     def turned(at):
-        piece = update[:, at * section_rows : (at + 1) * section_rows]
+        low = at % 4 * section_rows
+        piece = updates[at // 4][:, low : low + section_rows]
         return jnp.concatenate([piece, below], axis=0).T.reshape(16, 8, LANES)
 
     def spill(rows, by):
@@ -140,27 +178,21 @@
         slots_ref[:, (y + offset) % 4] = packed.astype(BF16)
 
 
-def products(sections, place, width, padded):
-    columns = sections[0].shape[1]
-    total_rows = sum(part.shape[0] for part in sections)
+def products(sections, part, place, width, padded):
+    rows, columns = sections[0].shape
+    vmem = pl.BlockSpec(memory_space=pltpu.VMEM)
     return pl.pallas_call(
         lambda *refs: products_kernel(width, padded, *refs),
-        in_specs=[pl.BlockSpec(memory_space=pltpu.SMEM)]
-        + [pl.BlockSpec(memory_space=pl.ANY)] * len(sections),
-        out_specs=pl.BlockSpec(memory_space=pltpu.VMEM),
+        in_specs=[pl.BlockSpec(memory_space=pltpu.SMEM)] + [vmem] * 5,
+        out_specs=vmem,
         out_shape=jax.ShapeDtypeStruct((16, 4, SLOT_ROWS, LANES), BF16),
-        scratch_shapes=[
-            pltpu.VMEM((total_rows, columns), BF16),
-            pltpu.SemaphoreType.DMA((len(sections),)),
-        ],
+        scratch_shapes=[pltpu.VMEM((columns, columns), BF16)],
         compiler_params=pltpu.CompilerParams(vmem_limit_bytes=VMEM_LIMIT),
         cost_estimate=pl.CostEstimate(
-            flops=20 * padded * total_rows * columns,
-            bytes_accessed=2 * total_rows * columns,
-            transcendentals=0,
+            flops=8 * rows * columns * columns, bytes_accessed=0, transcendentals=0
         ),
         name="products",
-    )(place, *sections)
+    )(place, *sections, part)
 
 
 def regroup_kernel(width, place_ref, owner_ref, returned_ref, update_ref, norms_ref):
@@ -216,8 +248,11 @@
     down = [((i + 1) % 4, i) for i in range(4)]
     swap = [(0, 1), (1, 0)]
 
-    new_momentum, payload = momentum_step(grad, momentum)
-    halves = lax.all_to_all(payload, "core", split_axis=0, concat_axis=0, tiled=True)
+    new_momentum, keep, send = momentum_step(place, grad, momentum)
+    got = lax.ppermute(send, "core", swap)
+    halves = jnp.where(
+        core == 0, jnp.concatenate([keep, got], axis=0), jnp.concatenate([got, keep], axis=0)
+    )
     mine = lax.all_to_all(
         halves.reshape(16, rows // 4, columns), "z", split_axis=0, concat_axis=0, tiled=True
     ).reshape(-1, columns)
@@ -232,9 +267,8 @@
     mine_swapped = lax.ppermute(mine, "core", swap)
     other = jnp.concatenate([other, other_left, other_right, other_far], axis=0)
     other_swapped = lax.ppermute(other, "core", swap)
-    sections = [mine, other, mine_swapped, other_swapped]
-
-    slots = products(sections, place, width, padded)
+    part = gram_part(mine, mine_swapped)
+    slots = products([mine, other, mine_swapped, other_swapped], part, place, width, padded)
     returned = lax.all_to_all(
         slots.reshape(64, SLOT_ROWS, LANES), ("z", "y"), split_axis=0, concat_axis=0, tiled=True
     )

time: 153 us -> 146 us (0.954)
  blocking collectives: 87.4 us -> 82.6 us
  Pallas kernels: 20.9 us -> 16.3 us
  starting transfers between devices: 26.1 us -> 28 us
  other arithmetic: 0.18 us -> 1.79 us
    pallas_call x1, Pallas kernels: 16.4 us -> 8.74 us  [products(): pl.pallas_call(lambda *refs: products_kernel(width, padded, *refs), in_sp...]
    all_to_all x1 -> x0, blocking collectives: 5.07 us -> none  [on_device(): lax.all_to_all(payload, 'core', split_axis=0, concat_axis=0, tiled=True)]
    ppermute x1, waiting for transfers between devices: 3.23 us -> 0.18 us  [on_device(): other_swapped = lax.ppermute(other, 'core', swap)]
    pallas_call x1 -> x2, Pallas kernels: 2.28 us -> 5.29 us  [the longest x1 2.99 us: gram_part(): pl.pallas_call(gram_part_kernel, in_specs=[vmem, vmem], out_specs=vmem, o...]
    ppermute x0 -> x1, starting transfers between devices: none -> 1.91 us  [on_device(): got = lax.ppermute(send, 'core', swap)]
    ppermute x0 -> x1, waiting for transfers between devices: none -> 1.59 us  [on_device(): got = lax.ppermute(send, 'core', swap)]
  transfers between devices with their start and end apart: 9 -> 10, of which waited for: 5 -> 6; matrix products, arithmetic and copies ran while one was open for 0% -> 0% of each run, Pallas kernels for 0% -> 2%
where the time goes in v6:
time: 146 us; the launch traced here: 144 us
  blocking collectives  82.6 us (57%)
  starting transfers between devices  28 us (19%)
  Pallas kernels  16.3 us (11%)
  waiting for transfers between devices  14.6 us (10%)
  other arithmetic  1.79 us (1%)
    all_to_all x1, blocking collectives, on_device(): lax.all_to_all(slots.reshape(64, SLOT_ROWS, LANES), ('z', 'y'), split_axi...  40.5 us
    all_to_all x1, blocking collectives, on_device(): lax.all_to_all(halves.reshape(16, rows // 4, columns), 'z', split_axis=0,...  38 us
    pallas_call x1, Pallas kernels, products(): pl.pallas_call(lambda *refs: products_kernel(width, padded, *refs), in_sp...  8.74 us
    ppermute x1, waiting for transfers between devices, on_device(): other_far = lax.ppermute(other_right, 'y', down)  8.54 us
    ppermute x1, starting transfers between devices, on_device(): other_right = lax.ppermute(other, 'y', down)  4.78 us
    all_to_all x1, blocking collectives, on_device(): lax.all_to_all(returned.reshape(2, -1, SLOT_ROWS, LANES), 'core', split_a...  4.04 us
    ppermute x1, starting transfers between devices, on_device(): other_far = lax.ppermute(other_right, 'y', down)  3.9 us
    ppermute x1, starting transfers between devices, on_device(): mine_right = lax.ppermute(mine, 'y', down)  3.57 us
  transfers between devices with their start and end apart: 10, of which 6 were waited for; matrix products, arithmetic and copies ran while one was open for 0% of the time, Pallas kernels for 2%

profile of v6, /device:TPU:6, one launch (start us, length us, event | category | flops | bytes accessed | tf_op | source)
XLA Modules:
  0.0 144.2 jit_solution(5840157468728678329)
XLA Ops:
  0.6 0.6 pad_add_fusion.place_ref.refs_0_
  1.2 2.3 %momentum_step.1 = (f32[4,32,1408]{2,1,0:T(8,128)}, bf16[4,16,1408]{2,1,0:T(8,128)(2,1)}, bf16[4,16,1408]{2,1,0:T(8,128)(2,1)}) custom-call(s32[4]{0:T(128)} %pad_add_fusion.place_ref.refs_0_, bf16[4,32,1408]{2,1,0:T(8,128)(2,1)} %grad_ref.1, f32[4,32,1408]{2,1,0:T(8,128)} %momentum_ref.1), custom_call_target="tpu_custom_call" | custom-call | tf_op jit(solution)/shard_map/momentum_step/pallas_call | solution.py:40
  3.5 1.9 %collective-permute-start = (bf16[4,16,1408]{2,1,0:T(8,128)(2,1)}, bf16[4,16,1408]{2,1,0:T(8,128)(2,1)S(1)}, u32[]{:S(2)}, u32[]{:S(2)}) collective-permute-start(bf16[4,16,1408]{2,1,0:T(8,128)(2,1)} %get-tuple-element.10), channel_id=1, source_target_pairs={{0,64},{64,0},{1,65},{65,1},{2,66},{66,2},{3,67},{67,3},{4,68},{68... | collective-permute-start | bytes 540680 | tf_op jit(solution)/shard_map/ppermute | solution.py:252
  5.5 1.6 %collective-permute-done = bf16[4,16,1408]{2,1,0:T(8,128)(2,1)S(1)} collective-permute-done((bf16[4,16,1408]{2,1,0:T(8,128)(2,1)}, bf16[4,16,1408]{2,1,0:T(8,128)(2,1)S(1)}, u32[]{:S(2)}, u32[]{:S(2)}) %collective-permute-start) | collective-permute-done | bytes 180256 | tf_op jit(solution)/shard_map/ppermute | solution.py:252
  7.1 1.1 maximum_select_fusion
  8.1 38.0 %all_to_all.15 = bf16[16,8,1408]{2,1,0:T(8,128)(2,1)S(1)} all-to-all(bf16[16,8,1408]{2,1,0:T(8,128)(2,1)S(1)} %bitcast.14), channel_id=1, replica_groups=mesh['x'=4,'core'=2,'y'=4,'z'=16] {'z'}, dimensions={0} | all-to-all | bytes 720896 | tf_op jit(solution)/shard_map/all_to_all | solution.py:256
  46.2 3.5 %collective-permute-start.1 = (bf16[128,1408]{1,0:T(8,128)(2,1)S(1)}, bf16[128,1408]{1,0:T(8,128)(2,1)S(1)}, u32[]{:S(2)}, u32[]{:S(2)}) collective-permute-start(bf16[128,1408]{1,0:T(8,128)(2,1)S(1)} %bitcast.15), channel_id=1, source_target_pairs={{0,16},{16,32},{32,48},{48,0},{1,17},{17,33},{33,49},{49,1},{2,18}... | collective-permute-start | bytes 1081352 | tf_op jit(solution)/shard_map/ppermute | solution.py:260
  49.6 2.4 %collective-permute-start.4 = (bf16[128,1408]{1,0:T(8,128)(2,1)S(1)}, bf16[128,1408]{1,0:T(8,128)(2,1)S(1)}, u32[]{:S(2)}, u32[]{:S(2)}) collective-permute-start(bf16[128,1408]{1,0:T(8,128)(2,1)S(1)} %bitcast.16), channel_id=1, source_target_pairs={{0,1},{1,0},{2,3},{3,2},{4,5},{5,4},{6,7},{7,6},{8,9},{9,8},{10,11... | collective-permute-start | bytes 1081352 | tf_op jit(solution)/shard_map/ppermute | solution.py:259
  52.0 3.6 %collective-permute-start.2 = (bf16[128,1408]{1,0:T(8,128)(2,1)S(1)}, bf16[128,1408]{1,0:T(8,128)(2,1)S(1)}, u32[]{:S(2)}, u32[]{:S(2)}) collective-permute-start(bf16[128,1408]{1,0:T(8,128)(2,1)S(1)} %bitcast.17), channel_id=1, source_target_pairs={{16,0},{32,16},{48,32},{0,48},{17,1},{33,17},{49,33},{1,49},{18,2}... | collective-permute-start | bytes 1081352 | tf_op jit(solution)/shard_map/ppermute | solution.py:261
  55.6 1.1 collective-permute-done.1
  56.7 2.3 %collective-permute-start.3 = (bf16[128,1408]{1,0:T(8,128)(2,1)S(1)}, bf16[128,1408]{1,0:T(8,128)(2,1)S(1)}, u32[]{:S(2)}, u32[]{:S(2)}) collective-permute-start(bf16[128,1408]{1,0:T(8,128)(2,1)S(1)} %collective-permute-done.1), channel_id=1, source_target_pairs={{0,16},{16,32},{32,48},{48,0},{1,17},{17,33},{33,49},{49,1},{2,18}... | collective-permute-start | bytes 1081352 | tf_op jit(solution)/shard_map/ppermute | solution.py:264
  58.9 0.0 collective-permute-done.4
  59.0 4.8 %collective-permute-start.6 = (bf16[128,1408]{1,0:T(8,128)(2,1)S(1)}, bf16[128,1408]{1,0:T(8,128)(2,1)S(1)}, u32[]{:S(2)}, u32[]{:S(2)}) collective-permute-start(bf16[128,1408]{1,0:T(8,128)(2,1)S(1)} %collective-permute-done.4), channel_id=1, source_target_pairs={{16,0},{32,16},{48,32},{0,48},{17,1},{33,17},{49,33},{1,49},{18,2}... | collective-permute-start | bytes 1081352 | tf_op jit(solution)/shard_map/ppermute | solution.py:263
  63.7 1.9 %collective-permute-start.5 = (bf16[128,1408]{1,0:T(8,128)(2,1)S(1)}, bf16[128,1408]{1,0:T(8,128)(2,1)S(1)}, u32[]{:S(2)}, u32[]{:S(2)}) collective-permute-start(bf16[128,1408]{1,0:T(8,128)(2,1)S(1)} %collective-permute-done.4), channel_id=1, source_target_pairs={{0,16},{16,32},{32,48},{48,0},{1,17},{17,33},{33,49},{49,1},{2,18}... | collective-permute-start | bytes 1081352 | tf_op jit(solution)/shard_map/ppermute | solution.py:262
  65.7 0.0 collective-permute-done.2
  65.7 3.1 %collective-permute-done.3 = bf16[128,1408]{1,0:T(8,128)(2,1)S(1)} collective-permute-done((bf16[128,1408]{1,0:T(8,128)(2,1)S(1)}, bf16[128,1408]{1,0:T(8,128)(2,1)S(1)}, u32[]{:S(2)}, u32[]{:S(2)}) %collective-permute-start.3) | collective-permute-done | bytes 360480 | tf_op jit(solution)/shard_map/ppermute | solution.py:264
  68.8 0.1 pad_maximum_fusion.one_ref.refs_1_
  68.9 1.9 %collective-permute-start.8 = (bf16[512,1408]{1,0:T(8,128)(2,1)S(1)}, bf16[512,1408]{1,0:T(8,128)(2,1)S(1)}, u32[]{:S(2)}, u32[]{:S(2)}) collective-permute-start(bf16[512,1408]{1,0:T(8,128)(2,1)S(1)} %pad_maximum_fusion.one_ref.refs_1_), channel_id=1, source_target_pairs={{0,64},{64,0},{1,65},{65,1},{2,66},{66,2},{3,67},{67,3},{4,68},{68... | collective-permute-start | bytes 4325384 | tf_op jit(solution)/shard_map/ppermute | solution.py:267
  70.8 0.0 collective-permute-done.6
  70.8 3.9 %collective-permute-start.7 = (bf16[128,1408]{1,0:T(8,128)(2,1)S(1)}, bf16[128,1408]{1,0:T(8,128)(2,1)S(1)}, u32[]{:S(2)}, u32[]{:S(2)}) collective-permute-start(bf16[128,1408]{1,0:T(8,128)(2,1)S(1)} %collective-permute-done.6), channel_id=1, source_target_pairs={{16,0},{32,16},{48,32},{0,48},{17,1},{33,17},{49,33},{1,49},{18,2}... | collective-permute-start | bytes 1081352 | tf_op jit(solution)/shard_map/ppermute | solution.py:265
  74.7 0.2 collective-permute-done.5
  75.0 8.5 %collective-permute-done.7 = bf16[128,1408]{1,0:T(8,128)(2,1)S(1)} collective-permute-done((bf16[128,1408]{1,0:T(8,128)(2,1)S(1)}, bf16[128,1408]{1,0:T(8,128)(2,1)S(1)}, u32[]{:S(2)}, u32[]{:S(2)}) %collective-permute-start.7) | collective-permute-done | bytes 360480 | tf_op jit(solution)/shard_map/ppermute | solution.py:265
  83.6 0.0 copy-start
  83.6 1.9 %collective-permute-start.9 = (bf16[512,1408]{1,0:T(8,128)(2,1)S(1)}, bf16[512,1408]{1,0:T(8,128)(2,1)S(1)}, u32[]{:S(2)}, u32[]{:S(2)}) collective-permute-start(bf16[512,1408]{1,0:T(8,128)(2,1)S(1)} %constant_dynamic-update-slice_fusion.refs_2_), channel_id=1, source_target_pairs={{0,64},{64,0},{1,65},{65,1},{2,66},{66,2},{3,67},{67,3},{4,68},{68... | collective-permute-start | bytes 4325384 | tf_op jit(solution)/shard_map/ppermute | solution.py:269
  85.5 0.0 collective-permute-done.8.two_ref.refs_3_
  85.5 3.0 %gram_part.1.refs_5_ = f32[1408,1408]{1,0:T(8,128)S(1)} custom-call(bf16[512,1408]{1,0:T(8,128)(2,1)S(1)} %pad_maximum_fusion.one_ref.refs_1_, bf16[512,1408]{1,0:T(8,128)(2,1)S(1)} %collective-permute-done.8.two_ref.refs_3_), custom_call_target="tpu_custom_call" | custom-call | flops 2030043136 | tf_op jit(solution)/shard_map/gram_part/pallas_call | solution.py:72
  88.5 0.2 collective-permute-done.9.refs_4_
  88.7 8.7 %products.1 = bf16[16,4,24,128]{3,2,1,0:T(8,128)(2,1)S(1)} custom-call(s32[4]{0:T(128)S(1)} %copy-done, bf16[512,1408]{1,0:T(8,128)(2,1)S(1)} %pad_maximum_fusion.one_ref.refs_1_, bf16[512,1408]{1,0:T(8,128)(2,1)S(1)} %constant_dynamic-update-slice_fusion.refs_2_, bf16[512,1408]{1,0:T(8,128)(2,1)S(1)} %collective-permute-done.8.two_ref.refs_3_, ...), custom_call_target="tpu_custom_call" | custom-call | flops 8120172544 | tf_op jit(solution)/shard_map/products/pallas_call | solution.py:184
  97.4 0.0 copy-start.1
  97.5 40.5 %all_to_all.16 = bf16[64,24,128]{2,1,0:T(8,128)(2,1)S(1)} all-to-all(bf16[64,24,128]{2,1,0:T(8,128)(2,1)S(1)} %bitcast.11), channel_id=1, replica_groups=mesh['x'=4,'core'=2,'y'=4,'z'=16] {'z','y'}, dimensions={0} | all-to-all | bytes 786432 | tf_op jit(solution)/shard_map/all_to_all | solution.py:272
  138.0 4.0 %all_to_all.17 = bf16[2,32,24,128]{3,2,1,0:T(8,128)(2,1)S(1)} all-to-all(bf16[2,32,24,128]{3,2,1,0:T(8,128)(2,1)S(1)} %bitcast.13), channel_id=1, replica_groups=mesh['x'=4,'core'=2,'y'=4,'z'=16] {'core'}, dimensions={0} | all-to-all | bytes 786432 | tf_op jit(solution)/shard_map/all_to_all | solution.py:275
  142.0 2.2 %regroup.1 = (bf16[4,32,1408]{2,1,0:T(8,128)(2,1)}, f32[1,88]{1,0:T(1,128)}) custom-call(s32[4]{0:T(128)S(1)} %copy-done, s32[4]{0:T(128)S(1)} %bitcast.12, bf16[2,4,2,4,24,128]{5,4,3,2,1,0:T(8,128)(2,1)S(1)} %bitcast.10), custom_call_target="tpu_custom_call" | custom-call | tf_op jit(solution)/shard_map/regroup/pallas_call | solution.py:228
  (6 shorter events, 0.1 us)
Async XLA Ops:
  3.5 3.5 %collective-permute-start = (bf16[4,16,1408]{2,1,0:T(8,128)(2,1)}, bf16[4,16,1408]{2,1,0:T(8,128)(2,1)S(1)}, u32[]{:S(2)}, u32[]{:S(2)}) collective-permute-start(bf16[4,16,1408]{2,1,0:T(8,128)(2,1)} %get-tuple-element.10), channel_id=1, source_target_pairs={{0,64},{64,0},{1,65},{65,1},{2,66},{66,2},{3,67},{67,3},{4,68},{68... | collective-permute-start | bytes 540680 | tf_op jit(solution)/shard_map/ppermute | solution.py:252
  46.2 10.5 %collective-permute-start.1 = (bf16[128,1408]{1,0:T(8,128)(2,1)S(1)}, bf16[128,1408]{1,0:T(8,128)(2,1)S(1)}, u32[]{:S(2)}, u32[]{:S(2)}) collective-permute-start(bf16[128,1408]{1,0:T(8,128)(2,1)S(1)} %bitcast.15), channel_id=1, source_target_pairs={{0,16},{16,32},{32,48},{48,0},{1,17},{17,33},{33,49},{49,1},{2,18}... | collective-permute-start | bytes 1081352 | tf_op jit(solution)/shard_map/ppermute | solution.py:260
  49.6 9.3 %collective-permute-start.4 = (bf16[128,1408]{1,0:T(8,128)(2,1)S(1)}, bf16[128,1408]{1,0:T(8,128)(2,1)S(1)}, u32[]{:S(2)}, u32[]{:S(2)}) collective-permute-start(bf16[128,1408]{1,0:T(8,128)(2,1)S(1)} %bitcast.16), channel_id=1, source_target_pairs={{0,1},{1,0},{2,3},{3,2},{4,5},{5,4},{6,7},{7,6},{8,9},{9,8},{10,11... | collective-permute-start | bytes 1081352 | tf_op jit(solution)/shard_map/ppermute | solution.py:259
  52.0 13.7 %collective-permute-start.2 = (bf16[128,1408]{1,0:T(8,128)(2,1)S(1)}, bf16[128,1408]{1,0:T(8,128)(2,1)S(1)}, u32[]{:S(2)}, u32[]{:S(2)}) collective-permute-start(bf16[128,1408]{1,0:T(8,128)(2,1)S(1)} %bitcast.17), channel_id=1, source_target_pairs={{16,0},{32,16},{48,32},{0,48},{17,1},{33,17},{49,33},{1,49},{18,2}... | collective-permute-start | bytes 1081352 | tf_op jit(solution)/shard_map/ppermute | solution.py:261
  56.7 12.1 %collective-permute-start.3 = (bf16[128,1408]{1,0:T(8,128)(2,1)S(1)}, bf16[128,1408]{1,0:T(8,128)(2,1)S(1)}, u32[]{:S(2)}, u32[]{:S(2)}) collective-permute-start(bf16[128,1408]{1,0:T(8,128)(2,1)S(1)} %collective-permute-done.1), channel_id=1, source_target_pairs={{0,16},{16,32},{32,48},{48,0},{1,17},{17,33},{33,49},{49,1},{2,18}... | collective-permute-start | bytes 1081352 | tf_op jit(solution)/shard_map/ppermute | solution.py:264
  59.0 11.9 %collective-permute-start.6 = (bf16[128,1408]{1,0:T(8,128)(2,1)S(1)}, bf16[128,1408]{1,0:T(8,128)(2,1)S(1)}, u32[]{:S(2)}, u32[]{:S(2)}) collective-permute-start(bf16[128,1408]{1,0:T(8,128)(2,1)S(1)} %collective-permute-done.4), channel_id=1, source_target_pairs={{16,0},{32,16},{48,32},{0,48},{17,1},{33,17},{49,33},{1,49},{18,2}... | collective-permute-start | bytes 1081352 | tf_op jit(solution)/shard_map/ppermute | solution.py:263
  63.7 11.2 %collective-permute-start.5 = (bf16[128,1408]{1,0:T(8,128)(2,1)S(1)}, bf16[128,1408]{1,0:T(8,128)(2,1)S(1)}, u32[]{:S(2)}, u32[]{:S(2)}) collective-permute-start(bf16[128,1408]{1,0:T(8,128)(2,1)S(1)} %collective-permute-done.4), channel_id=1, source_target_pairs={{0,16},{16,32},{32,48},{48,0},{1,17},{17,33},{33,49},{49,1},{2,18}... | collective-permute-start | bytes 1081352 | tf_op jit(solution)/shard_map/ppermute | solution.py:262
  68.9 16.6 %collective-permute-start.8 = (bf16[512,1408]{1,0:T(8,128)(2,1)S(1)}, bf16[512,1408]{1,0:T(8,128)(2,1)S(1)}, u32[]{:S(2)}, u32[]{:S(2)}) collective-permute-start(bf16[512,1408]{1,0:T(8,128)(2,1)S(1)} %pad_maximum_fusion.one_ref.refs_1_), channel_id=1, source_target_pairs={{0,64},{64,0},{1,65},{65,1},{2,66},{66,2},{3,67},{67,3},{4,68},{68... | collective-permute-start | bytes 4325384 | tf_op jit(solution)/shard_map/ppermute | solution.py:267
  70.8 12.7 %collective-permute-start.7 = (bf16[128,1408]{1,0:T(8,128)(2,1)S(1)}, bf16[128,1408]{1,0:T(8,128)(2,1)S(1)}, u32[]{:S(2)}, u32[]{:S(2)}) collective-permute-start(bf16[128,1408]{1,0:T(8,128)(2,1)S(1)} %collective-permute-done.6), channel_id=1, source_target_pairs={{16,0},{32,16},{48,32},{0,48},{17,1},{33,17},{49,33},{1,49},{18,2}... | collective-permute-start | bytes 1081352 | tf_op jit(solution)/shard_map/ppermute | solution.py:265
  83.6 5.1 %copy-start = (s32[4]{0:T(128)S(1)}, s32[4]{0:T(128)}, u32[]{:S(2)}) copy-start(s32[4]{0:T(128)} %pad_add_fusion.place_ref.refs_0_) | copy-start | bytes 52
  83.6 5.1 %collective-permute-start.9 = (bf16[512,1408]{1,0:T(8,128)(2,1)S(1)}, bf16[512,1408]{1,0:T(8,128)(2,1)S(1)}, u32[]{:S(2)}, u32[]{:S(2)}) collective-permute-start(bf16[512,1408]{1,0:T(8,128)(2,1)S(1)} %constant_dynamic-update-slice_fusion.refs_2_), channel_id=1, source_target_pairs={{0,64},{64,0},{1,65},{65,1},{2,66},{66,2},{3,67},{67,3},{4,68},{68... | collective-permute-start | bytes 4325384 | tf_op jit(solution)/shard_map/ppermute | solution.py:269
  97.4 44.5 %copy-start.1 = (s32[1,4]{1,0:T(1,128)S(1)}, s32[1,4]{1,0:T(1,128)}, u32[]{:S(2)}) copy-start(s32[1,4]{1,0:T(1,128)} %param.5) | copy-start | bytes 52

commit v7 on v6

v7 whole, which is shorter than its diff:
```python
import math

import jax
import jax.numpy as jnp
from jax import lax
from jax.experimental import pallas as pl
from jax.experimental.pallas import tpu as pltpu
from jax.sharding import Mesh, PartitionSpec as P

DECAY = 0.95
COEF_A = 3.4445
COEF_B = -4.775
COEF_C = 2.0315
EPSILON = 1e-07

F32 = jnp.float32
BF16 = jnp.bfloat16
VMEM_LIMIT = 36 * 1024 * 1024
LANES = 128
STRIP = 256
LOW_LANE = 64


def momentum_kernel(grad_ref, momentum_ref, new_ref, keep_ref, send_ref):
    core = lax.axis_index("core")
    new = DECAY * momentum_ref[...] + grad_ref[...].astype(F32)
    new_ref[...] = new
    half = send_ref.shape[1]
    first = core == 0
    keep_ref[core] = jnp.where(first, new[:, :half], new[:, half:]).astype(BF16)
    send_ref[...] = jnp.where(first, new[:, half:], new[:, :half]).astype(BF16)


def momentum_step(grad, momentum):
    matrices, rows, columns = grad.shape
    vmem = pl.BlockSpec(memory_space=pltpu.VMEM)
    half = (matrices, rows // 2, columns)
    return pl.pallas_call(
        momentum_kernel,
        in_specs=[vmem, vmem],
        out_specs=[vmem, vmem, vmem],
        out_shape=[
            jax.ShapeDtypeStruct(grad.shape, F32),
            jax.ShapeDtypeStruct((2,) + half, BF16),
            jax.ShapeDtypeStruct(half, BF16),
        ],
        compiler_params=pltpu.CompilerParams(vmem_limit_bytes=60 * 1024 * 1024),
        name="momentum_step",
    )(grad, momentum)


def strips(columns):
    return [(at, min(STRIP, columns - at)) for at in range(0, columns, STRIP)]


def gram_strip(x_ref, at, size):
    return lax.dot_general(
        x_ref[:, at : at + size],
        x_ref[:, at:],
        (((0,), (0,)), ((), ())),
        preferred_element_type=F32,
    )


def gram_part_kernel(one_ref, two_ref, part_ref):
    for at, size in strips(one_ref.shape[1]):
        total = gram_strip(one_ref, at, size) + gram_strip(two_ref, at, size)
        part_ref[at : at + size, at:] = total


def gram_part(one, two):
    rows, columns = one.shape
    vmem = pl.BlockSpec(memory_space=pltpu.VMEM)
    return pl.pallas_call(
        gram_part_kernel,
        in_specs=[vmem, vmem],
        out_specs=vmem,
        out_shape=jax.ShapeDtypeStruct((columns, columns), F32),
        compiler_params=pltpu.CompilerParams(vmem_limit_bytes=24 * 1024 * 1024),
        cost_estimate=pl.CostEstimate(
            flops=2 * rows * columns * columns, bytes_accessed=0, transcendentals=0
        ),
        name="gram_part",
    )(one, two)


def times(block, matrix):
    return jnp.dot(block, matrix, preferred_element_type=F32)


def mirror(matrix_ref, cuts, index):
    at, size = cuts[index]
    for low, count in cuts[index + 1 :]:
        matrix_ref[low : low + count, at : at + size] = matrix_ref[
            at : at + size, low : low + count
        ].T


def products_kernel(
    mine_ref, other_ref, mine2_ref, other2_ref, part_ref, slots_ref, gram_ref, poly_ref
):
    core, b = lax.axis_index("core"), lax.axis_index("z") % 2
    section_rows, columns = mine_ref.shape
    total_rows = 4 * section_rows
    cuts = strips(columns)
    squares = jnp.zeros((1, 1), F32)
    for index, (at, size) in enumerate(cuts):
        piece = part_ref[at : at + size, at:]
        piece = piece + gram_strip(other_ref, at, size) + gram_strip(other2_ref, at, size)
        row = lax.broadcasted_iota(jnp.int32, (size, size), 0)
        column = lax.broadcasted_iota(jnp.int32, (size, size), 1)
        diagonal = jnp.where(row == column, piece[:, :size], 0.0)
        squares = squares + jnp.sum(diagonal, keepdims=True)
        gram_ref[at : at + size, at:] = piece.astype(BF16)
        mirror(gram_ref, cuts, index)
    scale = 0.5 * math.sqrt(columns) / (jnp.sqrt(squares) + EPSILON)
    scale_squared = scale * scale
    for index, (at, size) in enumerate(cuts):
        rows = gram_ref[at : at + size, :]
        square = scale_squared * times(rows, gram_ref[:, at:])
        poly = scale_squared * (COEF_B * rows[:, at:].astype(F32) + COEF_C * square)
        poly_ref[at : at + size, at:] = poly.astype(BF16)
        mirror(poly_ref, cuts, index)
    own = mine_ref[: total_rows // 16, :]
    ortho = COEF_A * own.astype(F32) + times(own, poly_ref[...])
    update = (math.sqrt(total_rows) * scale) * ortho
    slots_ref[:, :, :columns] = update.reshape(16, -1, columns).astype(BF16)

    width = columns // 4
    start = pl.multiple_of(width * (core * 2 + b), 16)
    block = pl.ds(start, width)
    row = lax.broadcasted_iota(jnp.int32, (width, columns), 0)
    column = lax.broadcasted_iota(jnp.int32, (width, columns), 1)
    cross = COEF_A * gram_ref[block, :].astype(F32) + times(poly_ref[block, :], gram_ref[...])
    cross = (scale_squared * cross).astype(BF16)
    resid = COEF_A * cross.astype(F32) + times(cross, poly_ref[...])
    resid = resid - (column == row + start).astype(F32)
    norms = jnp.sqrt(jnp.sum(resid * resid, axis=1, keepdims=True))
    high = norms.astype(BF16).astype(F32)
    low = norms - high
    lane = lax.broadcasted_iota(jnp.int32, (8, LANES), 1)
    extra = jnp.zeros((8, LANES), F32)
    for part in range(width // 8):
        cut = slice(8 * part, 8 * part + 8)
        extra = jnp.where(lane == part, high[cut], extra)
        extra = jnp.where(lane == LOW_LANE + part, low[cut], extra)
    slots_ref[:, :, columns:] = jnp.broadcast_to(extra[None], (16, 8, LANES)).astype(BF16)


def products(sections, part):
    rows, columns = sections[0].shape
    vmem = pl.BlockSpec(memory_space=pltpu.VMEM)
    return pl.pallas_call(
        products_kernel,
        in_specs=[vmem] * 5,
        out_specs=vmem,
        out_shape=jax.ShapeDtypeStruct((16, 8, columns + LANES), BF16),
        scratch_shapes=[pltpu.VMEM((columns, columns), BF16)] * 2,
        compiler_params=pltpu.CompilerParams(vmem_limit_bytes=VMEM_LIMIT),
        cost_estimate=pl.CostEstimate(
            flops=12 * rows * columns * columns, bytes_accessed=0, transcendentals=0
        ),
        name="products",
    )(*sections, part)


def regroup_kernel(owner_ref, near_ref, far_ref, update_ref, norms_ref):
    core, y, z = lax.axis_index("core"), lax.axis_index("y"), lax.axis_index("z")
    matrices, rows, columns = update_ref.shape
    half = rows // 2
    near, far = near_ref[core], far_ref[core]
    update_ref[:, :half] = jnp.where(core == 0, near, far)[:, :, :columns]
    update_ref[:, half:] = jnp.where(core == 0, far, near)[:, :, :columns]
    near, far = near[:, :, columns:].astype(F32), far[:, :, columns:].astype(F32)
    tiles = jnp.where(z // 8 == core, near, far)
    tiles = jnp.where(z // 4 % 2 == 0, tiles[:, :8], tiles[:, 8:])
    tile = tiles[0]
    for m in range(1, matrices):
        tile = jnp.where(owner_ref[m] == y, tiles[m], tile)
    turned = jnp.concatenate([tile] * 4, axis=0).T
    count = norms_ref.shape[1] // 8
    for quarter in range(4):

        @pl.when(z % 4 == quarter)
        def _():
            for part in range(count):
                at = quarter * count + part
                value = turned[at : at + 1, :8] + turned[LOW_LANE + at : LOW_LANE + at + 1, :8]
                norms_ref[:, 8 * part : 8 * part + 8] = value


def regroup(owner, near, far):
    matrices, half = near.shape[1:3]
    columns = near.shape[3] - LANES
    vmem = pl.BlockSpec(memory_space=pltpu.VMEM)
    return pl.pallas_call(
        regroup_kernel,
        in_specs=[pl.BlockSpec(memory_space=pltpu.SMEM), vmem, vmem],
        out_specs=[vmem, vmem],
        out_shape=[
            jax.ShapeDtypeStruct((matrices, 2 * half, columns), BF16),
            jax.ShapeDtypeStruct((1, columns // 16), F32),
        ],
        compiler_params=pltpu.CompilerParams(vmem_limit_bytes=VMEM_LIMIT),
        name="regroup",
    )(owner, near, far)


def on_device(grad, momentum, owner):
    matrices, rows, columns = grad.shape
    core = lax.axis_index("core")
    up = [(i, (i + 1) % 4) for i in range(4)]
    down = [((i + 1) % 4, i) for i in range(4)]
    swap = [(0, 1), (1, 0)]

    new_momentum, halves, send = momentum_step(grad, momentum)
    got = lax.ppermute(send, "core", swap)
    halves = lax.dynamic_update_slice_in_dim(halves, got[None], 1 - core, 0)
    mine = lax.all_to_all(
        halves.reshape(16, rows // 4, columns), "z", split_axis=0, concat_axis=0, tiled=True
    ).reshape(-1, columns)
    other = lax.ppermute(mine, "z", [(i, i ^ 1) for i in range(16)])
    mine_left = lax.ppermute(mine, "y", up)
    mine_right = lax.ppermute(mine, "y", down)
    other_left = lax.ppermute(other, "y", up)
    other_right = lax.ppermute(other, "y", down)
    mine_far = lax.ppermute(mine_left, "y", up)
    other_far = lax.ppermute(other_right, "y", down)
    mine = jnp.concatenate([mine, mine_left, mine_right, mine_far], axis=0)
    mine_swapped = lax.ppermute(mine, "core", swap)
    other = jnp.concatenate([other, other_left, other_right, other_far], axis=0)
    other_swapped = lax.ppermute(other, "core", swap)
    part = gram_part(mine, mine_swapped)
    slots = products([mine, other, mine_swapped, other_swapped], part)
    near = lax.all_to_all(slots, "z", split_axis=0, concat_axis=0, tiled=True)
    near = near.reshape(2, matrices, rows // 2, columns + LANES)
    far = lax.ppermute(near, "core", swap)
    out_update, norms = regroup(owner.reshape(matrices), near, far)
    return new_momentum, out_update, norms


def solution(mesh):
    experts, shards = mesh.devices.shape
    split = Mesh(mesh.devices.reshape(experts // 2, 2, 4, shards // 4), ("x", "core", "y", "z"))
    groups, rows = ("x", "core"), ("y", "z")
    return jax.shard_map(
        on_device,
        mesh=split,
        in_specs=(P(groups, rows, None), P(groups, rows, None), P(groups, None)),
        out_specs=(P(groups, rows, None), P(groups, rows, None), P(groups, rows)),
        check_vma=False,
    )
```

time: 146 us -> 141 us (0.966)
  blocking collectives: 82.6 us -> 73 us
  Pallas kernels: 16.3 us -> 18.4 us
  starting transfers between devices: 28 us -> 29.9 us
  waiting for transfers between devices: 14.6 us -> 16.3 us
  other arithmetic: 1.79 us -> 0.11 us
    all_to_all x2 -> x1, blocking collectives: 44.5 us -> 34.8 us  [on_device(): near = lax.all_to_all(slots, 'z', split_axis=0, concat_axis=0, tiled=True)]
    pallas_call x3, Pallas kernels: 13.3 us -> 15.4 us  [the longest x1 11.6 us: products(): pl.pallas_call(products_kernel, in_specs=[vmem] * 5, out_specs=vmem, out_...]
    ppermute x0 -> x1, starting transfers between devices: none -> 1.91 us  [on_device(): far = lax.ppermute(near, 'core', swap)]
    ppermute x0 -> x1, waiting for transfers between devices: none -> 1.69 us  [on_device(): far = lax.ppermute(near, 'core', swap)]
  transfers between devices with their start and end apart: 10 -> 11, of which waited for: 6 -> 7; matrix products, arithmetic and copies ran while one was open for 0% -> 0% of each run, Pallas kernels for 2% -> 2%
where the time goes in v7:
time: 141 us; the launch traced here: 139 us
  blocking collectives  73 us (52%)
  starting transfers between devices  29.9 us (21%)
  Pallas kernels  18.4 us (13%)
  waiting for transfers between devices  16.3 us (12%)
    all_to_all x1, blocking collectives, on_device(): lax.all_to_all(halves.reshape(16, rows // 4, columns), 'z', split_axis=0,...  38.2 us
    all_to_all x1, blocking collectives, on_device(): near = lax.all_to_all(slots, 'z', split_axis=0, concat_axis=0, tiled=True)  34.8 us
    pallas_call x1, Pallas kernels, products(): pl.pallas_call(products_kernel, in_specs=[vmem] * 5, out_specs=vmem, out_...  11.6 us
    ppermute x1, waiting for transfers between devices, on_device(): other_far = lax.ppermute(other_right, 'y', down)  8.54 us
    ppermute x1, starting transfers between devices, on_device(): other_right = lax.ppermute(other, 'y', down)  4.78 us
    ppermute x1, starting transfers between devices, on_device(): other_far = lax.ppermute(other_right, 'y', down)  3.89 us
    ppermute x1, starting transfers between devices, on_device(): mine_right = lax.ppermute(mine, 'y', down)  3.57 us
    ppermute x1, starting transfers between devices, on_device(): mine_left = lax.ppermute(mine, 'y', up)  3.47 us
  transfers between devices with their start and end apart: 11, of which 7 were waited for; matrix products, arithmetic and copies ran while one was open for 0% of the time, Pallas kernels for 2%

profile of v7, /device:TPU:6, one launch (start us, length us, event | category | flops | bytes accessed | tf_op | source)
XLA Modules:
  0.0 139.4 jit_solution(13367680274538024184)
XLA Ops:
  0.6 2.4 %momentum_step.1 = (f32[4,32,1408]{2,1,0:T(8,128)}, bf16[2,4,16,1408]{3,2,1,0:T(8,128)(2,1)}, bf16[4,16,1408]{2,1,0:T(8,128)(2,1)}) custom-call(bf16[4,32,1408]{2,1,0:T(8,128)(2,1)} %grad_ref.1, f32[4,32,1408]{2,1,0:T(8,128)} %momentum_ref.1), custom_call_target="tpu_custom_call" | custom-call | tf_op jit(solution)/shard_map/momentum_step/pallas_call | solution.py:38
  3.0 1.9 %collective-permute-start = (bf16[4,16,1408]{2,1,0:T(8,128)(2,1)}, bf16[4,16,1408]{2,1,0:T(8,128)(2,1)S(1)}, u32[]{:S(2)}, u32[]{:S(2)}) collective-permute-start(bf16[4,16,1408]{2,1,0:T(8,128)(2,1)} %get-tuple-element.10), channel_id=1, source_target_pairs={{0,64},{64,0},{1,65},{65,1},{2,66},{66,2},{3,67},{67,3},{4,68},{68... | collective-permute-start | bytes 540680 | tf_op jit(solution)/shard_map/ppermute | solution.py:217
  4.9 1.6 %collective-permute-done = bf16[4,16,1408]{2,1,0:T(8,128)(2,1)S(1)} collective-permute-done((bf16[4,16,1408]{2,1,0:T(8,128)(2,1)}, bf16[4,16,1408]{2,1,0:T(8,128)(2,1)S(1)}, u32[]{:S(2)}, u32[]{:S(2)}) %collective-permute-start) | collective-permute-done | bytes 180256 | tf_op jit(solution)/shard_map/ppermute | solution.py:217
  6.5 0.7 bitcast_dynamic-update-slice_fusion
  7.2 38.2 %all_to_all.10 = bf16[16,8,1408]{2,1,0:T(8,128)(2,1)S(1)} all-to-all(bf16[16,8,1408]{2,1,0:T(8,128)(2,1)} %bitcast.13), channel_id=1, replica_groups=mesh['x'=4,'core'=2,'y'=4,'z'=16] {'z'}, dimensions={0} | all-to-all | bytes 720896 | tf_op jit(solution)/shard_map/all_to_all | solution.py:219
  45.4 3.5 %collective-permute-start.1 = (bf16[128,1408]{1,0:T(8,128)(2,1)S(1)}, bf16[128,1408]{1,0:T(8,128)(2,1)S(1)}, u32[]{:S(2)}, u32[]{:S(2)}) collective-permute-start(bf16[128,1408]{1,0:T(8,128)(2,1)S(1)} %bitcast.9), channel_id=1, source_target_pairs={{0,16},{16,32},{32,48},{48,0},{1,17},{17,33},{33,49},{49,1},{2,18}... | collective-permute-start | bytes 1081352 | tf_op jit(solution)/shard_map/ppermute | solution.py:223
  48.9 2.4 %collective-permute-start.4 = (bf16[128,1408]{1,0:T(8,128)(2,1)S(1)}, bf16[128,1408]{1,0:T(8,128)(2,1)S(1)}, u32[]{:S(2)}, u32[]{:S(2)}) collective-permute-start(bf16[128,1408]{1,0:T(8,128)(2,1)S(1)} %bitcast.10), channel_id=1, source_target_pairs={{0,1},{1,0},{2,3},{3,2},{4,5},{5,4},{6,7},{7,6},{8,9},{9,8},{10,11... | collective-permute-start | bytes 1081352 | tf_op jit(solution)/shard_map/ppermute | solution.py:222
  51.3 3.6 %collective-permute-start.2 = (bf16[128,1408]{1,0:T(8,128)(2,1)S(1)}, bf16[128,1408]{1,0:T(8,128)(2,1)S(1)}, u32[]{:S(2)}, u32[]{:S(2)}) collective-permute-start(bf16[128,1408]{1,0:T(8,128)(2,1)S(1)} %bitcast.11), channel_id=1, source_target_pairs={{16,0},{32,16},{48,32},{0,48},{17,1},{33,17},{49,33},{1,49},{18,2}... | collective-permute-start | bytes 1081352 | tf_op jit(solution)/shard_map/ppermute | solution.py:224
  54.8 1.1 collective-permute-done.1
  55.9 2.3 %collective-permute-start.3 = (bf16[128,1408]{1,0:T(8,128)(2,1)S(1)}, bf16[128,1408]{1,0:T(8,128)(2,1)S(1)}, u32[]{:S(2)}, u32[]{:S(2)}) collective-permute-start(bf16[128,1408]{1,0:T(8,128)(2,1)S(1)} %collective-permute-done.1), channel_id=1, source_target_pairs={{0,16},{16,32},{32,48},{48,0},{1,17},{17,33},{33,49},{49,1},{2,18}... | collective-permute-start | bytes 1081352 | tf_op jit(solution)/shard_map/ppermute | solution.py:227
  58.2 0.0 collective-permute-done.4
  58.2 4.8 %collective-permute-start.6 = (bf16[128,1408]{1,0:T(8,128)(2,1)S(1)}, bf16[128,1408]{1,0:T(8,128)(2,1)S(1)}, u32[]{:S(2)}, u32[]{:S(2)}) collective-permute-start(bf16[128,1408]{1,0:T(8,128)(2,1)S(1)} %collective-permute-done.4), channel_id=1, source_target_pairs={{16,0},{32,16},{48,32},{0,48},{17,1},{33,17},{49,33},{1,49},{18,2}... | collective-permute-start | bytes 1081352 | tf_op jit(solution)/shard_map/ppermute | solution.py:226
  63.0 1.9 %collective-permute-start.5 = (bf16[128,1408]{1,0:T(8,128)(2,1)S(1)}, bf16[128,1408]{1,0:T(8,128)(2,1)S(1)}, u32[]{:S(2)}, u32[]{:S(2)}) collective-permute-start(bf16[128,1408]{1,0:T(8,128)(2,1)S(1)} %collective-permute-done.4), channel_id=1, source_target_pairs={{0,16},{16,32},{32,48},{48,0},{1,17},{17,33},{33,49},{49,1},{2,18}... | collective-permute-start | bytes 1081352 | tf_op jit(solution)/shard_map/ppermute | solution.py:225
  64.9 0.0 collective-permute-done.2
  65.0 3.1 %collective-permute-done.3 = bf16[128,1408]{1,0:T(8,128)(2,1)S(1)} collective-permute-done((bf16[128,1408]{1,0:T(8,128)(2,1)S(1)}, bf16[128,1408]{1,0:T(8,128)(2,1)S(1)}, u32[]{:S(2)}, u32[]{:S(2)}) %collective-permute-start.3) | collective-permute-done | bytes 360480 | tf_op jit(solution)/shard_map/ppermute | solution.py:227
  68.0 0.1 pad_maximum_fusion.one_ref.mine_ref
  68.1 1.9 %collective-permute-start.8 = (bf16[512,1408]{1,0:T(8,128)(2,1)S(1)}, bf16[512,1408]{1,0:T(8,128)(2,1)S(1)}, u32[]{:S(2)}, u32[]{:S(2)}) collective-permute-start(bf16[512,1408]{1,0:T(8,128)(2,1)S(1)} %pad_maximum_fusion.one_ref.mine_ref), channel_id=1, source_target_pairs={{0,64},{64,0},{1,65},{65,1},{2,66},{66,2},{3,67},{67,3},{4,68},{68... | collective-permute-start | bytes 4325384 | tf_op jit(solution)/shard_map/ppermute | solution.py:230
  70.1 0.0 collective-permute-done.6
  70.1 3.9 %collective-permute-start.7 = (bf16[128,1408]{1,0:T(8,128)(2,1)S(1)}, bf16[128,1408]{1,0:T(8,128)(2,1)S(1)}, u32[]{:S(2)}, u32[]{:S(2)}) collective-permute-start(bf16[128,1408]{1,0:T(8,128)(2,1)S(1)} %collective-permute-done.6), channel_id=1, source_target_pairs={{16,0},{32,16},{48,32},{0,48},{17,1},{33,17},{49,33},{1,49},{18,2}... | collective-permute-start | bytes 1081352 | tf_op jit(solution)/shard_map/ppermute | solution.py:228
  74.0 0.2 collective-permute-done.5
  74.2 8.5 %collective-permute-done.7 = bf16[128,1408]{1,0:T(8,128)(2,1)S(1)} collective-permute-done((bf16[128,1408]{1,0:T(8,128)(2,1)S(1)}, bf16[128,1408]{1,0:T(8,128)(2,1)S(1)}, u32[]{:S(2)}, u32[]{:S(2)}) %collective-permute-start.7) | collective-permute-done | bytes 360480 | tf_op jit(solution)/shard_map/ppermute | solution.py:228
  82.8 1.9 %collective-permute-start.9 = (bf16[512,1408]{1,0:T(8,128)(2,1)S(1)}, bf16[512,1408]{1,0:T(8,128)(2,1)S(1)}, u32[]{:S(2)}, u32[]{:S(2)}) collective-permute-start(bf16[512,1408]{1,0:T(8,128)(2,1)S(1)} %constant_dynamic-update-slice_fusion.other_ref), channel_id=1, source_target_pairs={{0,64},{64,0},{1,65},{65,1},{2,66},{66,2},{3,67},{67,3},{4,68},{68... | collective-permute-start | bytes 4325384 | tf_op jit(solution)/shard_map/ppermute | solution.py:232
  84.7 0.0 collective-permute-done.8.two_ref.mine2_ref
  84.8 3.0 %gram_part.1.part_ref = f32[1408,1408]{1,0:T(8,128)S(1)} custom-call(bf16[512,1408]{1,0:T(8,128)(2,1)S(1)} %pad_maximum_fusion.one_ref.mine_ref, bf16[512,1408]{1,0:T(8,128)(2,1)S(1)} %collective-permute-done.8.two_ref.mine2_ref), custom_call_target="tpu_custom_call" | custom-call | flops 2030043136 | tf_op jit(solution)/shard_map/gram_part/pallas_call | solution.py:74
  87.7 0.0 copy-start
  87.8 0.2 collective-permute-done.9.other2_ref
  87.9 11.6 %products.1 = bf16[16,8,1536]{2,1,0:T(8,128)(2,1)S(1)} custom-call(bf16[512,1408]{1,0:T(8,128)(2,1)S(1)} %pad_maximum_fusion.one_ref.mine_ref, bf16[512,1408]{1,0:T(8,128)(2,1)S(1)} %constant_dynamic-update-slice_fusion.other_ref, bf16[512,1408]{1,0:T(8,128)(2,1)S(1)} %collective-permute-done.8.two_ref.mine2_ref, ...), custom_call_target="tpu_custom_call" | custom-call | flops 12180258816 | tf_op jit(solution)/shard_map/products/pallas_call | solution.py:153
  99.5 34.8 %all_to_all.11 = bf16[16,8,1536]{2,1,0:T(8,128)(2,1)S(1)} all-to-all(bf16[16,8,1536]{2,1,0:T(8,128)(2,1)S(1)} %products.1), channel_id=1, replica_groups=mesh['x'=4,'core'=2,'y'=4,'z'=16] {'z'}, dimensions={0} | all-to-all | bytes 786432 | tf_op jit(solution)/shard_map/all_to_all | solution.py:235
  134.3 1.9 %collective-permute-start.10 = (bf16[2,4,16,1536]{3,2,1,0:T(8,128)(2,1)S(1)}, bf16[2,4,16,1536]{3,2,1,0:T(8,128)(2,1)S(1)}, u32[]{:S(2)}, u32[]{:S(2)}) collective-permute-start(bf16[2,4,16,1536]{3,2,1,0:T(8,128)(2,1)S(1)} %bitcast.6), channel_id=1, source_target_pairs={{0,64},{64,0},{1,65},{65,1},{2,66},{66,2},{3,67},{67,3},{4,68},{68... | collective-permute-start | bytes 1179656 | tf_op jit(solution)/shard_map/ppermute | solution.py:237
  136.3 1.7 %collective-permute-done.10.far_ref = bf16[2,4,16,1536]{3,2,1,0:T(8,128)(2,1)S(1)} collective-permute-done((bf16[2,4,16,1536]{3,2,1,0:T(8,128)(2,1)S(1)}, bf16[2,4,16,1536]{3,2,1,0:T(8,128)(2,1)S(1)}, u32[]{:S(2)}, u32[]{:S(2)}) %collective-permute-start.10) | collective-permute-done | bytes 393248 | tf_op jit(solution)/shard_map/ppermute | solution.py:237
  137.9 0.0 copy-done
  137.9 1.5 %regroup.1 = (bf16[4,32,1408]{2,1,0:T(8,128)(2,1)}, f32[1,88]{1,0:T(1,128)}) custom-call(s32[4]{0:T(128)S(1)} %bitcast.8, bf16[2,4,16,1536]{3,2,1,0:T(8,128)(2,1)S(1)} %bitcast.7, bf16[2,4,16,1536]{3,2,1,0:T(8,128)(2,1)S(1)} %collective-permute-done.10.far_ref), custom_call_target="tpu_custom_call" | custom-call | tf_op jit(solution)/shard_map/regroup/pallas_call | solution.py:196
  (4 shorter events, 0.1 us)
Async XLA Ops:
  3.0 3.5 %collective-permute-start = (bf16[4,16,1408]{2,1,0:T(8,128)(2,1)}, bf16[4,16,1408]{2,1,0:T(8,128)(2,1)S(1)}, u32[]{:S(2)}, u32[]{:S(2)}) collective-permute-start(bf16[4,16,1408]{2,1,0:T(8,128)(2,1)} %get-tuple-element.10), channel_id=1, source_target_pairs={{0,64},{64,0},{1,65},{65,1},{2,66},{66,2},{3,67},{67,3},{4,68},{68... | collective-permute-start | bytes 540680 | tf_op jit(solution)/shard_map/ppermute | solution.py:217
  45.4 10.5 %collective-permute-start.1 = (bf16[128,1408]{1,0:T(8,128)(2,1)S(1)}, bf16[128,1408]{1,0:T(8,128)(2,1)S(1)}, u32[]{:S(2)}, u32[]{:S(2)}) collective-permute-start(bf16[128,1408]{1,0:T(8,128)(2,1)S(1)} %bitcast.9), channel_id=1, source_target_pairs={{0,16},{16,32},{32,48},{48,0},{1,17},{17,33},{33,49},{49,1},{2,18}... | collective-permute-start | bytes 1081352 | tf_op jit(solution)/shard_map/ppermute | solution.py:223
  48.9 9.3 %collective-permute-start.4 = (bf16[128,1408]{1,0:T(8,128)(2,1)S(1)}, bf16[128,1408]{1,0:T(8,128)(2,1)S(1)}, u32[]{:S(2)}, u32[]{:S(2)}) collective-permute-start(bf16[128,1408]{1,0:T(8,128)(2,1)S(1)} %bitcast.10), channel_id=1, source_target_pairs={{0,1},{1,0},{2,3},{3,2},{4,5},{5,4},{6,7},{7,6},{8,9},{9,8},{10,11... | collective-permute-start | bytes 1081352 | tf_op jit(solution)/shard_map/ppermute | solution.py:222
  51.3 13.7 %collective-permute-start.2 = (bf16[128,1408]{1,0:T(8,128)(2,1)S(1)}, bf16[128,1408]{1,0:T(8,128)(2,1)S(1)}, u32[]{:S(2)}, u32[]{:S(2)}) collective-permute-start(bf16[128,1408]{1,0:T(8,128)(2,1)S(1)} %bitcast.11), channel_id=1, source_target_pairs={{16,0},{32,16},{48,32},{0,48},{17,1},{33,17},{49,33},{1,49},{18,2}... | collective-permute-start | bytes 1081352 | tf_op jit(solution)/shard_map/ppermute | solution.py:224
  55.9 12.1 %collective-permute-start.3 = (bf16[128,1408]{1,0:T(8,128)(2,1)S(1)}, bf16[128,1408]{1,0:T(8,128)(2,1)S(1)}, u32[]{:S(2)}, u32[]{:S(2)}) collective-permute-start(bf16[128,1408]{1,0:T(8,128)(2,1)S(1)} %collective-permute-done.1), channel_id=1, source_target_pairs={{0,16},{16,32},{32,48},{48,0},{1,17},{17,33},{33,49},{49,1},{2,18}... | collective-permute-start | bytes 1081352 | tf_op jit(solution)/shard_map/ppermute | solution.py:227
  58.2 11.9 %collective-permute-start.6 = (bf16[128,1408]{1,0:T(8,128)(2,1)S(1)}, bf16[128,1408]{1,0:T(8,128)(2,1)S(1)}, u32[]{:S(2)}, u32[]{:S(2)}) collective-permute-start(bf16[128,1408]{1,0:T(8,128)(2,1)S(1)} %collective-permute-done.4), channel_id=1, source_target_pairs={{16,0},{32,16},{48,32},{0,48},{17,1},{33,17},{49,33},{1,49},{18,2}... | collective-permute-start | bytes 1081352 | tf_op jit(solution)/shard_map/ppermute | solution.py:226
  63.0 11.2 %collective-permute-start.5 = (bf16[128,1408]{1,0:T(8,128)(2,1)S(1)}, bf16[128,1408]{1,0:T(8,128)(2,1)S(1)}, u32[]{:S(2)}, u32[]{:S(2)}) collective-permute-start(bf16[128,1408]{1,0:T(8,128)(2,1)S(1)} %collective-permute-done.4), channel_id=1, source_target_pairs={{0,16},{16,32},{32,48},{48,0},{1,17},{17,33},{33,49},{49,1},{2,18}... | collective-permute-start | bytes 1081352 | tf_op jit(solution)/shard_map/ppermute | solution.py:225
  68.1 16.6 %collective-permute-start.8 = (bf16[512,1408]{1,0:T(8,128)(2,1)S(1)}, bf16[512,1408]{1,0:T(8,128)(2,1)S(1)}, u32[]{:S(2)}, u32[]{:S(2)}) collective-permute-start(bf16[512,1408]{1,0:T(8,128)(2,1)S(1)} %pad_maximum_fusion.one_ref.mine_ref), channel_id=1, source_target_pairs={{0,64},{64,0},{1,65},{65,1},{2,66},{66,2},{3,67},{67,3},{4,68},{68... | collective-permute-start | bytes 4325384 | tf_op jit(solution)/shard_map/ppermute | solution.py:230
  70.1 12.7 %collective-permute-start.7 = (bf16[128,1408]{1,0:T(8,128)(2,1)S(1)}, bf16[128,1408]{1,0:T(8,128)(2,1)S(1)}, u32[]{:S(2)}, u32[]{:S(2)}) collective-permute-start(bf16[128,1408]{1,0:T(8,128)(2,1)S(1)} %collective-permute-done.6), channel_id=1, source_target_pairs={{16,0},{32,16},{48,32},{0,48},{17,1},{33,17},{49,33},{1,49},{18,2}... | collective-permute-start | bytes 1081352 | tf_op jit(solution)/shard_map/ppermute | solution.py:228
  82.8 5.1 %collective-permute-start.9 = (bf16[512,1408]{1,0:T(8,128)(2,1)S(1)}, bf16[512,1408]{1,0:T(8,128)(2,1)S(1)}, u32[]{:S(2)}, u32[]{:S(2)}) collective-permute-start(bf16[512,1408]{1,0:T(8,128)(2,1)S(1)} %constant_dynamic-update-slice_fusion.other_ref), channel_id=1, source_target_pairs={{0,64},{64,0},{1,65},{65,1},{2,66},{66,2},{3,67},{67,3},{4,68},{68... | collective-permute-start | bytes 4325384 | tf_op jit(solution)/shard_map/ppermute | solution.py:232
  87.7 50.2 %copy-start = (s32[1,4]{1,0:T(1,128)S(1)}, s32[1,4]{1,0:T(1,128)}, u32[]{:S(2)}) copy-start(s32[1,4]{1,0:T(1,128)} %param.5) | copy-start | bytes 52
  134.3 3.6 %collective-permute-start.10 = (bf16[2,4,16,1536]{3,2,1,0:T(8,128)(2,1)S(1)}, bf16[2,4,16,1536]{3,2,1,0:T(8,128)(2,1)S(1)}, u32[]{:S(2)}, u32[]{:S(2)}) collective-permute-start(bf16[2,4,16,1536]{3,2,1,0:T(8,128)(2,1)S(1)} %bitcast.6), channel_id=1, source_target_pairs={{0,64},{64,0},{1,65},{65,1},{2,66},{66,2},{3,67},{67,3},{4,68},{68... | collective-permute-start | bytes 1179656 | tf_op jit(solution)/shard_map/ppermute | solution.py:237

commit v8 on v7

--- a/solution.py
+++ b/solution.py
@@ -62,18 +62,25 @@
     )
 
 
-def gram_part_kernel(one_ref, two_ref, part_ref):
-    for at, size in strips(one_ref.shape[1]):
-        total = gram_strip(one_ref, at, size) + gram_strip(two_ref, at, size)
-        part_ref[at : at + size, at:] = total
-
-
-def gram_part(one, two):
-    rows, columns = one.shape
+def gram_sum(refs, at, size):
+    total = gram_strip(refs[0], at, size)
+    for ref in refs[1:]:
+        total = total + gram_strip(ref, at, size)
+    return total
+
+
+def gram_part_kernel(*refs):
+    part_ref = refs[-1]
+    for at, size in strips(part_ref.shape[1]):
+        part_ref[at : at + size, at:] = gram_sum(refs[:-1], at, size)
+
+
+def gram_part(*blocks):
+    rows, columns = sum(block.shape[0] for block in blocks), blocks[0].shape[1]
     vmem = pl.BlockSpec(memory_space=pltpu.VMEM)
     return pl.pallas_call(
         gram_part_kernel,
-        in_specs=[vmem, vmem],
+        in_specs=[vmem] * len(blocks),
         out_specs=vmem,
         out_shape=jax.ShapeDtypeStruct((columns, columns), F32),
         compiler_params=pltpu.CompilerParams(vmem_limit_bytes=24 * 1024 * 1024),
@@ -81,7 +88,7 @@
             flops=2 * rows * columns * columns, bytes_accessed=0, transcendentals=0
         ),
         name="gram_part",
-    )(one, two)
+    )(*blocks)
 
 
 def times(block, matrix):
@@ -96,17 +103,16 @@
         ].T
 
 
-def products_kernel(
-    mine_ref, other_ref, mine2_ref, other2_ref, part_ref, slots_ref, gram_ref, poly_ref
-):
+def products_kernel(mine_ref, part_ref, *refs):
+    slots_ref, gram_ref, poly_ref = refs[-3:]
     core, b = lax.axis_index("core"), lax.axis_index("z") % 2
-    section_rows, columns = mine_ref.shape
-    total_rows = 4 * section_rows
+    columns = mine_ref.shape[1]
+    own_rows = slots_ref.shape[0] * slots_ref.shape[1]
+    total_rows = 16 * own_rows
     cuts = strips(columns)
     squares = jnp.zeros((1, 1), F32)
     for index, (at, size) in enumerate(cuts):
-        piece = part_ref[at : at + size, at:]
-        piece = piece + gram_strip(other_ref, at, size) + gram_strip(other2_ref, at, size)
+        piece = part_ref[at : at + size, at:] + gram_sum(refs[:-3], at, size)
         row = lax.broadcasted_iota(jnp.int32, (size, size), 0)
         column = lax.broadcasted_iota(jnp.int32, (size, size), 1)
         diagonal = jnp.where(row == column, piece[:, :size], 0.0)
@@ -121,7 +127,7 @@
         poly = scale_squared * (COEF_B * rows[:, at:].astype(F32) + COEF_C * square)
         poly_ref[at : at + size, at:] = poly.astype(BF16)
         mirror(poly_ref, cuts, index)
-    own = mine_ref[: total_rows // 16, :]
+    own = mine_ref[:own_rows, :]
     ortho = COEF_A * own.astype(F32) + times(own, poly_ref[...])
     update = (math.sqrt(total_rows) * scale) * ortho
     slots_ref[:, :, :columns] = update.reshape(16, -1, columns).astype(BF16)
@@ -147,21 +153,21 @@
     slots_ref[:, :, columns:] = jnp.broadcast_to(extra[None], (16, 8, LANES)).astype(BF16)
 
 
-def products(sections, part):
-    rows, columns = sections[0].shape
+def products(mine, part, *blocks):
+    columns = mine.shape[1]
     vmem = pl.BlockSpec(memory_space=pltpu.VMEM)
     return pl.pallas_call(
         products_kernel,
-        in_specs=[vmem] * 5,
+        in_specs=[vmem] * (2 + len(blocks)),
         out_specs=vmem,
         out_shape=jax.ShapeDtypeStruct((16, 8, columns + LANES), BF16),
         scratch_shapes=[pltpu.VMEM((columns, columns), BF16)] * 2,
         compiler_params=pltpu.CompilerParams(vmem_limit_bytes=VMEM_LIMIT),
         cost_estimate=pl.CostEstimate(
-            flops=12 * rows * columns * columns, bytes_accessed=0, transcendentals=0
+            flops=12 * 512 * columns * columns, bytes_accessed=0, transcendentals=0
         ),
         name="products",
-    )(*sections, part)
+    )(mine, part, *blocks)
 
 
 def regroup_kernel(owner_ref, near_ref, far_ref, update_ref, norms_ref):
@@ -206,6 +212,11 @@
     )(owner, near, far)
 
 
+def move(name, block, axis, pairs):
+    with jax.named_scope(name):
+        return lax.ppermute(block, axis, pairs)
+
+
 def on_device(grad, momentum, owner):
     matrices, rows, columns = grad.shape
     core = lax.axis_index("core")
@@ -219,19 +230,23 @@
     mine = lax.all_to_all(
         halves.reshape(16, rows // 4, columns), "z", split_axis=0, concat_axis=0, tiled=True
     ).reshape(-1, columns)
-    other = lax.ppermute(mine, "z", [(i, i ^ 1) for i in range(16)])
-    mine_left = lax.ppermute(mine, "y", up)
-    mine_right = lax.ppermute(mine, "y", down)
-    other_left = lax.ppermute(other, "y", up)
-    other_right = lax.ppermute(other, "y", down)
-    mine_far = lax.ppermute(mine_left, "y", up)
-    other_far = lax.ppermute(other_right, "y", down)
-    mine = jnp.concatenate([mine, mine_left, mine_right, mine_far], axis=0)
-    mine_swapped = lax.ppermute(mine, "core", swap)
-    other = jnp.concatenate([other, other_left, other_right, other_far], axis=0)
-    other_swapped = lax.ppermute(other, "core", swap)
-    part = gram_part(mine, mine_swapped)
-    slots = products([mine, other, mine_swapped, other_swapped], part)
+    other = move("pair", mine, "z", [(i, i ^ 1) for i in range(16)])
+    mine_left = move("mine_left", mine, "y", up)
+    mine_right = move("mine_right", mine, "y", down)
+    other_left = move("other_left", other, "y", up)
+    other_right = move("other_right", other, "y", down)
+    mine_far = move("mine_far", mine_left, "y", up)
+    other_far = move("other_far", other_right, "y", down)
+    first = jnp.concatenate([mine, mine_left], axis=0)
+    second = jnp.concatenate([mine_right, mine_far], axis=0)
+    third = jnp.concatenate([other, other_left], axis=0)
+    part = gram_part(first, second, third, other_right)
+    blocks = [first, second, third]
+    for at, block in enumerate(blocks):
+        held, part = lax.optimization_barrier((block, part))
+        blocks[at] = move("swap", held, "core", swap)
+    last = move("swap_last", jnp.concatenate([other_right, other_far], axis=0), "core", swap)
+    slots = products(first, part, other_far, *blocks, last)
     near = lax.all_to_all(slots, "z", split_axis=0, concat_axis=0, tiled=True)
     near = near.reshape(2, matrices, rows // 2, columns + LANES)
     far = lax.ppermute(near, "core", swap)

time: 141 us -> 145 us (1.028)
  starting transfers between devices: 29.9 us -> 36.2 us
  waiting for transfers between devices: 16.3 us -> 13.1 us
    ppermute x9 -> x11, starting transfers between devices: 26.1 us -> 32.4 us  [move(): return lax.ppermute(block, axis, pairs)]
    ppermute x9 -> x11, waiting for transfers between devices: 13.1 us -> 9.87 us  [move(): return lax.ppermute(block, axis, pairs)]
  transfers between devices with their start and end apart: 11 -> 13, of which waited for: 7 -> 6; matrix products, arithmetic and copies ran while one was open for 0% -> 0% of each run, Pallas kernels for 2% -> 2%
where the time goes in v8:
time: 145 us; the launch traced here: 144 us
  blocking collectives  73.6 us (51%)
  starting transfers between devices  36.2 us (25%)
  Pallas kernels  19 us (13%)
  waiting for transfers between devices  13.1 us (9%)
    all_to_all x1, blocking collectives, on_device(): lax.all_to_all(halves.reshape(16, rows // 4, columns), 'z', split_axis=0,...  38.2 us
    all_to_all x1, blocking collectives, on_device(): near = lax.all_to_all(slots, 'z', split_axis=0, concat_axis=0, tiled=True)  35.4 us
    ppermute x11, starting transfers between devices, move(): return lax.ppermute(block, axis, pairs)  32.4 us
    pallas_call x1, Pallas kernels, products(): pl.pallas_call(products_kernel, in_specs=[vmem] * (2 + len(blocks)), out_...  12.3 us
    ppermute x11, waiting for transfers between devices, move(): return lax.ppermute(block, axis, pairs)  9.87 us
  transfers between devices with their start and end apart: 13, of which 6 were waited for; matrix products, arithmetic and copies ran while one was open for 0% of the time, Pallas kernels for 2%

profile of v8, /device:TPU:6, one launch (start us, length us, event | category | flops | bytes accessed | tf_op | source)
XLA Modules:
  0.0 143.7 jit_solution(12847282316164924506)
XLA Ops:
  0.6 2.4 %momentum_step.1 = (f32[4,32,1408]{2,1,0:T(8,128)}, bf16[2,4,16,1408]{3,2,1,0:T(8,128)(2,1)}, bf16[4,16,1408]{2,1,0:T(8,128)(2,1)}) custom-call(bf16[4,32,1408]{2,1,0:T(8,128)(2,1)} %grad_ref.1, f32[4,32,1408]{2,1,0:T(8,128)} %momentum_ref.1), custom_call_target="tpu_custom_call" | custom-call | tf_op jit(solution)/shard_map/momentum_step/pallas_call | solution.py:38
  3.0 1.9 %collective-permute-start = (bf16[4,16,1408]{2,1,0:T(8,128)(2,1)}, bf16[4,16,1408]{2,1,0:T(8,128)(2,1)S(1)}, u32[]{:S(2)}, u32[]{:S(2)}) collective-permute-start(bf16[4,16,1408]{2,1,0:T(8,128)(2,1)} %get-tuple-element.16), channel_id=1, source_target_pairs={{0,64},{64,0},{1,65},{65,1},{2,66},{66,2},{3,67},{67,3},{4,68},{68... | collective-permute-start | bytes 540680 | tf_op jit(solution)/shard_map/ppermute | solution.py:228
  4.9 1.6 %collective-permute-done = bf16[4,16,1408]{2,1,0:T(8,128)(2,1)S(1)} collective-permute-done((bf16[4,16,1408]{2,1,0:T(8,128)(2,1)}, bf16[4,16,1408]{2,1,0:T(8,128)(2,1)S(1)}, u32[]{:S(2)}, u32[]{:S(2)}) %collective-permute-start) | collective-permute-done | bytes 180256 | tf_op jit(solution)/shard_map/ppermute | solution.py:228
  6.5 0.7 bitcast_dynamic-update-slice_fusion
  7.2 38.2 %all_to_all.10 = bf16[16,8,1408]{2,1,0:T(8,128)(2,1)S(1)} all-to-all(bf16[16,8,1408]{2,1,0:T(8,128)(2,1)} %bitcast.13), channel_id=1, replica_groups=mesh['x'=4,'core'=2,'y'=4,'z'=16] {'z'}, dimensions={0} | all-to-all | bytes 720896 | tf_op jit(solution)/shard_map/all_to_all | solution.py:230
  45.4 2.4 %collective-permute-start.2 = (bf16[128,1408]{1,0:T(8,128)(2,1)S(1)}, bf16[128,1408]{1,0:T(8,128)(2,1)S(1)}, u32[]{:S(2)}, u32[]{:S(2)}) collective-permute-start(bf16[128,1408]{1,0:T(8,128)(2,1)S(1)} %bitcast.9), channel_id=1, source_target_pairs={{0,1},{1,0},{2,3},{3,2},{4,5},{5,4},{6,7},{7,6},{8,9},{9,8},{10,11... | collective-permute-start | bytes 1081352 | tf_op jit(solution)/shard_map/pair/ppermute | solution.py:217
  47.8 3.5 %collective-permute-start.1 = (bf16[128,1408]{1,0:T(8,128)(2,1)S(1)}, bf16[128,1408]{1,0:T(8,128)(2,1)S(1)}, u32[]{:S(2)}, u32[]{:S(2)}) collective-permute-start(bf16[128,1408]{1,0:T(8,128)(2,1)S(1)} %bitcast.10), channel_id=1, source_target_pairs={{0,16},{16,32},{32,48},{48,0},{1,17},{17,33},{33,49},{49,1},{2,18}... | collective-permute-start | bytes 1081352 | tf_op jit(solution)/shard_map/mine_left/ppermute | solution.py:217
  51.3 3.6 %collective-permute-start.4 = (bf16[128,1408]{1,0:T(8,128)(2,1)S(1)}, bf16[128,1408]{1,0:T(8,128)(2,1)S(1)}, u32[]{:S(2)}, u32[]{:S(2)}) collective-permute-start(bf16[128,1408]{1,0:T(8,128)(2,1)S(1)} %bitcast.11), channel_id=1, source_target_pairs={{16,0},{32,16},{48,32},{0,48},{17,1},{33,17},{49,33},{1,49},{18,2}... | collective-permute-start | bytes 1081352 | tf_op jit(solution)/shard_map/mine_right/ppermute | solution.py:217
  54.9 0.0 collective-permute-done.2
  54.9 4.9 %collective-permute-start.6 = (bf16[128,1408]{1,0:T(8,128)(2,1)S(1)}, bf16[128,1408]{1,0:T(8,128)(2,1)S(1)}, u32[]{:S(2)}, u32[]{:S(2)}) collective-permute-start(bf16[128,1408]{1,0:T(8,128)(2,1)S(1)} %collective-permute-done.2), channel_id=1, source_target_pairs={{16,0},{32,16},{48,32},{0,48},{17,1},{33,17},{49,33},{1,49},{18,2}... | collective-permute-start | bytes 1081352 | tf_op jit(solution)/shard_map/other_right/ppermute | solution.py:217
  59.7 1.9 %collective-permute-start.3 = (bf16[128,1408]{1,0:T(8,128)(2,1)S(1)}, bf16[128,1408]{1,0:T(8,128)(2,1)S(1)}, u32[]{:S(2)}, u32[]{:S(2)}) collective-permute-start(bf16[128,1408]{1,0:T(8,128)(2,1)S(1)} %collective-permute-done.2), channel_id=1, source_target_pairs={{0,16},{16,32},{32,48},{48,0},{1,17},{17,33},{33,49},{49,1},{2,18}... | collective-permute-start | bytes 1081352 | tf_op jit(solution)/shard_map/other_left/ppermute | solution.py:217
  61.7 0.1 pad_maximum_fusion.refs_0_.mine_ref
  61.7 2.5 %collective-permute-start.5 = (bf16[128,1408]{1,0:T(8,128)(2,1)S(1)}, bf16[128,1408]{1,0:T(8,128)(2,1)S(1)}, u32[]{:S(2)}, u32[]{:S(2)}) collective-permute-start(bf16[128,1408]{1,0:T(8,128)(2,1)S(1)} %collective-permute-done.1), channel_id=1, source_target_pairs={{0,16},{16,32},{32,48},{48,0},{1,17},{17,33},{33,49},{49,1},{2,18}... | collective-permute-start | bytes 1081352 | tf_op jit(solution)/shard_map/mine_far/ppermute | solution.py:217
  64.3 0.2 collective-permute-done.4
  64.6 4.6 %collective-permute-done.6.refs_3_ = bf16[128,1408]{1,0:T(8,128)(2,1)S(1)} collective-permute-done((bf16[128,1408]{1,0:T(8,128)(2,1)S(1)}, bf16[128,1408]{1,0:T(8,128)(2,1)S(1)}, u32[]{:S(2)}, u32[]{:S(2)}) %collective-permute-start.6) | collective-permute-done | bytes 360480 | tf_op jit(solution)/shard_map/other_right/ppermute | solution.py:217
  69.1 4.8 %collective-permute-start.7 = (bf16[128,1408]{1,0:T(8,128)(2,1)S(1)}, bf16[128,1408]{1,0:T(8,128)(2,1)S(1)}, u32[]{:S(2)}, u32[]{:S(2)}) collective-permute-start(bf16[128,1408]{1,0:T(8,128)(2,1)S(1)} %collective-permute-done.6.refs_3_), channel_id=1, source_target_pairs={{16,0},{32,16},{48,32},{0,48},{17,1},{33,17},{49,33},{1,49},{18,2}... | collective-permute-start | bytes 1081352 | tf_op jit(solution)/shard_map/other_far/ppermute | solution.py:217
  74.0 3.4 %collective-permute-done.5 = bf16[128,1408]{1,0:T(8,128)(2,1)S(1)} collective-permute-done((bf16[128,1408]{1,0:T(8,128)(2,1)S(1)}, bf16[128,1408]{1,0:T(8,128)(2,1)S(1)}, u32[]{:S(2)}, u32[]{:S(2)}) %collective-permute-start.5) | collective-permute-done | bytes 360480 | tf_op jit(solution)/shard_map/mine_far/ppermute | solution.py:217
  77.5 2.9 %gram_part.1.part_ref = f32[1408,1408]{1,0:T(8,128)S(1)} custom-call(bf16[256,1408]{1,0:T(8,128)(2,1)S(1)} %pad_maximum_fusion.refs_0_.mine_ref, bf16[256,1408]{1,0:T(8,128)(2,1)S(1)} %constant_dynamic-update-slice_fusion.2.refs_1_, bf16[256,1408]{1,0:T(8,128)(2,1)S(1)} %constant_dynamic-update-slice_fusion.refs_2_, ...), custom_call_target="tpu_custom_call" | custom-call | flops 3552575488 | tf_op jit(solution)/shard_map/gram_part/pallas_call | solution.py:81
  80.4 1.9 %collective-permute-start.10 = (bf16[256,1408]{1,0:T(8,128)(2,1)S(1)}, bf16[256,1408]{1,0:T(8,128)(2,1)S(1)}, u32[]{:S(2)}, u32[]{:S(2)}) collective-permute-start(bf16[256,1408]{1,0:T(8,128)(2,1)S(1)} %constant_dynamic-update-slice_fusion.refs_2_), channel_id=1, source_target_pairs={{0,64},{64,0},{1,65},{65,1},{2,66},{66,2},{3,67},{67,3},{4,68},{68... | collective-permute-start | bytes 2162696 | tf_op jit(solution)/shard_map/swap/ppermute | solution.py:217
  82.3 2.4 %collective-permute-start.9 = (bf16[256,1408]{1,0:T(8,128)(2,1)S(1)}, bf16[256,1408]{1,0:T(8,128)(2,1)S(1)}, u32[]{:S(2)}, u32[]{:S(2)}) collective-permute-start(bf16[256,1408]{1,0:T(8,128)(2,1)S(1)} %constant_dynamic-update-slice_fusion.2.refs_1_), channel_id=1, source_target_pairs={{0,64},{64,0},{1,65},{65,1},{2,66},{66,2},{3,67},{67,3},{4,68},{68... | collective-permute-start | bytes 2162696 | tf_op jit(solution)/shard_map/swap/ppermute | solution.py:217
  84.7 1.9 %collective-permute-start.8 = (bf16[256,1408]{1,0:T(8,128)(2,1)S(1)}, bf16[256,1408]{1,0:T(8,128)(2,1)S(1)}, u32[]{:S(2)}, u32[]{:S(2)}) collective-permute-start(bf16[256,1408]{1,0:T(8,128)(2,1)S(1)} %pad_maximum_fusion.refs_0_.mine_ref), channel_id=1, source_target_pairs={{0,64},{64,0},{1,65},{65,1},{2,66},{66,2},{3,67},{67,3},{4,68},{68... | collective-permute-start | bytes 2162696 | tf_op jit(solution)/shard_map/swap/ppermute | solution.py:217
  86.7 0.1 pad_maximum_fusion.1
  86.8 0.0 copy-start
  86.8 2.6 %collective-permute-start.11 = (bf16[256,1408]{1,0:T(8,128)(2,1)S(1)}, bf16[256,1408]{1,0:T(8,128)(2,1)S(1)}, u32[]{:S(2)}, u32[]{:S(2)}) collective-permute-start(bf16[256,1408]{1,0:T(8,128)(2,1)S(1)} %pad_maximum_fusion.1), channel_id=1, source_target_pairs={{0,64},{64,0},{1,65},{65,1},{2,66},{66,2},{3,67},{67,3},{4,68},{68... | collective-permute-start | bytes 2162696 | tf_op jit(solution)/shard_map/swap_last/ppermute | solution.py:217
  89.4 0.0 collective-permute-done.10.refs_3_
  89.4 0.0 collective-permute-done.8.refs_1_
  89.4 1.6 %collective-permute-done.11.refs_4_ = bf16[256,1408]{1,0:T(8,128)(2,1)S(1)} collective-permute-done((bf16[256,1408]{1,0:T(8,128)(2,1)S(1)}, bf16[256,1408]{1,0:T(8,128)(2,1)S(1)}, u32[]{:S(2)}, u32[]{:S(2)}) %collective-permute-start.11) | collective-permute-done | bytes 720928 | tf_op jit(solution)/shard_map/swap_last/ppermute | solution.py:217
  91.0 12.3 %products.1 = bf16[16,8,1536]{2,1,0:T(8,128)(2,1)S(1)} custom-call(bf16[256,1408]{1,0:T(8,128)(2,1)S(1)} %pad_maximum_fusion.refs_0_.mine_ref, f32[1408,1408]{1,0:T(8,128)S(1)} %gram_part.1.part_ref, bf16[128,1408]{1,0:T(8,128)(2,1)S(1)} %collective-permute-done.7.refs_0_, bf16[256,1408]{1,0:T(8,128)(2,1)S(1)} %collective-permute-done.8.refs_1_, ...), custom_call_target="tpu_custom_call" | custom-call | flops 12180258816 | tf_op jit(solution)/shard_map/products/pallas_call | solution.py:159
  103.3 35.4 %all_to_all.11 = bf16[16,8,1536]{2,1,0:T(8,128)(2,1)S(1)} all-to-all(bf16[16,8,1536]{2,1,0:T(8,128)(2,1)S(1)} %products.1), channel_id=1, replica_groups=mesh['x'=4,'core'=2,'y'=4,'z'=16] {'z'}, dimensions={0} | all-to-all | bytes 786432 | tf_op jit(solution)/shard_map/all_to_all | solution.py:250
  138.6 1.9 %collective-permute-start.12 = (bf16[2,4,16,1536]{3,2,1,0:T(8,128)(2,1)S(1)}, bf16[2,4,16,1536]{3,2,1,0:T(8,128)(2,1)S(1)}, u32[]{:S(2)}, u32[]{:S(2)}) collective-permute-start(bf16[2,4,16,1536]{3,2,1,0:T(8,128)(2,1)S(1)} %bitcast.6), channel_id=1, source_target_pairs={{0,64},{64,0},{1,65},{65,1},{2,66},{66,2},{3,67},{67,3},{4,68},{68... | collective-permute-start | bytes 1179656 | tf_op jit(solution)/shard_map/ppermute | solution.py:252
  140.6 1.7 %collective-permute-done.12.far_ref = bf16[2,4,16,1536]{3,2,1,0:T(8,128)(2,1)S(1)} collective-permute-done((bf16[2,4,16,1536]{3,2,1,0:T(8,128)(2,1)S(1)}, bf16[2,4,16,1536]{3,2,1,0:T(8,128)(2,1)S(1)}, u32[]{:S(2)}, u32[]{:S(2)}) %collective-permute-start.12) | collective-permute-done | bytes 393248 | tf_op jit(solution)/shard_map/ppermute | solution.py:252
  142.2 1.5 %regroup.1 = (bf16[4,32,1408]{2,1,0:T(8,128)(2,1)}, f32[1,88]{1,0:T(1,128)}) custom-call(s32[4]{0:T(128)S(1)} %bitcast.8, bf16[2,4,16,1536]{3,2,1,0:T(8,128)(2,1)S(1)} %bitcast.7, bf16[2,4,16,1536]{3,2,1,0:T(8,128)(2,1)S(1)} %collective-permute-done.12.far_ref), custom_call_target="tpu_custom_call" | custom-call | tf_op jit(solution)/shard_map/regroup/pallas_call | solution.py:202
  (9 shorter events, 0.1 us)
Async XLA Ops:
  3.0 3.5 %collective-permute-start = (bf16[4,16,1408]{2,1,0:T(8,128)(2,1)}, bf16[4,16,1408]{2,1,0:T(8,128)(2,1)S(1)}, u32[]{:S(2)}, u32[]{:S(2)}) collective-permute-start(bf16[4,16,1408]{2,1,0:T(8,128)(2,1)} %get-tuple-element.16), channel_id=1, source_target_pairs={{0,64},{64,0},{1,65},{65,1},{2,66},{66,2},{3,67},{67,3},{4,68},{68... | collective-permute-start | bytes 540680 | tf_op jit(solution)/shard_map/ppermute | solution.py:228
  45.4 9.4 %collective-permute-start.2 = (bf16[128,1408]{1,0:T(8,128)(2,1)S(1)}, bf16[128,1408]{1,0:T(8,128)(2,1)S(1)}, u32[]{:S(2)}, u32[]{:S(2)}) collective-permute-start(bf16[128,1408]{1,0:T(8,128)(2,1)S(1)} %bitcast.9), channel_id=1, source_target_pairs={{0,1},{1,0},{2,3},{3,2},{4,5},{5,4},{6,7},{7,6},{8,9},{9,8},{10,11... | collective-permute-start | bytes 1081352 | tf_op jit(solution)/shard_map/pair/ppermute | solution.py:217
  47.8 13.9 %collective-permute-start.1 = (bf16[128,1408]{1,0:T(8,128)(2,1)S(1)}, bf16[128,1408]{1,0:T(8,128)(2,1)S(1)}, u32[]{:S(2)}, u32[]{:S(2)}) collective-permute-start(bf16[128,1408]{1,0:T(8,128)(2,1)S(1)} %bitcast.10), channel_id=1, source_target_pairs={{0,16},{16,32},{32,48},{48,0},{1,17},{17,33},{33,49},{49,1},{2,18}... | collective-permute-start | bytes 1081352 | tf_op jit(solution)/shard_map/mine_left/ppermute | solution.py:217
  51.3 13.2 %collective-permute-start.4 = (bf16[128,1408]{1,0:T(8,128)(2,1)S(1)}, bf16[128,1408]{1,0:T(8,128)(2,1)S(1)}, u32[]{:S(2)}, u32[]{:S(2)}) collective-permute-start(bf16[128,1408]{1,0:T(8,128)(2,1)S(1)} %bitcast.11), channel_id=1, source_target_pairs={{16,0},{32,16},{48,32},{0,48},{17,1},{33,17},{49,33},{1,49},{18,2}... | collective-permute-start | bytes 1081352 | tf_op jit(solution)/shard_map/mine_right/ppermute | solution.py:217
  54.9 14.3 %collective-permute-start.6 = (bf16[128,1408]{1,0:T(8,128)(2,1)S(1)}, bf16[128,1408]{1,0:T(8,128)(2,1)S(1)}, u32[]{:S(2)}, u32[]{:S(2)}) collective-permute-start(bf16[128,1408]{1,0:T(8,128)(2,1)S(1)} %collective-permute-done.2), channel_id=1, source_target_pairs={{16,0},{32,16},{48,32},{0,48},{17,1},{33,17},{49,33},{1,49},{18,2}... | collective-permute-start | bytes 1081352 | tf_op jit(solution)/shard_map/other_right/ppermute | solution.py:217
  59.7 17.7 %collective-permute-start.3 = (bf16[128,1408]{1,0:T(8,128)(2,1)S(1)}, bf16[128,1408]{1,0:T(8,128)(2,1)S(1)}, u32[]{:S(2)}, u32[]{:S(2)}) collective-permute-start(bf16[128,1408]{1,0:T(8,128)(2,1)S(1)} %collective-permute-done.2), channel_id=1, source_target_pairs={{0,16},{16,32},{32,48},{48,0},{1,17},{17,33},{33,49},{49,1},{2,18}... | collective-permute-start | bytes 1081352 | tf_op jit(solution)/shard_map/other_left/ppermute | solution.py:217
  61.7 15.7 %collective-permute-start.5 = (bf16[128,1408]{1,0:T(8,128)(2,1)S(1)}, bf16[128,1408]{1,0:T(8,128)(2,1)S(1)}, u32[]{:S(2)}, u32[]{:S(2)}) collective-permute-start(bf16[128,1408]{1,0:T(8,128)(2,1)S(1)} %collective-permute-done.1), channel_id=1, source_target_pairs={{0,16},{16,32},{32,48},{48,0},{1,17},{17,33},{33,49},{49,1},{2,18}... | collective-permute-start | bytes 1081352 | tf_op jit(solution)/shard_map/mine_far/ppermute | solution.py:217
  69.1 17.5 %collective-permute-start.7 = (bf16[128,1408]{1,0:T(8,128)(2,1)S(1)}, bf16[128,1408]{1,0:T(8,128)(2,1)S(1)}, u32[]{:S(2)}, u32[]{:S(2)}) collective-permute-start(bf16[128,1408]{1,0:T(8,128)(2,1)S(1)} %collective-permute-done.6.refs_3_), channel_id=1, source_target_pairs={{16,0},{32,16},{48,32},{0,48},{17,1},{33,17},{49,33},{1,49},{18,2}... | collective-permute-start | bytes 1081352 | tf_op jit(solution)/shard_map/other_far/ppermute | solution.py:217
  80.4 9.0 %collective-permute-start.10 = (bf16[256,1408]{1,0:T(8,128)(2,1)S(1)}, bf16[256,1408]{1,0:T(8,128)(2,1)S(1)}, u32[]{:S(2)}, u32[]{:S(2)}) collective-permute-start(bf16[256,1408]{1,0:T(8,128)(2,1)S(1)} %constant_dynamic-update-slice_fusion.refs_2_), channel_id=1, source_target_pairs={{0,64},{64,0},{1,65},{65,1},{2,66},{66,2},{3,67},{67,3},{4,68},{68... | collective-permute-start | bytes 2162696 | tf_op jit(solution)/shard_map/swap/ppermute | solution.py:217
  82.3 7.0 %collective-permute-start.9 = (bf16[256,1408]{1,0:T(8,128)(2,1)S(1)}, bf16[256,1408]{1,0:T(8,128)(2,1)S(1)}, u32[]{:S(2)}, u32[]{:S(2)}) collective-permute-start(bf16[256,1408]{1,0:T(8,128)(2,1)S(1)} %constant_dynamic-update-slice_fusion.2.refs_1_), channel_id=1, source_target_pairs={{0,64},{64,0},{1,65},{65,1},{2,66},{66,2},{3,67},{67,3},{4,68},{68... | collective-permute-start | bytes 2162696 | tf_op jit(solution)/shard_map/swap/ppermute | solution.py:217
  84.7 4.6 %collective-permute-start.8 = (bf16[256,1408]{1,0:T(8,128)(2,1)S(1)}, bf16[256,1408]{1,0:T(8,128)(2,1)S(1)}, u32[]{:S(2)}, u32[]{:S(2)}) collective-permute-start(bf16[256,1408]{1,0:T(8,128)(2,1)S(1)} %pad_maximum_fusion.refs_0_.mine_ref), channel_id=1, source_target_pairs={{0,64},{64,0},{1,65},{65,1},{2,66},{66,2},{3,67},{67,3},{4,68},{68... | collective-permute-start | bytes 2162696 | tf_op jit(solution)/shard_map/swap/ppermute | solution.py:217
  86.8 55.5 %copy-start = (s32[1,4]{1,0:T(1,128)S(1)}, s32[1,4]{1,0:T(1,128)}, u32[]{:S(2)}) copy-start(s32[1,4]{1,0:T(1,128)} %param.5) | copy-start | bytes 52
  86.8 4.2 %collective-permute-start.11 = (bf16[256,1408]{1,0:T(8,128)(2,1)S(1)}, bf16[256,1408]{1,0:T(8,128)(2,1)S(1)}, u32[]{:S(2)}, u32[]{:S(2)}) collective-permute-start(bf16[256,1408]{1,0:T(8,128)(2,1)S(1)} %pad_maximum_fusion.1), channel_id=1, source_target_pairs={{0,64},{64,0},{1,65},{65,1},{2,66},{66,2},{3,67},{67,3},{4,68},{68... | collective-permute-start | bytes 2162696 | tf_op jit(solution)/shard_map/swap_last/ppermute | solution.py:217
  138.6 3.6 %collective-permute-start.12 = (bf16[2,4,16,1536]{3,2,1,0:T(8,128)(2,1)S(1)}, bf16[2,4,16,1536]{3,2,1,0:T(8,128)(2,1)S(1)}, u32[]{:S(2)}, u32[]{:S(2)}) collective-permute-start(bf16[2,4,16,1536]{3,2,1,0:T(8,128)(2,1)S(1)} %bitcast.6), channel_id=1, source_target_pairs={{0,64},{64,0},{1,65},{65,1},{2,66},{66,2},{3,67},{67,3},{4,68},{68... | collective-permute-start | bytes 1179656 | tf_op jit(solution)/shard_map/ppermute | solution.py:252

commit v9 on v8

--- a/solution.py
+++ b/solution.py
@@ -222,6 +222,7 @@
     core = lax.axis_index("core")
     up = [(i, (i + 1) % 4) for i in range(4)]
     down = [((i + 1) % 4, i) for i in range(4)]
+    pairs = [(i, i ^ 1) for i in range(16)]
     swap = [(0, 1), (1, 0)]
 
     new_momentum, halves, send = momentum_step(grad, momentum)
@@ -230,23 +231,19 @@
     mine = lax.all_to_all(
         halves.reshape(16, rows // 4, columns), "z", split_axis=0, concat_axis=0, tiled=True
     ).reshape(-1, columns)
-    other = move("pair", mine, "z", [(i, i ^ 1) for i in range(16)])
+    other = move("pair", mine, "z", pairs)
     mine_left = move("mine_left", mine, "y", up)
     mine_right = move("mine_right", mine, "y", down)
-    other_left = move("other_left", other, "y", up)
+    mine_far = move("mine_far", mine_left, "y", up)
     other_right = move("other_right", other, "y", down)
-    mine_far = move("mine_far", mine_left, "y", up)
-    other_far = move("other_far", other_right, "y", down)
-    first = jnp.concatenate([mine, mine_left], axis=0)
-    second = jnp.concatenate([mine_right, mine_far], axis=0)
-    third = jnp.concatenate([other, other_left], axis=0)
-    part = gram_part(first, second, third, other_right)
-    blocks = [first, second, third]
-    for at, block in enumerate(blocks):
-        held, part = lax.optimization_barrier((block, part))
-        blocks[at] = move("swap", held, "core", swap)
-    last = move("swap_last", jnp.concatenate([other_right, other_far], axis=0), "core", swap)
-    slots = products(first, part, other_far, *blocks, last)
+    other_left = move("pair_left", mine_left, "z", pairs)
+    other_far = move("pair_far", mine_far, "z", pairs)
+    mine = jnp.concatenate([mine, mine_left, mine_right, mine_far], axis=0)
+    mine_swapped = move("swap_mine", mine, "core", swap)
+    other = jnp.concatenate([other, other_left, other_right, other_far], axis=0)
+    other_swapped = move("swap_other", other, "core", swap)
+    part = gram_part(mine, mine_swapped)
+    slots = products(mine, part, other, other_swapped)
     near = lax.all_to_all(slots, "z", split_axis=0, concat_axis=0, tiled=True)
     near = near.reshape(2, matrices, rows // 2, columns + LANES)
     far = lax.ppermute(near, "core", swap)

time: 145 us -> 140 us (0.966)
  starting transfers between devices: 36.2 us -> 31.8 us
    ppermute x11 -> x9, starting transfers between devices: 32.4 us -> 28 us  [move(): return lax.ppermute(block, axis, pairs)]
    ppermute x11 -> x9, waiting for transfers between devices: 9.87 us -> 10.2 us  [move(): return lax.ppermute(block, axis, pairs)]
  transfers between devices with their start and end apart: 13 -> 11, of which waited for: 6 -> 5; matrix products, arithmetic and copies ran while one was open for 0% -> 0% of each run, Pallas kernels for 2% -> 2%
where the time goes in v9:
time: 140 us; the launch traced here: 138 us
  blocking collectives  72.8 us (52%)
  starting transfers between devices  31.8 us (23%)
  Pallas kernels  18.4 us (13%)
  waiting for transfers between devices  13.5 us (10%)
    all_to_all x1, blocking collectives, on_device(): lax.all_to_all(halves.reshape(16, rows // 4, columns), 'z', split_axis=0,...  38.2 us
    all_to_all x1, blocking collectives, on_device(): near = lax.all_to_all(slots, 'z', split_axis=0, concat_axis=0, tiled=True)  34.6 us
    ppermute x9, starting transfers between devices, move(): return lax.ppermute(block, axis, pairs)  28 us
    pallas_call x1, Pallas kernels, products(): pl.pallas_call(products_kernel, in_specs=[vmem] * (2 + len(blocks)), out_...  11.6 us
    ppermute x9, waiting for transfers between devices, move(): return lax.ppermute(block, axis, pairs)  10.2 us
    pallas_call x1, Pallas kernels, gram_part(): pl.pallas_call(gram_part_kernel, in_specs=[vmem] * len(blocks), out_specs...  2.98 us
  transfers between devices with their start and end apart: 11, of which 5 were waited for; matrix products, arithmetic and copies ran while one was open for 0% of the time, Pallas kernels for 2%

profile of v9, /device:TPU:6, one launch (start us, length us, event | category | flops | bytes accessed | tf_op | source)
XLA Modules:
  0.0 138.3 jit_solution(13976771455277995142)
XLA Ops:
  0.6 2.4 %momentum_step.1 = (f32[4,32,1408]{2,1,0:T(8,128)}, bf16[2,4,16,1408]{3,2,1,0:T(8,128)(2,1)}, bf16[4,16,1408]{2,1,0:T(8,128)(2,1)}) custom-call(bf16[4,32,1408]{2,1,0:T(8,128)(2,1)} %grad_ref.1, f32[4,32,1408]{2,1,0:T(8,128)} %momentum_ref.1), custom_call_target="tpu_custom_call" | custom-call | tf_op jit(solution)/shard_map/momentum_step/pallas_call | solution.py:38
  3.0 1.9 %collective-permute-start = (bf16[4,16,1408]{2,1,0:T(8,128)(2,1)}, bf16[4,16,1408]{2,1,0:T(8,128)(2,1)S(1)}, u32[]{:S(2)}, u32[]{:S(2)}) collective-permute-start(bf16[4,16,1408]{2,1,0:T(8,128)(2,1)} %get-tuple-element.10), channel_id=1, source_target_pairs={{0,64},{64,0},{1,65},{65,1},{2,66},{66,2},{3,67},{67,3},{4,68},{68... | collective-permute-start | bytes 540680 | tf_op jit(solution)/shard_map/ppermute | solution.py:229
  4.9 1.6 %collective-permute-done = bf16[4,16,1408]{2,1,0:T(8,128)(2,1)S(1)} collective-permute-done((bf16[4,16,1408]{2,1,0:T(8,128)(2,1)}, bf16[4,16,1408]{2,1,0:T(8,128)(2,1)S(1)}, u32[]{:S(2)}, u32[]{:S(2)}) %collective-permute-start) | collective-permute-done | bytes 180256 | tf_op jit(solution)/shard_map/ppermute | solution.py:229
  6.5 0.7 bitcast_dynamic-update-slice_fusion
  7.2 38.2 %all_to_all.10 = bf16[16,8,1408]{2,1,0:T(8,128)(2,1)S(1)} all-to-all(bf16[16,8,1408]{2,1,0:T(8,128)(2,1)} %bitcast.13), channel_id=1, replica_groups=mesh['x'=4,'core'=2,'y'=4,'z'=16] {'z'}, dimensions={0} | all-to-all | bytes 720896 | tf_op jit(solution)/shard_map/all_to_all | solution.py:231
  45.4 3.5 %collective-permute-start.1 = (bf16[128,1408]{1,0:T(8,128)(2,1)S(1)}, bf16[128,1408]{1,0:T(8,128)(2,1)S(1)}, u32[]{:S(2)}, u32[]{:S(2)}) collective-permute-start(bf16[128,1408]{1,0:T(8,128)(2,1)S(1)} %bitcast.9), channel_id=1, source_target_pairs={{0,16},{16,32},{32,48},{48,0},{1,17},{17,33},{33,49},{49,1},{2,18}... | collective-permute-start | bytes 1081352 | tf_op jit(solution)/shard_map/mine_left/ppermute | solution.py:217
  48.9 2.4 %collective-permute-start.5 = (bf16[128,1408]{1,0:T(8,128)(2,1)S(1)}, bf16[128,1408]{1,0:T(8,128)(2,1)S(1)}, u32[]{:S(2)}, u32[]{:S(2)}) collective-permute-start(bf16[128,1408]{1,0:T(8,128)(2,1)S(1)} %bitcast.10), channel_id=1, source_target_pairs={{0,1},{1,0},{2,3},{3,2},{4,5},{5,4},{6,7},{7,6},{8,9},{9,8},{10,11... | collective-permute-start | bytes 1081352 | tf_op jit(solution)/shard_map/pair/ppermute | solution.py:217
  51.3 3.6 %collective-permute-start.2 = (bf16[128,1408]{1,0:T(8,128)(2,1)S(1)}, bf16[128,1408]{1,0:T(8,128)(2,1)S(1)}, u32[]{:S(2)}, u32[]{:S(2)}) collective-permute-start(bf16[128,1408]{1,0:T(8,128)(2,1)S(1)} %bitcast.11), channel_id=1, source_target_pairs={{16,0},{32,16},{48,32},{0,48},{17,1},{33,17},{49,33},{1,49},{18,2}... | collective-permute-start | bytes 1081352 | tf_op jit(solution)/shard_map/mine_right/ppermute | solution.py:217
  54.8 1.1 collective-permute-done.1
  55.9 2.3 %collective-permute-start.3 = (bf16[128,1408]{1,0:T(8,128)(2,1)S(1)}, bf16[128,1408]{1,0:T(8,128)(2,1)S(1)}, u32[]{:S(2)}, u32[]{:S(2)}) collective-permute-start(bf16[128,1408]{1,0:T(8,128)(2,1)S(1)} %collective-permute-done.1), channel_id=1, source_target_pairs={{0,16},{16,32},{32,48},{48,0},{1,17},{17,33},{33,49},{49,1},{2,18}... | collective-permute-start | bytes 1081352 | tf_op jit(solution)/shard_map/mine_far/ppermute | solution.py:217
  58.2 3.8 %collective-permute-start.6 = (bf16[128,1408]{1,0:T(8,128)(2,1)S(1)}, bf16[128,1408]{1,0:T(8,128)(2,1)S(1)}, u32[]{:S(2)}, u32[]{:S(2)}) collective-permute-start(bf16[128,1408]{1,0:T(8,128)(2,1)S(1)} %collective-permute-done.1), channel_id=1, source_target_pairs={{0,1},{1,0},{2,3},{3,2},{4,5},{5,4},{6,7},{7,6},{8,9},{9,8},{10,11... | collective-permute-start | bytes 1081352 | tf_op jit(solution)/shard_map/pair_left/ppermute | solution.py:217
  61.9 0.0 collective-permute-done.5
  62.0 4.8 %collective-permute-start.7 = (bf16[128,1408]{1,0:T(8,128)(2,1)S(1)}, bf16[128,1408]{1,0:T(8,128)(2,1)S(1)}, u32[]{:S(2)}, u32[]{:S(2)}) collective-permute-start(bf16[128,1408]{1,0:T(8,128)(2,1)S(1)} %collective-permute-done.5), channel_id=1, source_target_pairs={{16,0},{32,16},{48,32},{0,48},{17,1},{33,17},{49,33},{1,49},{18,2}... | collective-permute-start | bytes 1081352 | tf_op jit(solution)/shard_map/other_right/ppermute | solution.py:217
  66.8 0.0 collective-permute-done.2
  66.9 0.0 collective-permute-done.3
  66.9 0.1 pad_maximum_fusion.refs_0_.mine_ref
  67.0 1.9 %collective-permute-start.4 = (bf16[512,1408]{1,0:T(8,128)(2,1)S(1)}, bf16[512,1408]{1,0:T(8,128)(2,1)S(1)}, u32[]{:S(2)}, u32[]{:S(2)}) collective-permute-start(bf16[512,1408]{1,0:T(8,128)(2,1)S(1)} %pad_maximum_fusion.refs_0_.mine_ref), channel_id=1, source_target_pairs={{0,64},{64,0},{1,65},{65,1},{2,66},{66,2},{3,67},{67,3},{4,68},{68... | collective-permute-start | bytes 4325384 | tf_op jit(solution)/shard_map/swap_mine/ppermute | solution.py:217
  68.9 3.9 %collective-permute-start.8 = (bf16[128,1408]{1,0:T(8,128)(2,1)S(1)}, bf16[128,1408]{1,0:T(8,128)(2,1)S(1)}, u32[]{:S(2)}, u32[]{:S(2)}) collective-permute-start(bf16[128,1408]{1,0:T(8,128)(2,1)S(1)} %collective-permute-done.3), channel_id=1, source_target_pairs={{0,1},{1,0},{2,3},{3,2},{4,5},{5,4},{6,7},{7,6},{8,9},{9,8},{10,11... | collective-permute-start | bytes 1081352 | tf_op jit(solution)/shard_map/pair_far/ppermute | solution.py:217
  72.8 0.0 collective-permute-done.6
  72.9 0.0 collective-permute-done.7
  72.9 9.0 %collective-permute-done.8 = bf16[128,1408]{1,0:T(8,128)(2,1)S(1)} collective-permute-done((bf16[128,1408]{1,0:T(8,128)(2,1)S(1)}, bf16[128,1408]{1,0:T(8,128)(2,1)S(1)}, u32[]{:S(2)}, u32[]{:S(2)}) %collective-permute-start.8) | collective-permute-done | bytes 360480 | tf_op jit(solution)/shard_map/pair_far/ppermute | solution.py:217
  81.9 1.9 %collective-permute-start.9 = (bf16[512,1408]{1,0:T(8,128)(2,1)S(1)}, bf16[512,1408]{1,0:T(8,128)(2,1)S(1)}, u32[]{:S(2)}, u32[]{:S(2)}) collective-permute-start(bf16[512,1408]{1,0:T(8,128)(2,1)S(1)} %constant_dynamic-update-slice_fusion.refs_0_), channel_id=1, source_target_pairs={{0,64},{64,0},{1,65},{65,1},{2,66},{66,2},{3,67},{67,3},{4,68},{68... | collective-permute-start | bytes 4325384 | tf_op jit(solution)/shard_map/swap_other/ppermute | solution.py:217
  83.8 0.0 collective-permute-done.4.refs_1_
  83.9 3.0 %gram_part.1.part_ref = f32[1408,1408]{1,0:T(8,128)S(1)} custom-call(bf16[512,1408]{1,0:T(8,128)(2,1)S(1)} %pad_maximum_fusion.refs_0_.mine_ref, bf16[512,1408]{1,0:T(8,128)(2,1)S(1)} %collective-permute-done.4.refs_1_), custom_call_target="tpu_custom_call" | custom-call | flops 4060086272 | tf_op jit(solution)/shard_map/gram_part/pallas_call | solution.py:81
  86.8 0.0 copy-start
  86.9 0.2 collective-permute-done.9.refs_1_
  87.0 11.6 %products.1 = bf16[16,8,1536]{2,1,0:T(8,128)(2,1)S(1)} custom-call(bf16[512,1408]{1,0:T(8,128)(2,1)S(1)} %pad_maximum_fusion.refs_0_.mine_ref, f32[1408,1408]{1,0:T(8,128)S(1)} %gram_part.1.part_ref, bf16[512,1408]{1,0:T(8,128)(2,1)S(1)} %constant_dynamic-update-slice_fusion.refs_0_, bf16[512,1408]{1,0:T(8,128)(2,1)S(1)} %collective-permute-done.9.refs_1_), custom_call_target="tpu_custom_call" | custom-call | flops 12180258816 | tf_op jit(solution)/shard_map/products/pallas_call | solution.py:159
  98.6 34.6 %all_to_all.11 = bf16[16,8,1536]{2,1,0:T(8,128)(2,1)S(1)} all-to-all(bf16[16,8,1536]{2,1,0:T(8,128)(2,1)S(1)} %products.1), channel_id=1, replica_groups=mesh['x'=4,'core'=2,'y'=4,'z'=16] {'z'}, dimensions={0} | all-to-all | bytes 786432 | tf_op jit(solution)/shard_map/all_to_all | solution.py:247
  133.2 1.9 %collective-permute-start.10 = (bf16[2,4,16,1536]{3,2,1,0:T(8,128)(2,1)S(1)}, bf16[2,4,16,1536]{3,2,1,0:T(8,128)(2,1)S(1)}, u32[]{:S(2)}, u32[]{:S(2)}) collective-permute-start(bf16[2,4,16,1536]{3,2,1,0:T(8,128)(2,1)S(1)} %bitcast.6), channel_id=1, source_target_pairs={{0,64},{64,0},{1,65},{65,1},{2,66},{66,2},{3,67},{67,3},{4,68},{68... | collective-permute-start | bytes 1179656 | tf_op jit(solution)/shard_map/ppermute | solution.py:249
  135.1 1.7 %collective-permute-done.10.far_ref = bf16[2,4,16,1536]{3,2,1,0:T(8,128)(2,1)S(1)} collective-permute-done((bf16[2,4,16,1536]{3,2,1,0:T(8,128)(2,1)S(1)}, bf16[2,4,16,1536]{3,2,1,0:T(8,128)(2,1)S(1)}, u32[]{:S(2)}, u32[]{:S(2)}) %collective-permute-start.10) | collective-permute-done | bytes 393248 | tf_op jit(solution)/shard_map/ppermute | solution.py:249
  136.8 0.0 copy-done
  136.8 1.5 %regroup.1 = (bf16[4,32,1408]{2,1,0:T(8,128)(2,1)}, f32[1,88]{1,0:T(1,128)}) custom-call(s32[4]{0:T(128)S(1)} %bitcast.8, bf16[2,4,16,1536]{3,2,1,0:T(8,128)(2,1)S(1)} %bitcast.7, bf16[2,4,16,1536]{3,2,1,0:T(8,128)(2,1)S(1)} %collective-permute-done.10.far_ref), custom_call_target="tpu_custom_call" | custom-call | tf_op jit(solution)/shard_map/regroup/pallas_call | solution.py:202
  (4 shorter events, 0.1 us)
Async XLA Ops:
  3.0 3.5 %collective-permute-start = (bf16[4,16,1408]{2,1,0:T(8,128)(2,1)}, bf16[4,16,1408]{2,1,0:T(8,128)(2,1)S(1)}, u32[]{:S(2)}, u32[]{:S(2)}) collective-permute-start(bf16[4,16,1408]{2,1,0:T(8,128)(2,1)} %get-tuple-element.10), channel_id=1, source_target_pairs={{0,64},{64,0},{1,65},{65,1},{2,66},{66,2},{3,67},{67,3},{4,68},{68... | collective-permute-start | bytes 540680 | tf_op jit(solution)/shard_map/ppermute | solution.py:229
  45.4 10.5 %collective-permute-start.1 = (bf16[128,1408]{1,0:T(8,128)(2,1)S(1)}, bf16[128,1408]{1,0:T(8,128)(2,1)S(1)}, u32[]{:S(2)}, u32[]{:S(2)}) collective-permute-start(bf16[128,1408]{1,0:T(8,128)(2,1)S(1)} %bitcast.9), channel_id=1, source_target_pairs={{0,16},{16,32},{32,48},{48,0},{1,17},{17,33},{33,49},{49,1},{2,18}... | collective-permute-start | bytes 1081352 | tf_op jit(solution)/shard_map/mine_left/ppermute | solution.py:217
  48.9 13.1 %collective-permute-start.5 = (bf16[128,1408]{1,0:T(8,128)(2,1)S(1)}, bf16[128,1408]{1,0:T(8,128)(2,1)S(1)}, u32[]{:S(2)}, u32[]{:S(2)}) collective-permute-start(bf16[128,1408]{1,0:T(8,128)(2,1)S(1)} %bitcast.10), channel_id=1, source_target_pairs={{0,1},{1,0},{2,3},{3,2},{4,5},{5,4},{6,7},{7,6},{8,9},{9,8},{10,11... | collective-permute-start | bytes 1081352 | tf_op jit(solution)/shard_map/pair/ppermute | solution.py:217
  51.3 15.6 %collective-permute-start.2 = (bf16[128,1408]{1,0:T(8,128)(2,1)S(1)}, bf16[128,1408]{1,0:T(8,128)(2,1)S(1)}, u32[]{:S(2)}, u32[]{:S(2)}) collective-permute-start(bf16[128,1408]{1,0:T(8,128)(2,1)S(1)} %bitcast.11), channel_id=1, source_target_pairs={{16,0},{32,16},{48,32},{0,48},{17,1},{33,17},{49,33},{1,49},{18,2}... | collective-permute-start | bytes 1081352 | tf_op jit(solution)/shard_map/mine_right/ppermute | solution.py:217
  55.9 10.9 %collective-permute-start.3 = (bf16[128,1408]{1,0:T(8,128)(2,1)S(1)}, bf16[128,1408]{1,0:T(8,128)(2,1)S(1)}, u32[]{:S(2)}, u32[]{:S(2)}) collective-permute-start(bf16[128,1408]{1,0:T(8,128)(2,1)S(1)} %collective-permute-done.1), channel_id=1, source_target_pairs={{0,16},{16,32},{32,48},{48,0},{1,17},{17,33},{33,49},{49,1},{2,18}... | collective-permute-start | bytes 1081352 | tf_op jit(solution)/shard_map/mine_far/ppermute | solution.py:217
  58.2 14.6 %collective-permute-start.6 = (bf16[128,1408]{1,0:T(8,128)(2,1)S(1)}, bf16[128,1408]{1,0:T(8,128)(2,1)S(1)}, u32[]{:S(2)}, u32[]{:S(2)}) collective-permute-start(bf16[128,1408]{1,0:T(8,128)(2,1)S(1)} %collective-permute-done.1), channel_id=1, source_target_pairs={{0,1},{1,0},{2,3},{3,2},{4,5},{5,4},{6,7},{7,6},{8,9},{9,8},{10,11... | collective-permute-start | bytes 1081352 | tf_op jit(solution)/shard_map/pair_left/ppermute | solution.py:217
  62.0 10.9 %collective-permute-start.7 = (bf16[128,1408]{1,0:T(8,128)(2,1)S(1)}, bf16[128,1408]{1,0:T(8,128)(2,1)S(1)}, u32[]{:S(2)}, u32[]{:S(2)}) collective-permute-start(bf16[128,1408]{1,0:T(8,128)(2,1)S(1)} %collective-permute-done.5), channel_id=1, source_target_pairs={{16,0},{32,16},{48,32},{0,48},{17,1},{33,17},{49,33},{1,49},{18,2}... | collective-permute-start | bytes 1081352 | tf_op jit(solution)/shard_map/other_right/ppermute | solution.py:217
  67.0 16.9 %collective-permute-start.4 = (bf16[512,1408]{1,0:T(8,128)(2,1)S(1)}, bf16[512,1408]{1,0:T(8,128)(2,1)S(1)}, u32[]{:S(2)}, u32[]{:S(2)}) collective-permute-start(bf16[512,1408]{1,0:T(8,128)(2,1)S(1)} %pad_maximum_fusion.refs_0_.mine_ref), channel_id=1, source_target_pairs={{0,64},{64,0},{1,65},{65,1},{2,66},{66,2},{3,67},{67,3},{4,68},{68... | collective-permute-start | bytes 4325384 | tf_op jit(solution)/shard_map/swap_mine/ppermute | solution.py:217
  68.9 13.0 %collective-permute-start.8 = (bf16[128,1408]{1,0:T(8,128)(2,1)S(1)}, bf16[128,1408]{1,0:T(8,128)(2,1)S(1)}, u32[]{:S(2)}, u32[]{:S(2)}) collective-permute-start(bf16[128,1408]{1,0:T(8,128)(2,1)S(1)} %collective-permute-done.3), channel_id=1, source_target_pairs={{0,1},{1,0},{2,3},{3,2},{4,5},{5,4},{6,7},{7,6},{8,9},{9,8},{10,11... | collective-permute-start | bytes 1081352 | tf_op jit(solution)/shard_map/pair_far/ppermute | solution.py:217
  81.9 5.1 %collective-permute-start.9 = (bf16[512,1408]{1,0:T(8,128)(2,1)S(1)}, bf16[512,1408]{1,0:T(8,128)(2,1)S(1)}, u32[]{:S(2)}, u32[]{:S(2)}) collective-permute-start(bf16[512,1408]{1,0:T(8,128)(2,1)S(1)} %constant_dynamic-update-slice_fusion.refs_0_), channel_id=1, source_target_pairs={{0,64},{64,0},{1,65},{65,1},{2,66},{66,2},{3,67},{67,3},{4,68},{68... | collective-permute-start | bytes 4325384 | tf_op jit(solution)/shard_map/swap_other/ppermute | solution.py:217
  86.8 50.0 %copy-start = (s32[1,4]{1,0:T(1,128)S(1)}, s32[1,4]{1,0:T(1,128)}, u32[]{:S(2)}) copy-start(s32[1,4]{1,0:T(1,128)} %param.5) | copy-start | bytes 52
  133.2 3.6 %collective-permute-start.10 = (bf16[2,4,16,1536]{3,2,1,0:T(8,128)(2,1)S(1)}, bf16[2,4,16,1536]{3,2,1,0:T(8,128)(2,1)S(1)}, u32[]{:S(2)}, u32[]{:S(2)}) collective-permute-start(bf16[2,4,16,1536]{3,2,1,0:T(8,128)(2,1)S(1)} %bitcast.6), channel_id=1, source_target_pairs={{0,64},{64,0},{1,65},{65,1},{2,66},{66,2},{3,67},{67,3},{4,68},{68... | collective-permute-start | bytes 1179656 | tf_op jit(solution)/shard_map/ppermute | solution.py:249

commit v10 on v9

--- a/solution.py
+++ b/solution.py
@@ -1,3 +1,4 @@
+import functools
 import math
 
 import jax
@@ -69,18 +70,22 @@
     return total
 
 
-def gram_part_kernel(*refs):
+def gram_part_kernel(more, *refs):
     part_ref = refs[-1]
     for at, size in strips(part_ref.shape[1]):
-        part_ref[at : at + size, at:] = gram_sum(refs[:-1], at, size)
-
-
-def gram_part(*blocks):
+        total = gram_sum(refs[more:-1], at, size)
+        if more:
+            total = total + refs[0][at : at + size, at:]
+        part_ref[at : at + size, at:] = total
+
+
+def gram_part(part, *blocks):
+    given = () if part is None else (part,)
     rows, columns = sum(block.shape[0] for block in blocks), blocks[0].shape[1]
     vmem = pl.BlockSpec(memory_space=pltpu.VMEM)
     return pl.pallas_call(
-        gram_part_kernel,
-        in_specs=[vmem] * len(blocks),
+        functools.partial(gram_part_kernel, len(given)),
+        in_specs=[vmem] * (len(given) + len(blocks)),
         out_specs=vmem,
         out_shape=jax.ShapeDtypeStruct((columns, columns), F32),
         compiler_params=pltpu.CompilerParams(vmem_limit_bytes=24 * 1024 * 1024),
@@ -88,7 +93,7 @@
             flops=2 * rows * columns * columns, bytes_accessed=0, transcendentals=0
         ),
         name="gram_part",
-    )(*blocks)
+    )(*given, *blocks)
 
 
 def times(block, matrix):
@@ -241,9 +246,11 @@
     mine = jnp.concatenate([mine, mine_left, mine_right, mine_far], axis=0)
     mine_swapped = move("swap_mine", mine, "core", swap)
     other = jnp.concatenate([other, other_left, other_right, other_far], axis=0)
-    other_swapped = move("swap_other", other, "core", swap)
-    part = gram_part(mine, mine_swapped)
-    slots = products(mine, part, other, other_swapped)
+    part = gram_part(None, mine)
+    held, part = lax.optimization_barrier((other, part))
+    other_swapped = move("swap_other", held, "core", swap)
+    part = gram_part(part, other, mine_swapped)
+    slots = products(mine, part, other_swapped)
     near = lax.all_to_all(slots, "z", split_axis=0, concat_axis=0, tiled=True)
     near = near.reshape(2, matrices, rows // 2, columns + LANES)
     far = lax.ppermute(near, "core", swap)

time: 140 us -> 139 us (level)
  waiting for transfers between devices: 13.5 us -> 11.7 us
    ppermute x9, waiting for transfers between devices: 10.2 us -> 8.46 us  [move(): return lax.ppermute(block, axis, pairs)]
    pallas_call x1 -> x2, Pallas kernels: 2.98 us -> 4.56 us  [gram_part(): pl.pallas_call(functools.partial(gram_part_kernel, len(given)), in_specs=...]
    pallas_call x1, Pallas kernels: 11.6 us -> 10.2 us  [products(): pl.pallas_call(products_kernel, in_specs=[vmem] * (2 + len(blocks)), out_...]
  transfers between devices with their start and end apart: 11 -> 11, of which waited for: 5 -> 4; matrix products, arithmetic and copies ran while one was open for 0% -> 0% of each run, Pallas kernels for 2% -> 3%
where the time goes in v10:
time: 139 us; the launch traced here: 138 us
  blocking collectives  73.5 us (53%)
  starting transfers between devices  32 us (23%)
  Pallas kernels  18.6 us (13%)
  waiting for transfers between devices  11.7 us (8%)
    all_to_all x1, blocking collectives, on_device(): lax.all_to_all(halves.reshape(16, rows // 4, columns), 'z', split_axis=0,...  38.2 us
    all_to_all x1, blocking collectives, on_device(): near = lax.all_to_all(slots, 'z', split_axis=0, concat_axis=0, tiled=True)  35.3 us
    ppermute x9, starting transfers between devices, move(): return lax.ppermute(block, axis, pairs)  28.2 us
    pallas_call x1, Pallas kernels, products(): pl.pallas_call(products_kernel, in_specs=[vmem] * (2 + len(blocks)), out_...  10.2 us
    ppermute x9, waiting for transfers between devices, move(): return lax.ppermute(block, axis, pairs)  8.46 us
    pallas_call x2, Pallas kernels, gram_part(): pl.pallas_call(functools.partial(gram_part_kernel, len(given)), in_specs=...  4.56 us
  transfers between devices with their start and end apart: 11, of which 4 were waited for; matrix products, arithmetic and copies ran while one was open for 0% of the time, Pallas kernels for 3%

profile of v10, /device:TPU:6, one launch (start us, length us, event | category | flops | bytes accessed | tf_op | source)
XLA Modules:
  0.0 137.6 jit_solution(13490752172224235652)
XLA Ops:
  0.6 2.4 %momentum_step.1 = (f32[4,32,1408]{2,1,0:T(8,128)}, bf16[2,4,16,1408]{3,2,1,0:T(8,128)(2,1)}, bf16[4,16,1408]{2,1,0:T(8,128)(2,1)}) custom-call(bf16[4,32,1408]{2,1,0:T(8,128)(2,1)} %grad_ref.1, f32[4,32,1408]{2,1,0:T(8,128)} %momentum_ref.1), custom_call_target="tpu_custom_call" | custom-call | tf_op jit(solution)/shard_map/momentum_step/pallas_call | solution.py:39
  3.0 1.9 %collective-permute-start = (bf16[4,16,1408]{2,1,0:T(8,128)(2,1)}, bf16[4,16,1408]{2,1,0:T(8,128)(2,1)S(1)}, u32[]{:S(2)}, u32[]{:S(2)}) collective-permute-start(bf16[4,16,1408]{2,1,0:T(8,128)(2,1)} %get-tuple-element.12), channel_id=1, source_target_pairs={{0,64},{64,0},{1,65},{65,1},{2,66},{66,2},{3,67},{67,3},{4,68},{68... | collective-permute-start | bytes 540680 | tf_op jit(solution)/shard_map/ppermute | solution.py:234
  4.9 1.6 %collective-permute-done = bf16[4,16,1408]{2,1,0:T(8,128)(2,1)S(1)} collective-permute-done((bf16[4,16,1408]{2,1,0:T(8,128)(2,1)}, bf16[4,16,1408]{2,1,0:T(8,128)(2,1)S(1)}, u32[]{:S(2)}, u32[]{:S(2)}) %collective-permute-start) | collective-permute-done | bytes 180256 | tf_op jit(solution)/shard_map/ppermute | solution.py:234
  6.5 0.7 bitcast_dynamic-update-slice_fusion
  7.2 38.2 %all_to_all.10 = bf16[16,8,1408]{2,1,0:T(8,128)(2,1)S(1)} all-to-all(bf16[16,8,1408]{2,1,0:T(8,128)(2,1)} %bitcast.13), channel_id=1, replica_groups=mesh['x'=4,'core'=2,'y'=4,'z'=16] {'z'}, dimensions={0} | all-to-all | bytes 720896 | tf_op jit(solution)/shard_map/all_to_all | solution.py:236
  45.4 3.5 %collective-permute-start.1 = (bf16[128,1408]{1,0:T(8,128)(2,1)S(1)}, bf16[128,1408]{1,0:T(8,128)(2,1)S(1)}, u32[]{:S(2)}, u32[]{:S(2)}) collective-permute-start(bf16[128,1408]{1,0:T(8,128)(2,1)S(1)} %bitcast.9), channel_id=1, source_target_pairs={{0,16},{16,32},{32,48},{48,0},{1,17},{17,33},{33,49},{49,1},{2,18}... | collective-permute-start | bytes 1081352 | tf_op jit(solution)/shard_map/mine_left/ppermute | solution.py:222
  48.9 2.4 %collective-permute-start.4 = (bf16[128,1408]{1,0:T(8,128)(2,1)S(1)}, bf16[128,1408]{1,0:T(8,128)(2,1)S(1)}, u32[]{:S(2)}, u32[]{:S(2)}) collective-permute-start(bf16[128,1408]{1,0:T(8,128)(2,1)S(1)} %bitcast.10), channel_id=1, source_target_pairs={{0,1},{1,0},{2,3},{3,2},{4,5},{5,4},{6,7},{7,6},{8,9},{9,8},{10,11... | collective-permute-start | bytes 1081352 | tf_op jit(solution)/shard_map/pair/ppermute | solution.py:222
  51.3 3.6 %collective-permute-start.2 = (bf16[128,1408]{1,0:T(8,128)(2,1)S(1)}, bf16[128,1408]{1,0:T(8,128)(2,1)S(1)}, u32[]{:S(2)}, u32[]{:S(2)}) collective-permute-start(bf16[128,1408]{1,0:T(8,128)(2,1)S(1)} %bitcast.11), channel_id=1, source_target_pairs={{16,0},{32,16},{48,32},{0,48},{17,1},{33,17},{49,33},{1,49},{18,2}... | collective-permute-start | bytes 1081352 | tf_op jit(solution)/shard_map/mine_right/ppermute | solution.py:222
  54.8 1.1 collective-permute-done.1
  55.9 2.3 %collective-permute-start.3 = (bf16[128,1408]{1,0:T(8,128)(2,1)S(1)}, bf16[128,1408]{1,0:T(8,128)(2,1)S(1)}, u32[]{:S(2)}, u32[]{:S(2)}) collective-permute-start(bf16[128,1408]{1,0:T(8,128)(2,1)S(1)} %collective-permute-done.1), channel_id=1, source_target_pairs={{0,16},{16,32},{32,48},{48,0},{1,17},{17,33},{33,49},{49,1},{2,18}... | collective-permute-start | bytes 1081352 | tf_op jit(solution)/shard_map/mine_far/ppermute | solution.py:222
  58.2 3.8 %collective-permute-start.5 = (bf16[128,1408]{1,0:T(8,128)(2,1)S(1)}, bf16[128,1408]{1,0:T(8,128)(2,1)S(1)}, u32[]{:S(2)}, u32[]{:S(2)}) collective-permute-start(bf16[128,1408]{1,0:T(8,128)(2,1)S(1)} %collective-permute-done.1), channel_id=1, source_target_pairs={{0,1},{1,0},{2,3},{3,2},{4,5},{5,4},{6,7},{7,6},{8,9},{9,8},{10,11... | collective-permute-start | bytes 1081352 | tf_op jit(solution)/shard_map/pair_left/ppermute | solution.py:222
  61.9 0.0 collective-permute-done.4
  62.0 4.8 %collective-permute-start.6 = (bf16[128,1408]{1,0:T(8,128)(2,1)S(1)}, bf16[128,1408]{1,0:T(8,128)(2,1)S(1)}, u32[]{:S(2)}, u32[]{:S(2)}) collective-permute-start(bf16[128,1408]{1,0:T(8,128)(2,1)S(1)} %collective-permute-done.4), channel_id=1, source_target_pairs={{16,0},{32,16},{48,32},{0,48},{17,1},{33,17},{49,33},{1,49},{18,2}... | collective-permute-start | bytes 1081352 | tf_op jit(solution)/shard_map/other_right/ppermute | solution.py:222
  66.8 0.0 collective-permute-done.2
  66.9 0.0 collective-permute-done.3
  66.9 0.1 pad_maximum_fusion.refs_0_.mine_ref
  67.0 1.9 %collective-permute-start.8 = (bf16[512,1408]{1,0:T(8,128)(2,1)S(1)}, bf16[512,1408]{1,0:T(8,128)(2,1)S(1)}, u32[]{:S(2)}, u32[]{:S(2)}) collective-permute-start(bf16[512,1408]{1,0:T(8,128)(2,1)S(1)} %pad_maximum_fusion.refs_0_.mine_ref), channel_id=1, source_target_pairs={{0,64},{64,0},{1,65},{65,1},{2,66},{66,2},{3,67},{67,3},{4,68},{68... | collective-permute-start | bytes 4325384 | tf_op jit(solution)/shard_map/swap_mine/ppermute | solution.py:222
  68.9 3.9 %collective-permute-start.7 = (bf16[128,1408]{1,0:T(8,128)(2,1)S(1)}, bf16[128,1408]{1,0:T(8,128)(2,1)S(1)}, u32[]{:S(2)}, u32[]{:S(2)}) collective-permute-start(bf16[128,1408]{1,0:T(8,128)(2,1)S(1)} %collective-permute-done.3), channel_id=1, source_target_pairs={{0,1},{1,0},{2,3},{3,2},{4,5},{5,4},{6,7},{7,6},{8,9},{9,8},{10,11... | collective-permute-start | bytes 1081352 | tf_op jit(solution)/shard_map/pair_far/ppermute | solution.py:222
  72.8 0.0 collective-permute-done.5
  72.9 0.0 collective-permute-done.6
  72.9 1.6 %gram_part.2.refs_0_ = f32[1408,1408]{1,0:T(8,128)S(1)} custom-call(bf16[512,1408]{1,0:T(8,128)(2,1)S(1)} %pad_maximum_fusion.refs_0_.mine_ref), custom_call_target="tpu_custom_call" | custom-call | flops 2030043136 | tf_op jit(solution)/shard_map/gram_part/pallas_call | solution.py:86
  74.5 7.4 %collective-permute-done.7 = bf16[128,1408]{1,0:T(8,128)(2,1)S(1)} collective-permute-done((bf16[128,1408]{1,0:T(8,128)(2,1)S(1)}, bf16[128,1408]{1,0:T(8,128)(2,1)S(1)}, u32[]{:S(2)}, u32[]{:S(2)}) %collective-permute-start.7) | collective-permute-done | bytes 360480 | tf_op jit(solution)/shard_map/pair_far/ppermute | solution.py:222
  81.9 2.1 %collective-permute-start.9 = (bf16[512,1408]{1,0:T(8,128)(2,1)S(1)}, bf16[512,1408]{1,0:T(8,128)(2,1)S(1)}, u32[]{:S(2)}, u32[]{:S(2)}) collective-permute-start(bf16[512,1408]{1,0:T(8,128)(2,1)S(1)} %constant_dynamic-update-slice_fusion.refs_1_), channel_id=1, source_target_pairs={{0,64},{64,0},{1,65},{65,1},{2,66},{66,2},{3,67},{67,3},{4,68},{68... | collective-permute-start | bytes 4325384 | tf_op jit(solution)/shard_map/swap_other/ppermute | solution.py:222
  84.0 0.0 collective-permute-done.8.refs_2_
  84.0 3.0 %gram_part.3.part_ref = f32[1408,1408]{1,0:T(8,128)S(1)} custom-call(f32[1408,1408]{1,0:T(8,128)S(1)} %gram_part.2.refs_0_, bf16[512,1408]{1,0:T(8,128)(2,1)S(1)} %constant_dynamic-update-slice_fusion.refs_1_, bf16[512,1408]{1,0:T(8,128)(2,1)S(1)} %collective-permute-done.8.refs_2_), custom_call_target="tpu_custom_call" | custom-call | flops 4060086272 | tf_op jit(solution)/shard_map/gram_part/pallas_call | solution.py:86
  87.0 0.0 copy-start
  87.0 0.0 collective-permute-done.9.refs_0_
  87.0 10.2 %products.1 = bf16[16,8,1536]{2,1,0:T(8,128)(2,1)S(1)} custom-call(bf16[512,1408]{1,0:T(8,128)(2,1)S(1)} %pad_maximum_fusion.refs_0_.mine_ref, f32[1408,1408]{1,0:T(8,128)S(1)} %gram_part.3.part_ref, bf16[512,1408]{1,0:T(8,128)(2,1)S(1)} %collective-permute-done.9.refs_0_), custom_call_target="tpu_custom_call" | custom-call | flops 12180258816 | tf_op jit(solution)/shard_map/products/pallas_call | solution.py:164
  97.2 35.3 %all_to_all.11 = bf16[16,8,1536]{2,1,0:T(8,128)(2,1)S(1)} all-to-all(bf16[16,8,1536]{2,1,0:T(8,128)(2,1)S(1)} %products.1), channel_id=1, replica_groups=mesh['x'=4,'core'=2,'y'=4,'z'=16] {'z'}, dimensions={0} | all-to-all | bytes 786432 | tf_op jit(solution)/shard_map/all_to_all | solution.py:254
  132.5 1.9 %collective-permute-start.10 = (bf16[2,4,16,1536]{3,2,1,0:T(8,128)(2,1)S(1)}, bf16[2,4,16,1536]{3,2,1,0:T(8,128)(2,1)S(1)}, u32[]{:S(2)}, u32[]{:S(2)}) collective-permute-start(bf16[2,4,16,1536]{3,2,1,0:T(8,128)(2,1)S(1)} %bitcast.6), channel_id=1, source_target_pairs={{0,64},{64,0},{1,65},{65,1},{2,66},{66,2},{3,67},{67,3},{4,68},{68... | collective-permute-start | bytes 1179656 | tf_op jit(solution)/shard_map/ppermute | solution.py:256
  134.4 1.7 %collective-permute-done.10.far_ref = bf16[2,4,16,1536]{3,2,1,0:T(8,128)(2,1)S(1)} collective-permute-done((bf16[2,4,16,1536]{3,2,1,0:T(8,128)(2,1)S(1)}, bf16[2,4,16,1536]{3,2,1,0:T(8,128)(2,1)S(1)}, u32[]{:S(2)}, u32[]{:S(2)}) %collective-permute-start.10) | collective-permute-done | bytes 393248 | tf_op jit(solution)/shard_map/ppermute | solution.py:256
  136.1 1.5 %regroup.1 = (bf16[4,32,1408]{2,1,0:T(8,128)(2,1)}, f32[1,88]{1,0:T(1,128)}) custom-call(s32[4]{0:T(128)S(1)} %bitcast.8, bf16[2,4,16,1536]{3,2,1,0:T(8,128)(2,1)S(1)} %bitcast.7, bf16[2,4,16,1536]{3,2,1,0:T(8,128)(2,1)S(1)} %collective-permute-done.10.far_ref), custom_call_target="tpu_custom_call" | custom-call | tf_op jit(solution)/shard_map/regroup/pallas_call | solution.py:207
  (5 shorter events, 0.1 us)
Async XLA Ops:
  3.0 3.5 %collective-permute-start = (bf16[4,16,1408]{2,1,0:T(8,128)(2,1)}, bf16[4,16,1408]{2,1,0:T(8,128)(2,1)S(1)}, u32[]{:S(2)}, u32[]{:S(2)}) collective-permute-start(bf16[4,16,1408]{2,1,0:T(8,128)(2,1)} %get-tuple-element.12), channel_id=1, source_target_pairs={{0,64},{64,0},{1,65},{65,1},{2,66},{66,2},{3,67},{67,3},{4,68},{68... | collective-permute-start | bytes 540680 | tf_op jit(solution)/shard_map/ppermute | solution.py:234
  45.4 10.5 %collective-permute-start.1 = (bf16[128,1408]{1,0:T(8,128)(2,1)S(1)}, bf16[128,1408]{1,0:T(8,128)(2,1)S(1)}, u32[]{:S(2)}, u32[]{:S(2)}) collective-permute-start(bf16[128,1408]{1,0:T(8,128)(2,1)S(1)} %bitcast.9), channel_id=1, source_target_pairs={{0,16},{16,32},{32,48},{48,0},{1,17},{17,33},{33,49},{49,1},{2,18}... | collective-permute-start | bytes 1081352 | tf_op jit(solution)/shard_map/mine_left/ppermute | solution.py:222
  48.9 13.1 %collective-permute-start.4 = (bf16[128,1408]{1,0:T(8,128)(2,1)S(1)}, bf16[128,1408]{1,0:T(8,128)(2,1)S(1)}, u32[]{:S(2)}, u32[]{:S(2)}) collective-permute-start(bf16[128,1408]{1,0:T(8,128)(2,1)S(1)} %bitcast.10), channel_id=1, source_target_pairs={{0,1},{1,0},{2,3},{3,2},{4,5},{5,4},{6,7},{7,6},{8,9},{9,8},{10,11... | collective-permute-start | bytes 1081352 | tf_op jit(solution)/shard_map/pair/ppermute | solution.py:222
  51.3 15.6 %collective-permute-start.2 = (bf16[128,1408]{1,0:T(8,128)(2,1)S(1)}, bf16[128,1408]{1,0:T(8,128)(2,1)S(1)}, u32[]{:S(2)}, u32[]{:S(2)}) collective-permute-start(bf16[128,1408]{1,0:T(8,128)(2,1)S(1)} %bitcast.11), channel_id=1, source_target_pairs={{16,0},{32,16},{48,32},{0,48},{17,1},{33,17},{49,33},{1,49},{18,2}... | collective-permute-start | bytes 1081352 | tf_op jit(solution)/shard_map/mine_right/ppermute | solution.py:222
  55.9 10.9 %collective-permute-start.3 = (bf16[128,1408]{1,0:T(8,128)(2,1)S(1)}, bf16[128,1408]{1,0:T(8,128)(2,1)S(1)}, u32[]{:S(2)}, u32[]{:S(2)}) collective-permute-start(bf16[128,1408]{1,0:T(8,128)(2,1)S(1)} %collective-permute-done.1), channel_id=1, source_target_pairs={{0,16},{16,32},{32,48},{48,0},{1,17},{17,33},{33,49},{49,1},{2,18}... | collective-permute-start | bytes 1081352 | tf_op jit(solution)/shard_map/mine_far/ppermute | solution.py:222
  58.2 14.6 %collective-permute-start.5 = (bf16[128,1408]{1,0:T(8,128)(2,1)S(1)}, bf16[128,1408]{1,0:T(8,128)(2,1)S(1)}, u32[]{:S(2)}, u32[]{:S(2)}) collective-permute-start(bf16[128,1408]{1,0:T(8,128)(2,1)S(1)} %collective-permute-done.1), channel_id=1, source_target_pairs={{0,1},{1,0},{2,3},{3,2},{4,5},{5,4},{6,7},{7,6},{8,9},{9,8},{10,11... | collective-permute-start | bytes 1081352 | tf_op jit(solution)/shard_map/pair_left/ppermute | solution.py:222
  62.0 10.9 %collective-permute-start.6 = (bf16[128,1408]{1,0:T(8,128)(2,1)S(1)}, bf16[128,1408]{1,0:T(8,128)(2,1)S(1)}, u32[]{:S(2)}, u32[]{:S(2)}) collective-permute-start(bf16[128,1408]{1,0:T(8,128)(2,1)S(1)} %collective-permute-done.4), channel_id=1, source_target_pairs={{16,0},{32,16},{48,32},{0,48},{17,1},{33,17},{49,33},{1,49},{18,2}... | collective-permute-start | bytes 1081352 | tf_op jit(solution)/shard_map/other_right/ppermute | solution.py:222
  67.0 17.0 %collective-permute-start.8 = (bf16[512,1408]{1,0:T(8,128)(2,1)S(1)}, bf16[512,1408]{1,0:T(8,128)(2,1)S(1)}, u32[]{:S(2)}, u32[]{:S(2)}) collective-permute-start(bf16[512,1408]{1,0:T(8,128)(2,1)S(1)} %pad_maximum_fusion.refs_0_.mine_ref), channel_id=1, source_target_pairs={{0,64},{64,0},{1,65},{65,1},{2,66},{66,2},{3,67},{67,3},{4,68},{68... | collective-permute-start | bytes 4325384 | tf_op jit(solution)/shard_map/swap_mine/ppermute | solution.py:222
  68.9 13.0 %collective-permute-start.7 = (bf16[128,1408]{1,0:T(8,128)(2,1)S(1)}, bf16[128,1408]{1,0:T(8,128)(2,1)S(1)}, u32[]{:S(2)}, u32[]{:S(2)}) collective-permute-start(bf16[128,1408]{1,0:T(8,128)(2,1)S(1)} %collective-permute-done.3), channel_id=1, source_target_pairs={{0,1},{1,0},{2,3},{3,2},{4,5},{5,4},{6,7},{7,6},{8,9},{9,8},{10,11... | collective-permute-start | bytes 1081352 | tf_op jit(solution)/shard_map/pair_far/ppermute | solution.py:222
  81.9 5.1 %collective-permute-start.9 = (bf16[512,1408]{1,0:T(8,128)(2,1)S(1)}, bf16[512,1408]{1,0:T(8,128)(2,1)S(1)}, u32[]{:S(2)}, u32[]{:S(2)}) collective-permute-start(bf16[512,1408]{1,0:T(8,128)(2,1)S(1)} %constant_dynamic-update-slice_fusion.refs_1_), channel_id=1, source_target_pairs={{0,64},{64,0},{1,65},{65,1},{2,66},{66,2},{3,67},{67,3},{4,68},{68... | collective-permute-start | bytes 4325384 | tf_op jit(solution)/shard_map/swap_other/ppermute | solution.py:222
  87.0 49.1 %copy-start = (s32[1,4]{1,0:T(1,128)S(1)}, s32[1,4]{1,0:T(1,128)}, u32[]{:S(2)}) copy-start(s32[1,4]{1,0:T(1,128)} %param.5) | copy-start | bytes 52
  132.5 3.6 %collective-permute-start.10 = (bf16[2,4,16,1536]{3,2,1,0:T(8,128)(2,1)S(1)}, bf16[2,4,16,1536]{3,2,1,0:T(8,128)(2,1)S(1)}, u32[]{:S(2)}, u32[]{:S(2)}) collective-permute-start(bf16[2,4,16,1536]{3,2,1,0:T(8,128)(2,1)S(1)} %bitcast.6), channel_id=1, source_target_pairs={{0,64},{64,0},{1,65},{65,1},{2,66},{66,2},{3,67},{67,3},{4,68},{68... | collective-permute-start | bytes 1179656 | tf_op jit(solution)/shard_map/ppermute | solution.py:256

commit v11 on v10

--- a/solution.py
+++ b/solution.py
@@ -244,12 +244,14 @@
     other_left = move("pair_left", mine_left, "z", pairs)
     other_far = move("pair_far", mine_far, "z", pairs)
     mine = jnp.concatenate([mine, mine_left, mine_right, mine_far], axis=0)
+    other_first = other
+    other = jnp.concatenate([other, other_left, other_right, other_far], axis=0)
+    part = gram_part(None, mine, other_left)
+    mine, part = lax.optimization_barrier((mine, part))
     mine_swapped = move("swap_mine", mine, "core", swap)
-    other = jnp.concatenate([other, other_left, other_right, other_far], axis=0)
-    part = gram_part(None, mine)
     held, part = lax.optimization_barrier((other, part))
     other_swapped = move("swap_other", held, "core", swap)
-    part = gram_part(part, other, mine_swapped)
+    part = gram_part(part, other_right, other_first, other_far, mine_swapped)
     slots = products(mine, part, other_swapped)
     near = lax.all_to_all(slots, "z", split_axis=0, concat_axis=0, tiled=True)
     near = near.reshape(2, matrices, rows // 2, columns + LANES)

time: 139 us -> 138 us (level)
  starting transfers between devices: 32 us -> 30.4 us
    ppermute x9, starting transfers between devices: 28.2 us -> 26.5 us  [move(): return lax.ppermute(block, axis, pairs)]
  transfers between devices with their start and end apart: 11 -> 11, of which waited for: 4 -> 6; matrix products, arithmetic and copies ran while one was open for 0% -> 0% of each run, Pallas kernels for 3% -> 4%
where the time goes in v11:
time: 138 us; the launch traced here: 136 us
  blocking collectives  72.3 us (52%)
  starting transfers between devices  30.4 us (22%)
  Pallas kernels  19.6 us (14%)
  waiting for transfers between devices  12.5 us (9%)
    all_to_all x1, blocking collectives, on_device(): lax.all_to_all(halves.reshape(16, rows // 4, columns), 'z', split_axis=0,...  38.2 us
    all_to_all x1, blocking collectives, on_device(): near = lax.all_to_all(slots, 'z', split_axis=0, concat_axis=0, tiled=True)  34 us
    ppermute x9, starting transfers between devices, move(): return lax.ppermute(block, axis, pairs)  26.5 us
    pallas_call x1, Pallas kernels, products(): pl.pallas_call(products_kernel, in_specs=[vmem] * (2 + len(blocks)), out_...  10.2 us
    ppermute x9, waiting for transfers between devices, move(): return lax.ppermute(block, axis, pairs)  9.18 us
    pallas_call x2, Pallas kernels, gram_part(): pl.pallas_call(functools.partial(gram_part_kernel, len(given)), in_specs=...  5.57 us
  transfers between devices with their start and end apart: 11, of which 6 were waited for; matrix products, arithmetic and copies ran while one was open for 0% of the time, Pallas kernels for 4%

profile of v11, /device:TPU:6, one launch (start us, length us, event | category | flops | bytes accessed | tf_op | source)
XLA Modules:
  0.0 136.4 jit_solution(15887250053813461894)
XLA Ops:
  0.6 2.4 %momentum_step.1 = (f32[4,32,1408]{2,1,0:T(8,128)}, bf16[2,4,16,1408]{3,2,1,0:T(8,128)(2,1)}, bf16[4,16,1408]{2,1,0:T(8,128)(2,1)}) custom-call(bf16[4,32,1408]{2,1,0:T(8,128)(2,1)} %grad_ref.1, f32[4,32,1408]{2,1,0:T(8,128)} %momentum_ref.1), custom_call_target="tpu_custom_call" | custom-call | tf_op jit(solution)/shard_map/momentum_step/pallas_call | solution.py:39
  3.0 1.9 %collective-permute-start = (bf16[4,16,1408]{2,1,0:T(8,128)(2,1)}, bf16[4,16,1408]{2,1,0:T(8,128)(2,1)S(1)}, u32[]{:S(2)}, u32[]{:S(2)}) collective-permute-start(bf16[4,16,1408]{2,1,0:T(8,128)(2,1)} %get-tuple-element.14), channel_id=1, source_target_pairs={{0,64},{64,0},{1,65},{65,1},{2,66},{66,2},{3,67},{67,3},{4,68},{68... | collective-permute-start | bytes 540680 | tf_op jit(solution)/shard_map/ppermute | solution.py:234
  4.9 1.6 %collective-permute-done = bf16[4,16,1408]{2,1,0:T(8,128)(2,1)S(1)} collective-permute-done((bf16[4,16,1408]{2,1,0:T(8,128)(2,1)}, bf16[4,16,1408]{2,1,0:T(8,128)(2,1)S(1)}, u32[]{:S(2)}, u32[]{:S(2)}) %collective-permute-start) | collective-permute-done | bytes 180256 | tf_op jit(solution)/shard_map/ppermute | solution.py:234
  6.5 0.7 bitcast_dynamic-update-slice_fusion
  7.2 38.2 %all_to_all.10 = bf16[16,8,1408]{2,1,0:T(8,128)(2,1)S(1)} all-to-all(bf16[16,8,1408]{2,1,0:T(8,128)(2,1)} %bitcast.13), channel_id=1, replica_groups=mesh['x'=4,'core'=2,'y'=4,'z'=16] {'z'}, dimensions={0} | all-to-all | bytes 720896 | tf_op jit(solution)/shard_map/all_to_all | solution.py:236
  45.4 3.5 %collective-permute-start.1 = (bf16[128,1408]{1,0:T(8,128)(2,1)S(1)}, bf16[128,1408]{1,0:T(8,128)(2,1)S(1)}, u32[]{:S(2)}, u32[]{:S(2)}) collective-permute-start(bf16[128,1408]{1,0:T(8,128)(2,1)S(1)} %bitcast.9), channel_id=1, source_target_pairs={{0,16},{16,32},{32,48},{48,0},{1,17},{17,33},{33,49},{49,1},{2,18}... | collective-permute-start | bytes 1081352 | tf_op jit(solution)/shard_map/mine_left/ppermute | solution.py:222
  48.9 2.4 %collective-permute-start.5 = (bf16[128,1408]{1,0:T(8,128)(2,1)S(1)}, bf16[128,1408]{1,0:T(8,128)(2,1)S(1)}, u32[]{:S(2)}, u32[]{:S(2)}) collective-permute-start(bf16[128,1408]{1,0:T(8,128)(2,1)S(1)} %bitcast.10), channel_id=1, source_target_pairs={{0,1},{1,0},{2,3},{3,2},{4,5},{5,4},{6,7},{7,6},{8,9},{9,8},{10,11... | collective-permute-start | bytes 1081352 | tf_op jit(solution)/shard_map/pair/ppermute | solution.py:222
  51.3 5.6 %collective-permute-done.1 = bf16[128,1408]{1,0:T(8,128)(2,1)S(1)} collective-permute-done((bf16[128,1408]{1,0:T(8,128)(2,1)S(1)}, bf16[128,1408]{1,0:T(8,128)(2,1)S(1)}, u32[]{:S(2)}, u32[]{:S(2)}) %collective-permute-start.1) | collective-permute-done | bytes 360480 | tf_op jit(solution)/shard_map/mine_left/ppermute | solution.py:222
  56.9 2.3 %collective-permute-start.3 = (bf16[128,1408]{1,0:T(8,128)(2,1)S(1)}, bf16[128,1408]{1,0:T(8,128)(2,1)S(1)}, u32[]{:S(2)}, u32[]{:S(2)}) collective-permute-start(bf16[128,1408]{1,0:T(8,128)(2,1)S(1)} %collective-permute-done.1), channel_id=1, source_target_pairs={{0,16},{16,32},{32,48},{48,0},{1,17},{17,33},{33,49},{49,1},{2,18}... | collective-permute-start | bytes 1081352 | tf_op jit(solution)/shard_map/mine_far/ppermute | solution.py:222
  59.1 4.8 %collective-permute-start.2 = (bf16[128,1408]{1,0:T(8,128)(2,1)S(1)}, bf16[128,1408]{1,0:T(8,128)(2,1)S(1)}, u32[]{:S(2)}, u32[]{:S(2)}) collective-permute-start(bf16[128,1408]{1,0:T(8,128)(2,1)S(1)} %bitcast.11), channel_id=1, source_target_pairs={{16,0},{32,16},{48,32},{0,48},{17,1},{33,17},{49,33},{1,49},{18,2}... | collective-permute-start | bytes 1081352 | tf_op jit(solution)/shard_map/mine_right/ppermute | solution.py:222
  63.9 2.9 %collective-permute-start.4 = (bf16[128,1408]{1,0:T(8,128)(2,1)S(1)}, bf16[128,1408]{1,0:T(8,128)(2,1)S(1)}, u32[]{:S(2)}, u32[]{:S(2)}) collective-permute-start(bf16[128,1408]{1,0:T(8,128)(2,1)S(1)} %collective-permute-done.1), channel_id=1, source_target_pairs={{0,1},{1,0},{2,3},{3,2},{4,5},{5,4},{6,7},{7,6},{8,9},{9,8},{10,11... | collective-permute-start | bytes 1081352 | tf_op jit(solution)/shard_map/pair_left/ppermute | solution.py:222
  66.8 0.0 collective-permute-done.5.refs_2_
  66.8 2.8 %collective-permute-start.6 = (bf16[128,1408]{1,0:T(8,128)(2,1)S(1)}, bf16[128,1408]{1,0:T(8,128)(2,1)S(1)}, u32[]{:S(2)}, u32[]{:S(2)}) collective-permute-start(bf16[128,1408]{1,0:T(8,128)(2,1)S(1)} %collective-permute-done.5.refs_2_), channel_id=1, source_target_pairs={{16,0},{32,16},{48,32},{0,48},{17,1},{33,17},{49,33},{1,49},{18,2}... | collective-permute-start | bytes 1081352 | tf_op jit(solution)/shard_map/other_right/ppermute | solution.py:222
  69.7 0.0 collective-permute-done.3
  69.7 3.9 %collective-permute-start.7 = (bf16[128,1408]{1,0:T(8,128)(2,1)S(1)}, bf16[128,1408]{1,0:T(8,128)(2,1)S(1)}, u32[]{:S(2)}, u32[]{:S(2)}) collective-permute-start(bf16[128,1408]{1,0:T(8,128)(2,1)S(1)} %collective-permute-done.3), channel_id=1, source_target_pairs={{0,1},{1,0},{2,3},{3,2},{4,5},{5,4},{6,7},{7,6},{8,9},{9,8},{10,11... | collective-permute-start | bytes 1081352 | tf_op jit(solution)/shard_map/pair_far/ppermute | solution.py:222
  73.6 0.1 pad_maximum_fusion.refs_0_.mine_ref
  73.7 2.6 %collective-permute-done.4.refs_1_ = bf16[128,1408]{1,0:T(8,128)(2,1)S(1)} collective-permute-done((bf16[128,1408]{1,0:T(8,128)(2,1)S(1)}, bf16[128,1408]{1,0:T(8,128)(2,1)S(1)}, u32[]{:S(2)}, u32[]{:S(2)}) %collective-permute-start.4) | collective-permute-done | bytes 360480 | tf_op jit(solution)/shard_map/pair_left/ppermute | solution.py:222
  76.3 2.2 %gram_part.2.refs_0_ = f32[1408,1408]{1,0:T(8,128)S(1)} custom-call(bf16[512,1408]{1,0:T(8,128)(2,1)S(1)} %pad_maximum_fusion.refs_0_.mine_ref, bf16[128,1408]{1,0:T(8,128)(2,1)S(1)} %collective-permute-done.4.refs_1_), custom_call_target="tpu_custom_call" | custom-call | flops 2537553920 | tf_op jit(solution)/shard_map/gram_part/pallas_call | solution.py:86
  78.5 1.9 %collective-permute-start.8 = (bf16[512,1408]{1,0:T(8,128)(2,1)S(1)}, bf16[512,1408]{1,0:T(8,128)(2,1)S(1)}, u32[]{:S(2)}, u32[]{:S(2)}) collective-permute-start(bf16[512,1408]{1,0:T(8,128)(2,1)S(1)} %pad_maximum_fusion.refs_0_.mine_ref), channel_id=1, source_target_pairs={{0,64},{64,0},{1,65},{65,1},{2,66},{66,2},{3,67},{67,3},{4,68},{68... | collective-permute-start | bytes 4325384 | tf_op jit(solution)/shard_map/swap_mine/ppermute | solution.py:222
  80.5 0.0 collective-permute-done.6.refs_1_
  80.5 0.5 collective-permute-done.7.refs_3_
  81.0 0.1 pad_maximum_fusion.1
  81.1 2.1 %collective-permute-start.9 = (bf16[512,1408]{1,0:T(8,128)(2,1)S(1)}, bf16[512,1408]{1,0:T(8,128)(2,1)S(1)}, u32[]{:S(2)}, u32[]{:S(2)}) collective-permute-start(bf16[512,1408]{1,0:T(8,128)(2,1)S(1)} %pad_maximum_fusion.1), channel_id=1, source_target_pairs={{0,64},{64,0},{1,65},{65,1},{2,66},{66,2},{3,67},{67,3},{4,68},{68... | collective-permute-start | bytes 4325384 | tf_op jit(solution)/shard_map/swap_other/ppermute | solution.py:222
  83.2 0.4 collective-permute-done.8.refs_4_
  83.6 3.4 %gram_part.3.part_ref = f32[1408,1408]{1,0:T(8,128)S(1)} custom-call(f32[1408,1408]{1,0:T(8,128)S(1)} %gram_part.2.refs_0_, bf16[128,1408]{1,0:T(8,128)(2,1)S(1)} %collective-permute-done.6.refs_1_, bf16[128,1408]{1,0:T(8,128)(2,1)S(1)} %collective-permute-done.5.refs_2_, bf16[128,1408]{1,0:T(8,128)(2,1)S(1)} %collective-permute-done.7.refs_3_, ...), custom_call_target="tpu_custom_call" | custom-call | flops 3552575488 | tf_op jit(solution)/shard_map/gram_part/pallas_call | solution.py:86
  87.0 0.0 copy-start
  87.0 0.0 collective-permute-done.9.refs_0_
  87.1 10.2 %products.1 = bf16[16,8,1536]{2,1,0:T(8,128)(2,1)S(1)} custom-call(bf16[512,1408]{1,0:T(8,128)(2,1)S(1)} %pad_maximum_fusion.refs_0_.mine_ref, f32[1408,1408]{1,0:T(8,128)S(1)} %gram_part.3.part_ref, bf16[512,1408]{1,0:T(8,128)(2,1)S(1)} %collective-permute-done.9.refs_0_), custom_call_target="tpu_custom_call" | custom-call | flops 12180258816 | tf_op jit(solution)/shard_map/products/pallas_call | solution.py:164
  97.2 34.0 %all_to_all.11 = bf16[16,8,1536]{2,1,0:T(8,128)(2,1)S(1)} all-to-all(bf16[16,8,1536]{2,1,0:T(8,128)(2,1)S(1)} %products.1), channel_id=1, replica_groups=mesh['x'=4,'core'=2,'y'=4,'z'=16] {'z'}, dimensions={0} | all-to-all | bytes 786432 | tf_op jit(solution)/shard_map/all_to_all | solution.py:256
  131.3 1.9 %collective-permute-start.10 = (bf16[2,4,16,1536]{3,2,1,0:T(8,128)(2,1)S(1)}, bf16[2,4,16,1536]{3,2,1,0:T(8,128)(2,1)S(1)}, u32[]{:S(2)}, u32[]{:S(2)}) collective-permute-start(bf16[2,4,16,1536]{3,2,1,0:T(8,128)(2,1)S(1)} %bitcast.6), channel_id=1, source_target_pairs={{0,64},{64,0},{1,65},{65,1},{2,66},{66,2},{3,67},{67,3},{4,68},{68... | collective-permute-start | bytes 1179656 | tf_op jit(solution)/shard_map/ppermute | solution.py:258
  133.2 1.7 %collective-permute-done.10.far_ref = bf16[2,4,16,1536]{3,2,1,0:T(8,128)(2,1)S(1)} collective-permute-done((bf16[2,4,16,1536]{3,2,1,0:T(8,128)(2,1)S(1)}, bf16[2,4,16,1536]{3,2,1,0:T(8,128)(2,1)S(1)}, u32[]{:S(2)}, u32[]{:S(2)}) %collective-permute-start.10) | collective-permute-done | bytes 393248 | tf_op jit(solution)/shard_map/ppermute | solution.py:258
  134.9 1.5 %regroup.1 = (bf16[4,32,1408]{2,1,0:T(8,128)(2,1)}, f32[1,88]{1,0:T(1,128)}) custom-call(s32[4]{0:T(128)S(1)} %bitcast.8, bf16[2,4,16,1536]{3,2,1,0:T(8,128)(2,1)S(1)} %bitcast.7, bf16[2,4,16,1536]{3,2,1,0:T(8,128)(2,1)S(1)} %collective-permute-done.10.far_ref), custom_call_target="tpu_custom_call" | custom-call | tf_op jit(solution)/shard_map/regroup/pallas_call | solution.py:207
  (2 shorter events, 0.0 us)
Async XLA Ops:
  3.0 3.5 %collective-permute-start = (bf16[4,16,1408]{2,1,0:T(8,128)(2,1)}, bf16[4,16,1408]{2,1,0:T(8,128)(2,1)S(1)}, u32[]{:S(2)}, u32[]{:S(2)}) collective-permute-start(bf16[4,16,1408]{2,1,0:T(8,128)(2,1)} %get-tuple-element.14), channel_id=1, source_target_pairs={{0,64},{64,0},{1,65},{65,1},{2,66},{66,2},{3,67},{67,3},{4,68},{68... | collective-permute-start | bytes 540680 | tf_op jit(solution)/shard_map/ppermute | solution.py:234
  45.4 11.5 %collective-permute-start.1 = (bf16[128,1408]{1,0:T(8,128)(2,1)S(1)}, bf16[128,1408]{1,0:T(8,128)(2,1)S(1)}, u32[]{:S(2)}, u32[]{:S(2)}) collective-permute-start(bf16[128,1408]{1,0:T(8,128)(2,1)S(1)} %bitcast.9), channel_id=1, source_target_pairs={{0,16},{16,32},{32,48},{48,0},{1,17},{17,33},{33,49},{49,1},{2,18}... | collective-permute-start | bytes 1081352 | tf_op jit(solution)/shard_map/mine_left/ppermute | solution.py:222
  48.9 17.9 %collective-permute-start.5 = (bf16[128,1408]{1,0:T(8,128)(2,1)S(1)}, bf16[128,1408]{1,0:T(8,128)(2,1)S(1)}, u32[]{:S(2)}, u32[]{:S(2)}) collective-permute-start(bf16[128,1408]{1,0:T(8,128)(2,1)S(1)} %bitcast.10), channel_id=1, source_target_pairs={{0,1},{1,0},{2,3},{3,2},{4,5},{5,4},{6,7},{7,6},{8,9},{9,8},{10,11... | collective-permute-start | bytes 1081352 | tf_op jit(solution)/shard_map/pair/ppermute | solution.py:222
  56.9 12.8 %collective-permute-start.3 = (bf16[128,1408]{1,0:T(8,128)(2,1)S(1)}, bf16[128,1408]{1,0:T(8,128)(2,1)S(1)}, u32[]{:S(2)}, u32[]{:S(2)}) collective-permute-start(bf16[128,1408]{1,0:T(8,128)(2,1)S(1)} %collective-permute-done.1), channel_id=1, source_target_pairs={{0,16},{16,32},{32,48},{48,0},{1,17},{17,33},{33,49},{49,1},{2,18}... | collective-permute-start | bytes 1081352 | tf_op jit(solution)/shard_map/mine_far/ppermute | solution.py:222
  59.1 14.5 %collective-permute-start.2 = (bf16[128,1408]{1,0:T(8,128)(2,1)S(1)}, bf16[128,1408]{1,0:T(8,128)(2,1)S(1)}, u32[]{:S(2)}, u32[]{:S(2)}) collective-permute-start(bf16[128,1408]{1,0:T(8,128)(2,1)S(1)} %bitcast.11), channel_id=1, source_target_pairs={{16,0},{32,16},{48,32},{0,48},{17,1},{33,17},{49,33},{1,49},{18,2}... | collective-permute-start | bytes 1081352 | tf_op jit(solution)/shard_map/mine_right/ppermute | solution.py:222
  63.9 12.4 %collective-permute-start.4 = (bf16[128,1408]{1,0:T(8,128)(2,1)S(1)}, bf16[128,1408]{1,0:T(8,128)(2,1)S(1)}, u32[]{:S(2)}, u32[]{:S(2)}) collective-permute-start(bf16[128,1408]{1,0:T(8,128)(2,1)S(1)} %collective-permute-done.1), channel_id=1, source_target_pairs={{0,1},{1,0},{2,3},{3,2},{4,5},{5,4},{6,7},{7,6},{8,9},{9,8},{10,11... | collective-permute-start | bytes 1081352 | tf_op jit(solution)/shard_map/pair_left/ppermute | solution.py:222
  66.8 13.6 %collective-permute-start.6 = (bf16[128,1408]{1,0:T(8,128)(2,1)S(1)}, bf16[128,1408]{1,0:T(8,128)(2,1)S(1)}, u32[]{:S(2)}, u32[]{:S(2)}) collective-permute-start(bf16[128,1408]{1,0:T(8,128)(2,1)S(1)} %collective-permute-done.5.refs_2_), channel_id=1, source_target_pairs={{16,0},{32,16},{48,32},{0,48},{17,1},{33,17},{49,33},{1,49},{18,2}... | collective-permute-start | bytes 1081352 | tf_op jit(solution)/shard_map/other_right/ppermute | solution.py:222
  69.7 11.3 %collective-permute-start.7 = (bf16[128,1408]{1,0:T(8,128)(2,1)S(1)}, bf16[128,1408]{1,0:T(8,128)(2,1)S(1)}, u32[]{:S(2)}, u32[]{:S(2)}) collective-permute-start(bf16[128,1408]{1,0:T(8,128)(2,1)S(1)} %collective-permute-done.3), channel_id=1, source_target_pairs={{0,1},{1,0},{2,3},{3,2},{4,5},{5,4},{6,7},{7,6},{8,9},{9,8},{10,11... | collective-permute-start | bytes 1081352 | tf_op jit(solution)/shard_map/pair_far/ppermute | solution.py:222
  78.5 5.1 %collective-permute-start.8 = (bf16[512,1408]{1,0:T(8,128)(2,1)S(1)}, bf16[512,1408]{1,0:T(8,128)(2,1)S(1)}, u32[]{:S(2)}, u32[]{:S(2)}) collective-permute-start(bf16[512,1408]{1,0:T(8,128)(2,1)S(1)} %pad_maximum_fusion.refs_0_.mine_ref), channel_id=1, source_target_pairs={{0,64},{64,0},{1,65},{65,1},{2,66},{66,2},{3,67},{67,3},{4,68},{68... | collective-permute-start | bytes 4325384 | tf_op jit(solution)/shard_map/swap_mine/ppermute | solution.py:222
  81.1 6.0 %collective-permute-start.9 = (bf16[512,1408]{1,0:T(8,128)(2,1)S(1)}, bf16[512,1408]{1,0:T(8,128)(2,1)S(1)}, u32[]{:S(2)}, u32[]{:S(2)}) collective-permute-start(bf16[512,1408]{1,0:T(8,128)(2,1)S(1)} %pad_maximum_fusion.1), channel_id=1, source_target_pairs={{0,64},{64,0},{1,65},{65,1},{2,66},{66,2},{3,67},{67,3},{4,68},{68... | collective-permute-start | bytes 4325384 | tf_op jit(solution)/shard_map/swap_other/ppermute | solution.py:222
  87.0 47.9 %copy-start = (s32[1,4]{1,0:T(1,128)S(1)}, s32[1,4]{1,0:T(1,128)}, u32[]{:S(2)}) copy-start(s32[1,4]{1,0:T(1,128)} %param.5) | copy-start | bytes 52
  131.3 3.6 %collective-permute-start.10 = (bf16[2,4,16,1536]{3,2,1,0:T(8,128)(2,1)S(1)}, bf16[2,4,16,1536]{3,2,1,0:T(8,128)(2,1)S(1)}, u32[]{:S(2)}, u32[]{:S(2)}) collective-permute-start(bf16[2,4,16,1536]{3,2,1,0:T(8,128)(2,1)S(1)} %bitcast.6), channel_id=1, source_target_pairs={{0,64},{64,0},{1,65},{65,1},{2,66},{66,2},{3,67},{67,3},{4,68},{68... | collective-permute-start | bytes 1179656 | tf_op jit(solution)/shard_map/ppermute | solution.py:258

commit v12 on v11

--- a/solution.py
+++ b/solution.py
@@ -246,12 +246,12 @@
     mine = jnp.concatenate([mine, mine_left, mine_right, mine_far], axis=0)
     other_first = other
     other = jnp.concatenate([other, other_left, other_right, other_far], axis=0)
-    part = gram_part(None, mine, other_left)
+    part = gram_part(None, mine, other_first)
     mine, part = lax.optimization_barrier((mine, part))
     mine_swapped = move("swap_mine", mine, "core", swap)
     held, part = lax.optimization_barrier((other, part))
     other_swapped = move("swap_other", held, "core", swap)
-    part = gram_part(part, other_right, other_first, other_far, mine_swapped)
+    part = gram_part(part, other_right, other_left, other_far, mine_swapped)
     slots = products(mine, part, other_swapped)
     near = lax.all_to_all(slots, "z", split_axis=0, concat_axis=0, tiled=True)
     near = near.reshape(2, matrices, rows // 2, columns + LANES)

time: 138 us -> 138 us (level)
  transfers between devices with their start and end apart: 11 -> 11, of which waited for: 6 -> 4; matrix products, arithmetic and copies ran while one was open for 0% -> 0% of each run, Pallas kernels for 4% -> 4%
where the time goes in v12:
time: 138 us; the launch traced here: 136 us
  blocking collectives  72.7 us (53%)
  starting transfers between devices  30.4 us (22%)
  Pallas kernels  19.6 us (14%)
  waiting for transfers between devices  12 us (9%)
    all_to_all x1, blocking collectives, on_device(): lax.all_to_all(halves.reshape(16, rows // 4, columns), 'z', split_axis=0,...  38.2 us
    all_to_all x1, blocking collectives, on_device(): near = lax.all_to_all(slots, 'z', split_axis=0, concat_axis=0, tiled=True)  34.5 us
    ppermute x9, starting transfers between devices, move(): return lax.ppermute(block, axis, pairs)  26.5 us
    pallas_call x1, Pallas kernels, products(): pl.pallas_call(products_kernel, in_specs=[vmem] * (2 + len(blocks)), out_...  10.2 us
    ppermute x9, waiting for transfers between devices, move(): return lax.ppermute(block, axis, pairs)  8.72 us
    pallas_call x2, Pallas kernels, gram_part(): pl.pallas_call(functools.partial(gram_part_kernel, len(given)), in_specs=...  5.58 us
  transfers between devices with their start and end apart: 11, of which 4 were waited for; matrix products, arithmetic and copies ran while one was open for 0% of the time, Pallas kernels for 4%

profile of v12, /device:TPU:6, one launch (start us, length us, event | category | flops | bytes accessed | tf_op | source)
XLA Modules:
  0.0 136.4 jit_solution(16088279398634390553)
XLA Ops:
  0.6 2.4 %momentum_step.1 = (f32[4,32,1408]{2,1,0:T(8,128)}, bf16[2,4,16,1408]{3,2,1,0:T(8,128)(2,1)}, bf16[4,16,1408]{2,1,0:T(8,128)(2,1)}) custom-call(bf16[4,32,1408]{2,1,0:T(8,128)(2,1)} %grad_ref.1, f32[4,32,1408]{2,1,0:T(8,128)} %momentum_ref.1), custom_call_target="tpu_custom_call" | custom-call | tf_op jit(solution)/shard_map/momentum_step/pallas_call | solution.py:39
  3.0 1.9 %collective-permute-start = (bf16[4,16,1408]{2,1,0:T(8,128)(2,1)}, bf16[4,16,1408]{2,1,0:T(8,128)(2,1)S(1)}, u32[]{:S(2)}, u32[]{:S(2)}) collective-permute-start(bf16[4,16,1408]{2,1,0:T(8,128)(2,1)} %get-tuple-element.14), channel_id=1, source_target_pairs={{0,64},{64,0},{1,65},{65,1},{2,66},{66,2},{3,67},{67,3},{4,68},{68... | collective-permute-start | bytes 540680 | tf_op jit(solution)/shard_map/ppermute | solution.py:234
  4.9 1.6 %collective-permute-done = bf16[4,16,1408]{2,1,0:T(8,128)(2,1)S(1)} collective-permute-done((bf16[4,16,1408]{2,1,0:T(8,128)(2,1)}, bf16[4,16,1408]{2,1,0:T(8,128)(2,1)S(1)}, u32[]{:S(2)}, u32[]{:S(2)}) %collective-permute-start) | collective-permute-done | bytes 180256 | tf_op jit(solution)/shard_map/ppermute | solution.py:234
  6.5 0.7 bitcast_dynamic-update-slice_fusion
  7.2 38.2 %all_to_all.10 = bf16[16,8,1408]{2,1,0:T(8,128)(2,1)S(1)} all-to-all(bf16[16,8,1408]{2,1,0:T(8,128)(2,1)} %bitcast.13), channel_id=1, replica_groups=mesh['x'=4,'core'=2,'y'=4,'z'=16] {'z'}, dimensions={0} | all-to-all | bytes 720896 | tf_op jit(solution)/shard_map/all_to_all | solution.py:236
  45.4 3.5 %collective-permute-start.1 = (bf16[128,1408]{1,0:T(8,128)(2,1)S(1)}, bf16[128,1408]{1,0:T(8,128)(2,1)S(1)}, u32[]{:S(2)}, u32[]{:S(2)}) collective-permute-start(bf16[128,1408]{1,0:T(8,128)(2,1)S(1)} %bitcast.9), channel_id=1, source_target_pairs={{0,16},{16,32},{32,48},{48,0},{1,17},{17,33},{33,49},{49,1},{2,18}... | collective-permute-start | bytes 1081352 | tf_op jit(solution)/shard_map/mine_left/ppermute | solution.py:222
  48.9 2.4 %collective-permute-start.4 = (bf16[128,1408]{1,0:T(8,128)(2,1)S(1)}, bf16[128,1408]{1,0:T(8,128)(2,1)S(1)}, u32[]{:S(2)}, u32[]{:S(2)}) collective-permute-start(bf16[128,1408]{1,0:T(8,128)(2,1)S(1)} %bitcast.10), channel_id=1, source_target_pairs={{0,1},{1,0},{2,3},{3,2},{4,5},{5,4},{6,7},{7,6},{8,9},{9,8},{10,11... | collective-permute-start | bytes 1081352 | tf_op jit(solution)/shard_map/pair/ppermute | solution.py:222
  51.3 5.6 %collective-permute-done.1 = bf16[128,1408]{1,0:T(8,128)(2,1)S(1)} collective-permute-done((bf16[128,1408]{1,0:T(8,128)(2,1)S(1)}, bf16[128,1408]{1,0:T(8,128)(2,1)S(1)}, u32[]{:S(2)}, u32[]{:S(2)}) %collective-permute-start.1) | collective-permute-done | bytes 360480 | tf_op jit(solution)/shard_map/mine_left/ppermute | solution.py:222
  56.9 2.3 %collective-permute-start.3 = (bf16[128,1408]{1,0:T(8,128)(2,1)S(1)}, bf16[128,1408]{1,0:T(8,128)(2,1)S(1)}, u32[]{:S(2)}, u32[]{:S(2)}) collective-permute-start(bf16[128,1408]{1,0:T(8,128)(2,1)S(1)} %collective-permute-done.1), channel_id=1, source_target_pairs={{0,16},{16,32},{32,48},{48,0},{1,17},{17,33},{33,49},{49,1},{2,18}... | collective-permute-start | bytes 1081352 | tf_op jit(solution)/shard_map/mine_far/ppermute | solution.py:222
  59.1 4.8 %collective-permute-start.2 = (bf16[128,1408]{1,0:T(8,128)(2,1)S(1)}, bf16[128,1408]{1,0:T(8,128)(2,1)S(1)}, u32[]{:S(2)}, u32[]{:S(2)}) collective-permute-start(bf16[128,1408]{1,0:T(8,128)(2,1)S(1)} %bitcast.11), channel_id=1, source_target_pairs={{16,0},{32,16},{48,32},{0,48},{17,1},{33,17},{49,33},{1,49},{18,2}... | collective-permute-start | bytes 1081352 | tf_op jit(solution)/shard_map/mine_right/ppermute | solution.py:222
  63.9 2.9 %collective-permute-start.5 = (bf16[128,1408]{1,0:T(8,128)(2,1)S(1)}, bf16[128,1408]{1,0:T(8,128)(2,1)S(1)}, u32[]{:S(2)}, u32[]{:S(2)}) collective-permute-start(bf16[128,1408]{1,0:T(8,128)(2,1)S(1)} %collective-permute-done.1), channel_id=1, source_target_pairs={{0,1},{1,0},{2,3},{3,2},{4,5},{5,4},{6,7},{7,6},{8,9},{9,8},{10,11... | collective-permute-start | bytes 1081352 | tf_op jit(solution)/shard_map/pair_left/ppermute | solution.py:222
  66.8 0.0 collective-permute-done.4.refs_1_
  66.8 2.8 %collective-permute-start.6 = (bf16[128,1408]{1,0:T(8,128)(2,1)S(1)}, bf16[128,1408]{1,0:T(8,128)(2,1)S(1)}, u32[]{:S(2)}, u32[]{:S(2)}) collective-permute-start(bf16[128,1408]{1,0:T(8,128)(2,1)S(1)} %collective-permute-done.4.refs_1_), channel_id=1, source_target_pairs={{16,0},{32,16},{48,32},{0,48},{17,1},{33,17},{49,33},{1,49},{18,2}... | collective-permute-start | bytes 1081352 | tf_op jit(solution)/shard_map/other_right/ppermute | solution.py:222
  69.7 0.0 collective-permute-done.3
  69.7 3.9 %collective-permute-start.7 = (bf16[128,1408]{1,0:T(8,128)(2,1)S(1)}, bf16[128,1408]{1,0:T(8,128)(2,1)S(1)}, u32[]{:S(2)}, u32[]{:S(2)}) collective-permute-start(bf16[128,1408]{1,0:T(8,128)(2,1)S(1)} %collective-permute-done.3), channel_id=1, source_target_pairs={{0,1},{1,0},{2,3},{3,2},{4,5},{5,4},{6,7},{7,6},{8,9},{9,8},{10,11... | collective-permute-start | bytes 1081352 | tf_op jit(solution)/shard_map/pair_far/ppermute | solution.py:222
  73.6 0.0 collective-permute-done.2
  73.6 0.1 pad_maximum_fusion.refs_0_.mine_ref
  73.7 2.2 %gram_part.2.refs_0_ = f32[1408,1408]{1,0:T(8,128)S(1)} custom-call(bf16[512,1408]{1,0:T(8,128)(2,1)S(1)} %pad_maximum_fusion.refs_0_.mine_ref, bf16[128,1408]{1,0:T(8,128)(2,1)S(1)} %collective-permute-done.4.refs_1_), custom_call_target="tpu_custom_call" | custom-call | flops 2537553920 | tf_op jit(solution)/shard_map/gram_part/pallas_call | solution.py:86
  75.9 1.9 %collective-permute-start.8 = (bf16[512,1408]{1,0:T(8,128)(2,1)S(1)}, bf16[512,1408]{1,0:T(8,128)(2,1)S(1)}, u32[]{:S(2)}, u32[]{:S(2)}) collective-permute-start(bf16[512,1408]{1,0:T(8,128)(2,1)S(1)} %pad_maximum_fusion.refs_0_.mine_ref), channel_id=1, source_target_pairs={{0,64},{64,0},{1,65},{65,1},{2,66},{66,2},{3,67},{67,3},{4,68},{68... | collective-permute-start | bytes 4325384 | tf_op jit(solution)/shard_map/swap_mine/ppermute | solution.py:222
  77.9 0.0 collective-permute-done.6.refs_1_
  77.9 0.0 collective-permute-done.5.refs_2_
  77.9 3.1 %collective-permute-done.7.refs_3_ = bf16[128,1408]{1,0:T(8,128)(2,1)S(1)} collective-permute-done((bf16[128,1408]{1,0:T(8,128)(2,1)S(1)}, bf16[128,1408]{1,0:T(8,128)(2,1)S(1)}, u32[]{:S(2)}, u32[]{:S(2)}) %collective-permute-start.7) | collective-permute-done | bytes 360480 | tf_op jit(solution)/shard_map/pair_far/ppermute | solution.py:222
  81.0 0.1 pad_maximum_fusion.1
  81.1 2.1 %collective-permute-start.9 = (bf16[512,1408]{1,0:T(8,128)(2,1)S(1)}, bf16[512,1408]{1,0:T(8,128)(2,1)S(1)}, u32[]{:S(2)}, u32[]{:S(2)}) collective-permute-start(bf16[512,1408]{1,0:T(8,128)(2,1)S(1)} %pad_maximum_fusion.1), channel_id=1, source_target_pairs={{0,64},{64,0},{1,65},{65,1},{2,66},{66,2},{3,67},{67,3},{4,68},{68... | collective-permute-start | bytes 4325384 | tf_op jit(solution)/shard_map/swap_other/ppermute | solution.py:222
  83.2 3.4 %gram_part.3.part_ref = f32[1408,1408]{1,0:T(8,128)S(1)} custom-call(f32[1408,1408]{1,0:T(8,128)S(1)} %gram_part.2.refs_0_, bf16[128,1408]{1,0:T(8,128)(2,1)S(1)} %collective-permute-done.6.refs_1_, bf16[128,1408]{1,0:T(8,128)(2,1)S(1)} %collective-permute-done.5.refs_2_, bf16[128,1408]{1,0:T(8,128)(2,1)S(1)} %collective-permute-done.7.refs_3_, ...), custom_call_target="tpu_custom_call" | custom-call | flops 3552575488 | tf_op jit(solution)/shard_map/gram_part/pallas_call | solution.py:86
  86.6 0.0 copy-start
  86.6 0.0 collective-permute-done.9.refs_0_
  86.6 10.2 %products.1 = bf16[16,8,1536]{2,1,0:T(8,128)(2,1)S(1)} custom-call(bf16[512,1408]{1,0:T(8,128)(2,1)S(1)} %pad_maximum_fusion.refs_0_.mine_ref, f32[1408,1408]{1,0:T(8,128)S(1)} %gram_part.3.part_ref, bf16[512,1408]{1,0:T(8,128)(2,1)S(1)} %collective-permute-done.9.refs_0_), custom_call_target="tpu_custom_call" | custom-call | flops 12180258816 | tf_op jit(solution)/shard_map/products/pallas_call | solution.py:164
  96.8 34.5 %all_to_all.11 = bf16[16,8,1536]{2,1,0:T(8,128)(2,1)S(1)} all-to-all(bf16[16,8,1536]{2,1,0:T(8,128)(2,1)S(1)} %products.1), channel_id=1, replica_groups=mesh['x'=4,'core'=2,'y'=4,'z'=16] {'z'}, dimensions={0} | all-to-all | bytes 786432 | tf_op jit(solution)/shard_map/all_to_all | solution.py:256
  131.3 1.9 %collective-permute-start.10 = (bf16[2,4,16,1536]{3,2,1,0:T(8,128)(2,1)S(1)}, bf16[2,4,16,1536]{3,2,1,0:T(8,128)(2,1)S(1)}, u32[]{:S(2)}, u32[]{:S(2)}) collective-permute-start(bf16[2,4,16,1536]{3,2,1,0:T(8,128)(2,1)S(1)} %bitcast.6), channel_id=1, source_target_pairs={{0,64},{64,0},{1,65},{65,1},{2,66},{66,2},{3,67},{67,3},{4,68},{68... | collective-permute-start | bytes 1179656 | tf_op jit(solution)/shard_map/ppermute | solution.py:258
  133.2 1.7 %collective-permute-done.10.far_ref = bf16[2,4,16,1536]{3,2,1,0:T(8,128)(2,1)S(1)} collective-permute-done((bf16[2,4,16,1536]{3,2,1,0:T(8,128)(2,1)S(1)}, bf16[2,4,16,1536]{3,2,1,0:T(8,128)(2,1)S(1)}, u32[]{:S(2)}, u32[]{:S(2)}) %collective-permute-start.10) | collective-permute-done | bytes 393248 | tf_op jit(solution)/shard_map/ppermute | solution.py:258
  134.9 1.5 %regroup.1 = (bf16[4,32,1408]{2,1,0:T(8,128)(2,1)}, f32[1,88]{1,0:T(1,128)}) custom-call(s32[4]{0:T(128)S(1)} %bitcast.8, bf16[2,4,16,1536]{3,2,1,0:T(8,128)(2,1)S(1)} %bitcast.7, bf16[2,4,16,1536]{3,2,1,0:T(8,128)(2,1)S(1)} %collective-permute-done.10.far_ref), custom_call_target="tpu_custom_call" | custom-call | tf_op jit(solution)/shard_map/regroup/pallas_call | solution.py:207
  (2 shorter events, 0.0 us)
Async XLA Ops:
  3.0 3.5 %collective-permute-start = (bf16[4,16,1408]{2,1,0:T(8,128)(2,1)}, bf16[4,16,1408]{2,1,0:T(8,128)(2,1)S(1)}, u32[]{:S(2)}, u32[]{:S(2)}) collective-permute-start(bf16[4,16,1408]{2,1,0:T(8,128)(2,1)} %get-tuple-element.14), channel_id=1, source_target_pairs={{0,64},{64,0},{1,65},{65,1},{2,66},{66,2},{3,67},{67,3},{4,68},{68... | collective-permute-start | bytes 540680 | tf_op jit(solution)/shard_map/ppermute | solution.py:234
  45.4 11.5 %collective-permute-start.1 = (bf16[128,1408]{1,0:T(8,128)(2,1)S(1)}, bf16[128,1408]{1,0:T(8,128)(2,1)S(1)}, u32[]{:S(2)}, u32[]{:S(2)}) collective-permute-start(bf16[128,1408]{1,0:T(8,128)(2,1)S(1)} %bitcast.9), channel_id=1, source_target_pairs={{0,16},{16,32},{32,48},{48,0},{1,17},{17,33},{33,49},{49,1},{2,18}... | collective-permute-start | bytes 1081352 | tf_op jit(solution)/shard_map/mine_left/ppermute | solution.py:222
  48.9 17.9 %collective-permute-start.4 = (bf16[128,1408]{1,0:T(8,128)(2,1)S(1)}, bf16[128,1408]{1,0:T(8,128)(2,1)S(1)}, u32[]{:S(2)}, u32[]{:S(2)}) collective-permute-start(bf16[128,1408]{1,0:T(8,128)(2,1)S(1)} %bitcast.10), channel_id=1, source_target_pairs={{0,1},{1,0},{2,3},{3,2},{4,5},{5,4},{6,7},{7,6},{8,9},{9,8},{10,11... | collective-permute-start | bytes 1081352 | tf_op jit(solution)/shard_map/pair/ppermute | solution.py:222
  56.9 12.8 %collective-permute-start.3 = (bf16[128,1408]{1,0:T(8,128)(2,1)S(1)}, bf16[128,1408]{1,0:T(8,128)(2,1)S(1)}, u32[]{:S(2)}, u32[]{:S(2)}) collective-permute-start(bf16[128,1408]{1,0:T(8,128)(2,1)S(1)} %collective-permute-done.1), channel_id=1, source_target_pairs={{0,16},{16,32},{32,48},{48,0},{1,17},{17,33},{33,49},{49,1},{2,18}... | collective-permute-start | bytes 1081352 | tf_op jit(solution)/shard_map/mine_far/ppermute | solution.py:222
  59.1 14.5 %collective-permute-start.2 = (bf16[128,1408]{1,0:T(8,128)(2,1)S(1)}, bf16[128,1408]{1,0:T(8,128)(2,1)S(1)}, u32[]{:S(2)}, u32[]{:S(2)}) collective-permute-start(bf16[128,1408]{1,0:T(8,128)(2,1)S(1)} %bitcast.11), channel_id=1, source_target_pairs={{16,0},{32,16},{48,32},{0,48},{17,1},{33,17},{49,33},{1,49},{18,2}... | collective-permute-start | bytes 1081352 | tf_op jit(solution)/shard_map/mine_right/ppermute | solution.py:222
  63.9 13.9 %collective-permute-start.5 = (bf16[128,1408]{1,0:T(8,128)(2,1)S(1)}, bf16[128,1408]{1,0:T(8,128)(2,1)S(1)}, u32[]{:S(2)}, u32[]{:S(2)}) collective-permute-start(bf16[128,1408]{1,0:T(8,128)(2,1)S(1)} %collective-permute-done.1), channel_id=1, source_target_pairs={{0,1},{1,0},{2,3},{3,2},{4,5},{5,4},{6,7},{7,6},{8,9},{9,8},{10,11... | collective-permute-start | bytes 1081352 | tf_op jit(solution)/shard_map/pair_left/ppermute | solution.py:222
  66.8 11.0 %collective-permute-start.6 = (bf16[128,1408]{1,0:T(8,128)(2,1)S(1)}, bf16[128,1408]{1,0:T(8,128)(2,1)S(1)}, u32[]{:S(2)}, u32[]{:S(2)}) collective-permute-start(bf16[128,1408]{1,0:T(8,128)(2,1)S(1)} %collective-permute-done.4.refs_1_), channel_id=1, source_target_pairs={{16,0},{32,16},{48,32},{0,48},{17,1},{33,17},{49,33},{1,49},{18,2}... | collective-permute-start | bytes 1081352 | tf_op jit(solution)/shard_map/other_right/ppermute | solution.py:222
  69.7 11.3 %collective-permute-start.7 = (bf16[128,1408]{1,0:T(8,128)(2,1)S(1)}, bf16[128,1408]{1,0:T(8,128)(2,1)S(1)}, u32[]{:S(2)}, u32[]{:S(2)}) collective-permute-start(bf16[128,1408]{1,0:T(8,128)(2,1)S(1)} %collective-permute-done.3), channel_id=1, source_target_pairs={{0,1},{1,0},{2,3},{3,2},{4,5},{5,4},{6,7},{7,6},{8,9},{9,8},{10,11... | collective-permute-start | bytes 1081352 | tf_op jit(solution)/shard_map/pair_far/ppermute | solution.py:222
  75.9 7.3 %collective-permute-start.8 = (bf16[512,1408]{1,0:T(8,128)(2,1)S(1)}, bf16[512,1408]{1,0:T(8,128)(2,1)S(1)}, u32[]{:S(2)}, u32[]{:S(2)}) collective-permute-start(bf16[512,1408]{1,0:T(8,128)(2,1)S(1)} %pad_maximum_fusion.refs_0_.mine_ref), channel_id=1, source_target_pairs={{0,64},{64,0},{1,65},{65,1},{2,66},{66,2},{3,67},{67,3},{4,68},{68... | collective-permute-start | bytes 4325384 | tf_op jit(solution)/shard_map/swap_mine/ppermute | solution.py:222
  81.1 5.5 %collective-permute-start.9 = (bf16[512,1408]{1,0:T(8,128)(2,1)S(1)}, bf16[512,1408]{1,0:T(8,128)(2,1)S(1)}, u32[]{:S(2)}, u32[]{:S(2)}) collective-permute-start(bf16[512,1408]{1,0:T(8,128)(2,1)S(1)} %pad_maximum_fusion.1), channel_id=1, source_target_pairs={{0,64},{64,0},{1,65},{65,1},{2,66},{66,2},{3,67},{67,3},{4,68},{68... | collective-permute-start | bytes 4325384 | tf_op jit(solution)/shard_map/swap_other/ppermute | solution.py:222
  86.6 48.3 %copy-start = (s32[1,4]{1,0:T(1,128)S(1)}, s32[1,4]{1,0:T(1,128)}, u32[]{:S(2)}) copy-start(s32[1,4]{1,0:T(1,128)} %param.5) | copy-start | bytes 52
  131.3 3.6 %collective-permute-start.10 = (bf16[2,4,16,1536]{3,2,1,0:T(8,128)(2,1)S(1)}, bf16[2,4,16,1536]{3,2,1,0:T(8,128)(2,1)S(1)}, u32[]{:S(2)}, u32[]{:S(2)}) collective-permute-start(bf16[2,4,16,1536]{3,2,1,0:T(8,128)(2,1)S(1)} %bitcast.6), channel_id=1, source_target_pairs={{0,64},{64,0},{1,65},{65,1},{2,66},{66,2},{3,67},{67,3},{4,68},{68... | collective-permute-start | bytes 1179656 | tf_op jit(solution)/shard_map/ppermute | solution.py:258

commit v13 on v12

--- a/solution.py
+++ b/solution.py
@@ -249,9 +249,10 @@
     part = gram_part(None, mine, other_first)
     mine, part = lax.optimization_barrier((mine, part))
     mine_swapped = move("swap_mine", mine, "core", swap)
+    part = gram_part(part, other_left, other_right)
     held, part = lax.optimization_barrier((other, part))
     other_swapped = move("swap_other", held, "core", swap)
-    part = gram_part(part, other_right, other_left, other_far, mine_swapped)
+    part = gram_part(part, other_far, mine_swapped)
     slots = products(mine, part, other_swapped)
     near = lax.all_to_all(slots, "z", split_axis=0, concat_axis=0, tiled=True)
     near = near.reshape(2, matrices, rows // 2, columns + LANES)

time: 138 us -> 137 us (level)
    pallas_call x2 -> x3, Pallas kernels: 5.58 us -> 5.79 us  [gram_part(): pl.pallas_call(functools.partial(gram_part_kernel, len(given)), in_specs=...]
  transfers between devices with their start and end apart: 11 -> 11, of which waited for: 4 -> 5; matrix products, arithmetic and copies ran while one was open for 0% -> 0% of each run, Pallas kernels for 4% -> 4%
where the time goes in v13:
time: 137 us; the launch traced here: 135 us
  blocking collectives  71.6 us (52%)
  starting transfers between devices  30.4 us (22%)
  Pallas kernels  19.9 us (15%)
  waiting for transfers between devices  11.4 us (8%)
    all_to_all x1, blocking collectives, on_device(): lax.all_to_all(halves.reshape(16, rows // 4, columns), 'z', split_axis=0,...  38.2 us
    all_to_all x1, blocking collectives, on_device(): near = lax.all_to_all(slots, 'z', split_axis=0, concat_axis=0, tiled=True)  33.4 us
    ppermute x9, starting transfers between devices, move(): return lax.ppermute(block, axis, pairs)  26.5 us
    pallas_call x1, Pallas kernels, products(): pl.pallas_call(products_kernel, in_specs=[vmem] * (2 + len(blocks)), out_...  10.3 us
    ppermute x9, waiting for transfers between devices, move(): return lax.ppermute(block, axis, pairs)  8.09 us
    pallas_call x3, Pallas kernels, gram_part(): pl.pallas_call(functools.partial(gram_part_kernel, len(given)), in_specs=...  5.79 us
  transfers between devices with their start and end apart: 11, of which 5 were waited for; matrix products, arithmetic and copies ran while one was open for 0% of the time, Pallas kernels for 4%

profile of v13, /device:TPU:6, one launch (start us, length us, event | category | flops | bytes accessed | tf_op | source)
XLA Modules:
  0.0 134.9 jit_solution(3390596199208245312)
XLA Ops:
  0.6 2.4 %momentum_step.1 = (f32[4,32,1408]{2,1,0:T(8,128)}, bf16[2,4,16,1408]{3,2,1,0:T(8,128)(2,1)}, bf16[4,16,1408]{2,1,0:T(8,128)(2,1)}) custom-call(bf16[4,32,1408]{2,1,0:T(8,128)(2,1)} %grad_ref.1, f32[4,32,1408]{2,1,0:T(8,128)} %momentum_ref.1), custom_call_target="tpu_custom_call" | custom-call | tf_op jit(solution)/shard_map/momentum_step/pallas_call | solution.py:39
  3.0 1.9 %collective-permute-start = (bf16[4,16,1408]{2,1,0:T(8,128)(2,1)}, bf16[4,16,1408]{2,1,0:T(8,128)(2,1)S(1)}, u32[]{:S(2)}, u32[]{:S(2)}) collective-permute-start(bf16[4,16,1408]{2,1,0:T(8,128)(2,1)} %get-tuple-element.14), channel_id=1, source_target_pairs={{0,64},{64,0},{1,65},{65,1},{2,66},{66,2},{3,67},{67,3},{4,68},{68... | collective-permute-start | bytes 540680 | tf_op jit(solution)/shard_map/ppermute | solution.py:234
  4.9 1.6 %collective-permute-done = bf16[4,16,1408]{2,1,0:T(8,128)(2,1)S(1)} collective-permute-done((bf16[4,16,1408]{2,1,0:T(8,128)(2,1)}, bf16[4,16,1408]{2,1,0:T(8,128)(2,1)S(1)}, u32[]{:S(2)}, u32[]{:S(2)}) %collective-permute-start) | collective-permute-done | bytes 180256 | tf_op jit(solution)/shard_map/ppermute | solution.py:234
  6.5 0.7 bitcast_dynamic-update-slice_fusion
  7.2 38.2 %all_to_all.10 = bf16[16,8,1408]{2,1,0:T(8,128)(2,1)S(1)} all-to-all(bf16[16,8,1408]{2,1,0:T(8,128)(2,1)} %bitcast.13), channel_id=1, replica_groups=mesh['x'=4,'core'=2,'y'=4,'z'=16] {'z'}, dimensions={0} | all-to-all | bytes 720896 | tf_op jit(solution)/shard_map/all_to_all | solution.py:236
  45.4 3.5 %collective-permute-start.1 = (bf16[128,1408]{1,0:T(8,128)(2,1)S(1)}, bf16[128,1408]{1,0:T(8,128)(2,1)S(1)}, u32[]{:S(2)}, u32[]{:S(2)}) collective-permute-start(bf16[128,1408]{1,0:T(8,128)(2,1)S(1)} %bitcast.9), channel_id=1, source_target_pairs={{0,16},{16,32},{32,48},{48,0},{1,17},{17,33},{33,49},{49,1},{2,18}... | collective-permute-start | bytes 1081352 | tf_op jit(solution)/shard_map/mine_left/ppermute | solution.py:222
  48.9 2.4 %collective-permute-start.4 = (bf16[128,1408]{1,0:T(8,128)(2,1)S(1)}, bf16[128,1408]{1,0:T(8,128)(2,1)S(1)}, u32[]{:S(2)}, u32[]{:S(2)}) collective-permute-start(bf16[128,1408]{1,0:T(8,128)(2,1)S(1)} %bitcast.10), channel_id=1, source_target_pairs={{0,1},{1,0},{2,3},{3,2},{4,5},{5,4},{6,7},{7,6},{8,9},{9,8},{10,11... | collective-permute-start | bytes 1081352 | tf_op jit(solution)/shard_map/pair/ppermute | solution.py:222
  51.3 5.6 %collective-permute-done.1 = bf16[128,1408]{1,0:T(8,128)(2,1)S(1)} collective-permute-done((bf16[128,1408]{1,0:T(8,128)(2,1)S(1)}, bf16[128,1408]{1,0:T(8,128)(2,1)S(1)}, u32[]{:S(2)}, u32[]{:S(2)}) %collective-permute-start.1) | collective-permute-done | bytes 360480 | tf_op jit(solution)/shard_map/mine_left/ppermute | solution.py:222
  56.9 2.3 %collective-permute-start.3 = (bf16[128,1408]{1,0:T(8,128)(2,1)S(1)}, bf16[128,1408]{1,0:T(8,128)(2,1)S(1)}, u32[]{:S(2)}, u32[]{:S(2)}) collective-permute-start(bf16[128,1408]{1,0:T(8,128)(2,1)S(1)} %collective-permute-done.1), channel_id=1, source_target_pairs={{0,16},{16,32},{32,48},{48,0},{1,17},{17,33},{33,49},{49,1},{2,18}... | collective-permute-start | bytes 1081352 | tf_op jit(solution)/shard_map/mine_far/ppermute | solution.py:222
  59.1 4.8 %collective-permute-start.2 = (bf16[128,1408]{1,0:T(8,128)(2,1)S(1)}, bf16[128,1408]{1,0:T(8,128)(2,1)S(1)}, u32[]{:S(2)}, u32[]{:S(2)}) collective-permute-start(bf16[128,1408]{1,0:T(8,128)(2,1)S(1)} %bitcast.11), channel_id=1, source_target_pairs={{16,0},{32,16},{48,32},{0,48},{17,1},{33,17},{49,33},{1,49},{18,2}... | collective-permute-start | bytes 1081352 | tf_op jit(solution)/shard_map/mine_right/ppermute | solution.py:222
  63.9 2.9 %collective-permute-start.5 = (bf16[128,1408]{1,0:T(8,128)(2,1)S(1)}, bf16[128,1408]{1,0:T(8,128)(2,1)S(1)}, u32[]{:S(2)}, u32[]{:S(2)}) collective-permute-start(bf16[128,1408]{1,0:T(8,128)(2,1)S(1)} %collective-permute-done.1), channel_id=1, source_target_pairs={{0,1},{1,0},{2,3},{3,2},{4,5},{5,4},{6,7},{7,6},{8,9},{9,8},{10,11... | collective-permute-start | bytes 1081352 | tf_op jit(solution)/shard_map/pair_left/ppermute | solution.py:222
  66.8 0.0 collective-permute-done.4.refs_1_
  66.8 2.8 %collective-permute-start.6 = (bf16[128,1408]{1,0:T(8,128)(2,1)S(1)}, bf16[128,1408]{1,0:T(8,128)(2,1)S(1)}, u32[]{:S(2)}, u32[]{:S(2)}) collective-permute-start(bf16[128,1408]{1,0:T(8,128)(2,1)S(1)} %collective-permute-done.4.refs_1_), channel_id=1, source_target_pairs={{16,0},{32,16},{48,32},{0,48},{17,1},{33,17},{49,33},{1,49},{18,2}... | collective-permute-start | bytes 1081352 | tf_op jit(solution)/shard_map/other_right/ppermute | solution.py:222
  69.7 0.0 collective-permute-done.3
  69.7 3.9 %collective-permute-start.7 = (bf16[128,1408]{1,0:T(8,128)(2,1)S(1)}, bf16[128,1408]{1,0:T(8,128)(2,1)S(1)}, u32[]{:S(2)}, u32[]{:S(2)}) collective-permute-start(bf16[128,1408]{1,0:T(8,128)(2,1)S(1)} %collective-permute-done.3), channel_id=1, source_target_pairs={{0,1},{1,0},{2,3},{3,2},{4,5},{5,4},{6,7},{7,6},{8,9},{9,8},{10,11... | collective-permute-start | bytes 1081352 | tf_op jit(solution)/shard_map/pair_far/ppermute | solution.py:222
  73.6 0.0 collective-permute-done.2
  73.6 0.1 pad_maximum_fusion.refs_0_.mine_ref
  73.7 2.2 %gram_part.3.refs_0_ = f32[1408,1408]{1,0:T(8,128)S(1)} custom-call(bf16[512,1408]{1,0:T(8,128)(2,1)S(1)} %pad_maximum_fusion.refs_0_.mine_ref, bf16[128,1408]{1,0:T(8,128)(2,1)S(1)} %collective-permute-done.4.refs_1_), custom_call_target="tpu_custom_call" | custom-call | flops 2537553920 | tf_op jit(solution)/shard_map/gram_part/pallas_call | solution.py:86
  75.9 1.9 %collective-permute-start.8 = (bf16[512,1408]{1,0:T(8,128)(2,1)S(1)}, bf16[512,1408]{1,0:T(8,128)(2,1)S(1)}, u32[]{:S(2)}, u32[]{:S(2)}) collective-permute-start(bf16[512,1408]{1,0:T(8,128)(2,1)S(1)} %pad_maximum_fusion.refs_0_.mine_ref), channel_id=1, source_target_pairs={{0,64},{64,0},{1,65},{65,1},{2,66},{66,2},{3,67},{67,3},{4,68},{68... | collective-permute-start | bytes 4325384 | tf_op jit(solution)/shard_map/swap_mine/ppermute | solution.py:222
  77.9 0.0 collective-permute-done.5.refs_1_
  77.9 1.4 %gram_part.4.refs_0_ = f32[1408,1408]{1,0:T(8,128)S(1)} custom-call(f32[1408,1408]{1,0:T(8,128)S(1)} %gram_part.3.refs_0_, bf16[128,1408]{1,0:T(8,128)(2,1)S(1)} %collective-permute-done.5.refs_1_, bf16[128,1408]{1,0:T(8,128)(2,1)S(1)} %collective-permute-done.6.refs_2_), custom_call_target="tpu_custom_call" | custom-call | flops 1015021568 | tf_op jit(solution)/shard_map/gram_part/pallas_call | solution.py:86
  79.3 1.7 %collective-permute-done.7.refs_1_ = bf16[128,1408]{1,0:T(8,128)(2,1)S(1)} collective-permute-done((bf16[128,1408]{1,0:T(8,128)(2,1)S(1)}, bf16[128,1408]{1,0:T(8,128)(2,1)S(1)}, u32[]{:S(2)}, u32[]{:S(2)}) %collective-permute-start.7) | collective-permute-done | bytes 360480 | tf_op jit(solution)/shard_map/pair_far/ppermute | solution.py:222
  81.0 0.1 pad_maximum_fusion.1
  81.1 2.1 %collective-permute-start.9 = (bf16[512,1408]{1,0:T(8,128)(2,1)S(1)}, bf16[512,1408]{1,0:T(8,128)(2,1)S(1)}, u32[]{:S(2)}, u32[]{:S(2)}) collective-permute-start(bf16[512,1408]{1,0:T(8,128)(2,1)S(1)} %pad_maximum_fusion.1), channel_id=1, source_target_pairs={{0,64},{64,0},{1,65},{65,1},{2,66},{66,2},{3,67},{67,3},{4,68},{68... | collective-permute-start | bytes 4325384 | tf_op jit(solution)/shard_map/swap_other/ppermute | solution.py:222
  83.2 2.2 %gram_part.5.part_ref = f32[1408,1408]{1,0:T(8,128)S(1)} custom-call(f32[1408,1408]{1,0:T(8,128)S(1)} %gram_part.4.refs_0_, bf16[128,1408]{1,0:T(8,128)(2,1)S(1)} %collective-permute-done.7.refs_1_, bf16[512,1408]{1,0:T(8,128)(2,1)S(1)} %collective-permute-done.8.refs_2_), custom_call_target="tpu_custom_call" | custom-call | flops 2537553920 | tf_op jit(solution)/shard_map/gram_part/pallas_call | solution.py:86
  85.4 0.0 copy-start
  85.4 0.8 collective-permute-done.9.refs_0_
  86.2 10.3 %products.1 = bf16[16,8,1536]{2,1,0:T(8,128)(2,1)S(1)} custom-call(bf16[512,1408]{1,0:T(8,128)(2,1)S(1)} %pad_maximum_fusion.refs_0_.mine_ref, f32[1408,1408]{1,0:T(8,128)S(1)} %gram_part.5.part_ref, bf16[512,1408]{1,0:T(8,128)(2,1)S(1)} %collective-permute-done.9.refs_0_), custom_call_target="tpu_custom_call" | custom-call | flops 12180258816 | tf_op jit(solution)/shard_map/products/pallas_call | solution.py:164
  96.5 33.4 %all_to_all.11 = bf16[16,8,1536]{2,1,0:T(8,128)(2,1)S(1)} all-to-all(bf16[16,8,1536]{2,1,0:T(8,128)(2,1)S(1)} %products.1), channel_id=1, replica_groups=mesh['x'=4,'core'=2,'y'=4,'z'=16] {'z'}, dimensions={0} | all-to-all | bytes 786432 | tf_op jit(solution)/shard_map/all_to_all | solution.py:257
  129.8 1.9 %collective-permute-start.10 = (bf16[2,4,16,1536]{3,2,1,0:T(8,128)(2,1)S(1)}, bf16[2,4,16,1536]{3,2,1,0:T(8,128)(2,1)S(1)}, u32[]{:S(2)}, u32[]{:S(2)}) collective-permute-start(bf16[2,4,16,1536]{3,2,1,0:T(8,128)(2,1)S(1)} %bitcast.6), channel_id=1, source_target_pairs={{0,64},{64,0},{1,65},{65,1},{2,66},{66,2},{3,67},{67,3},{4,68},{68... | collective-permute-start | bytes 1179656 | tf_op jit(solution)/shard_map/ppermute | solution.py:259
  131.8 1.7 %collective-permute-done.10.far_ref = bf16[2,4,16,1536]{3,2,1,0:T(8,128)(2,1)S(1)} collective-permute-done((bf16[2,4,16,1536]{3,2,1,0:T(8,128)(2,1)S(1)}, bf16[2,4,16,1536]{3,2,1,0:T(8,128)(2,1)S(1)}, u32[]{:S(2)}, u32[]{:S(2)}) %collective-permute-start.10) | collective-permute-done | bytes 393248 | tf_op jit(solution)/shard_map/ppermute | solution.py:259
  133.5 1.5 %regroup.1 = (bf16[4,32,1408]{2,1,0:T(8,128)(2,1)}, f32[1,88]{1,0:T(1,128)}) custom-call(s32[4]{0:T(128)S(1)} %bitcast.8, bf16[2,4,16,1536]{3,2,1,0:T(8,128)(2,1)S(1)} %bitcast.7, bf16[2,4,16,1536]{3,2,1,0:T(8,128)(2,1)S(1)} %collective-permute-done.10.far_ref), custom_call_target="tpu_custom_call" | custom-call | tf_op jit(solution)/shard_map/regroup/pallas_call | solution.py:207
  (3 shorter events, 0.0 us)
Async XLA Ops:
  3.0 3.5 %collective-permute-start = (bf16[4,16,1408]{2,1,0:T(8,128)(2,1)}, bf16[4,16,1408]{2,1,0:T(8,128)(2,1)S(1)}, u32[]{:S(2)}, u32[]{:S(2)}) collective-permute-start(bf16[4,16,1408]{2,1,0:T(8,128)(2,1)} %get-tuple-element.14), channel_id=1, source_target_pairs={{0,64},{64,0},{1,65},{65,1},{2,66},{66,2},{3,67},{67,3},{4,68},{68... | collective-permute-start | bytes 540680 | tf_op jit(solution)/shard_map/ppermute | solution.py:234
  45.4 11.5 %collective-permute-start.1 = (bf16[128,1408]{1,0:T(8,128)(2,1)S(1)}, bf16[128,1408]{1,0:T(8,128)(2,1)S(1)}, u32[]{:S(2)}, u32[]{:S(2)}) collective-permute-start(bf16[128,1408]{1,0:T(8,128)(2,1)S(1)} %bitcast.9), channel_id=1, source_target_pairs={{0,16},{16,32},{32,48},{48,0},{1,17},{17,33},{33,49},{49,1},{2,18}... | collective-permute-start | bytes 1081352 | tf_op jit(solution)/shard_map/mine_left/ppermute | solution.py:222
  48.9 17.9 %collective-permute-start.4 = (bf16[128,1408]{1,0:T(8,128)(2,1)S(1)}, bf16[128,1408]{1,0:T(8,128)(2,1)S(1)}, u32[]{:S(2)}, u32[]{:S(2)}) collective-permute-start(bf16[128,1408]{1,0:T(8,128)(2,1)S(1)} %bitcast.10), channel_id=1, source_target_pairs={{0,1},{1,0},{2,3},{3,2},{4,5},{5,4},{6,7},{7,6},{8,9},{9,8},{10,11... | collective-permute-start | bytes 1081352 | tf_op jit(solution)/shard_map/pair/ppermute | solution.py:222
  56.9 12.8 %collective-permute-start.3 = (bf16[128,1408]{1,0:T(8,128)(2,1)S(1)}, bf16[128,1408]{1,0:T(8,128)(2,1)S(1)}, u32[]{:S(2)}, u32[]{:S(2)}) collective-permute-start(bf16[128,1408]{1,0:T(8,128)(2,1)S(1)} %collective-permute-done.1), channel_id=1, source_target_pairs={{0,16},{16,32},{32,48},{48,0},{1,17},{17,33},{33,49},{49,1},{2,18}... | collective-permute-start | bytes 1081352 | tf_op jit(solution)/shard_map/mine_far/ppermute | solution.py:222
  59.1 14.5 %collective-permute-start.2 = (bf16[128,1408]{1,0:T(8,128)(2,1)S(1)}, bf16[128,1408]{1,0:T(8,128)(2,1)S(1)}, u32[]{:S(2)}, u32[]{:S(2)}) collective-permute-start(bf16[128,1408]{1,0:T(8,128)(2,1)S(1)} %bitcast.11), channel_id=1, source_target_pairs={{16,0},{32,16},{48,32},{0,48},{17,1},{33,17},{49,33},{1,49},{18,2}... | collective-permute-start | bytes 1081352 | tf_op jit(solution)/shard_map/mine_right/ppermute | solution.py:222
  63.9 13.9 %collective-permute-start.5 = (bf16[128,1408]{1,0:T(8,128)(2,1)S(1)}, bf16[128,1408]{1,0:T(8,128)(2,1)S(1)}, u32[]{:S(2)}, u32[]{:S(2)}) collective-permute-start(bf16[128,1408]{1,0:T(8,128)(2,1)S(1)} %collective-permute-done.1), channel_id=1, source_target_pairs={{0,1},{1,0},{2,3},{3,2},{4,5},{5,4},{6,7},{7,6},{8,9},{9,8},{10,11... | collective-permute-start | bytes 1081352 | tf_op jit(solution)/shard_map/pair_left/ppermute | solution.py:222
  66.8 11.0 %collective-permute-start.6 = (bf16[128,1408]{1,0:T(8,128)(2,1)S(1)}, bf16[128,1408]{1,0:T(8,128)(2,1)S(1)}, u32[]{:S(2)}, u32[]{:S(2)}) collective-permute-start(bf16[128,1408]{1,0:T(8,128)(2,1)S(1)} %collective-permute-done.4.refs_1_), channel_id=1, source_target_pairs={{16,0},{32,16},{48,32},{0,48},{17,1},{33,17},{49,33},{1,49},{18,2}... | collective-permute-start | bytes 1081352 | tf_op jit(solution)/shard_map/other_right/ppermute | solution.py:222
  69.7 11.3 %collective-permute-start.7 = (bf16[128,1408]{1,0:T(8,128)(2,1)S(1)}, bf16[128,1408]{1,0:T(8,128)(2,1)S(1)}, u32[]{:S(2)}, u32[]{:S(2)}) collective-permute-start(bf16[128,1408]{1,0:T(8,128)(2,1)S(1)} %collective-permute-done.3), channel_id=1, source_target_pairs={{0,1},{1,0},{2,3},{3,2},{4,5},{5,4},{6,7},{7,6},{8,9},{9,8},{10,11... | collective-permute-start | bytes 1081352 | tf_op jit(solution)/shard_map/pair_far/ppermute | solution.py:222
  75.9 7.3 %collective-permute-start.8 = (bf16[512,1408]{1,0:T(8,128)(2,1)S(1)}, bf16[512,1408]{1,0:T(8,128)(2,1)S(1)}, u32[]{:S(2)}, u32[]{:S(2)}) collective-permute-start(bf16[512,1408]{1,0:T(8,128)(2,1)S(1)} %pad_maximum_fusion.refs_0_.mine_ref), channel_id=1, source_target_pairs={{0,64},{64,0},{1,65},{65,1},{2,66},{66,2},{3,67},{67,3},{4,68},{68... | collective-permute-start | bytes 4325384 | tf_op jit(solution)/shard_map/swap_mine/ppermute | solution.py:222
  81.1 5.1 %collective-permute-start.9 = (bf16[512,1408]{1,0:T(8,128)(2,1)S(1)}, bf16[512,1408]{1,0:T(8,128)(2,1)S(1)}, u32[]{:S(2)}, u32[]{:S(2)}) collective-permute-start(bf16[512,1408]{1,0:T(8,128)(2,1)S(1)} %pad_maximum_fusion.1), channel_id=1, source_target_pairs={{0,64},{64,0},{1,65},{65,1},{2,66},{66,2},{3,67},{67,3},{4,68},{68... | collective-permute-start | bytes 4325384 | tf_op jit(solution)/shard_map/swap_other/ppermute | solution.py:222
  85.4 48.1 %copy-start = (s32[1,4]{1,0:T(1,128)S(1)}, s32[1,4]{1,0:T(1,128)}, u32[]{:S(2)}) copy-start(s32[1,4]{1,0:T(1,128)} %param.5) | copy-start | bytes 52
  129.8 3.6 %collective-permute-start.10 = (bf16[2,4,16,1536]{3,2,1,0:T(8,128)(2,1)S(1)}, bf16[2,4,16,1536]{3,2,1,0:T(8,128)(2,1)S(1)}, u32[]{:S(2)}, u32[]{:S(2)}) collective-permute-start(bf16[2,4,16,1536]{3,2,1,0:T(8,128)(2,1)S(1)} %bitcast.6), channel_id=1, source_target_pairs={{0,64},{64,0},{1,65},{65,1},{2,66},{66,2},{3,67},{67,3},{4,68},{68... | collective-permute-start | bytes 1179656 | tf_op jit(solution)/shard_map/ppermute | solution.py:259
